TPU v7x, 256 devices: a whole 4x4x8 slice. The times are simulated.
256 devices in a mesh: rows: 16 (over z_lo, x, core), cols: 16 (over z_hi, y).
Axes of the slice: x: 4, y: 4, z: 8 (z_hi: 4, z_lo: 2; z = z_hi * 2 + z_lo), core: 2. Of those that a mesh axis runs over, the one named last changes fastest.
Arguments:
- tensor: float32 [192, 512, 512], P('rows', 'cols'), may hold values from 0 to 1
- first_factor: float32 [192, 256], P('rows', 'cols'), may hold values from -2.5 to 2.5
- second_factor: float32 [512, 256], P('cols', 'rows'), may hold values from -2.5 to 2.5
- third_factor: float32 [512, 256], P(('rows', 'cols')), may hold values from -2.5 to 2.5
Outputs:
- first_new: float32 [192, 256], P('rows', 'cols')
- second_new: float32 [512, 256], P('cols', 'rows')
- third_new: float32 [512, 256], P(('rows', 'cols'))
All inputs are finite; a program needn't handle non-finite values.
Results may differ from a plain program's by a relative error of at most 0.0003.
Values sent between devices are 32-bit elements; how exact they have to be, the bound alone decides.
No kernel may reach another device: no remote copies, remote signals or barrier semaphores. Data moves between devices by JAX's collectives and lax.ppermute only.
A program may use at most 64 MiB of HBM per device.

v0:
```python
import jax
import jax.numpy as jnp
from jax import lax
from jax.sharding import PartitionSpec as P

STEPS = 2


def gather_third(piece):
    return lax.all_gather(piece, ("rows", "cols"), axis=0, tiled=True)


def scatter_third(term):
    return lax.psum_scatter(term, ("rows", "cols"), scatter_dimension=0, tiled=True)


def per_device(tensor, first_factor, second_factor, third_factor):
    high = lax.Precision.HIGHEST
    rows_dev, cols_dev, depth = tensor.shape
    size_i = rows_dev * lax.axis_size("rows")
    size_j = cols_dev * lax.axis_size("cols")
    rate_a = 4.0 / jnp.sqrt(jnp.float32(size_j * depth))
    rate_b = 4.0 / jnp.sqrt(jnp.float32(size_i * depth))
    rate_c = 4.0 / jnp.sqrt(jnp.float32(size_i * size_j))
    flat_target = tensor.reshape(-1, depth)
    shard_a, shard_b = (first_factor, second_factor)
    whole_c = gather_third(third_factor)
    shard_c = third_factor
    for step_index in range(STEPS):
        whole_a = lax.all_gather(shard_a, "cols", axis=1, tiled=True)
        whole_b = lax.all_gather(shard_b, "rows", axis=1, tiled=True)
        if step_index > 0:
            whole_c = gather_third(shard_c)
        khatri = (whole_a[:, None, :] * whole_b[None, :, :]).reshape(-1, whole_a.shape[1])
        model_tile = jnp.dot(khatri, whole_c.T, precision=high, preferred_element_type=jnp.float32)
        deriv = jax.nn.sigmoid(model_tile) - flat_target
        deriv_c = jnp.dot(
            deriv, whole_c, precision=high, preferred_element_type=jnp.float32
        ).reshape(rows_dev, cols_dev, -1)
        term_a = jnp.einsum("ijr,jr->ir", deriv_c, whole_b, precision=high)
        term_b = jnp.einsum("ijr,ir->jr", deriv_c, whole_a, precision=high)
        term_c = lax.dot_general(
            deriv,
            khatri,
            (((0,), (0,)), ((), ())),
            precision=high,
            preferred_element_type=jnp.float32,
        )
        shard_a = shard_a - rate_a * lax.psum_scatter(
            term_a, "cols", scatter_dimension=1, tiled=True
        )
        shard_b = shard_b - rate_b * lax.psum_scatter(
            term_b, "rows", scatter_dimension=1, tiled=True
        )
        shard_c = shard_c - rate_c * scatter_third(term_c)
    return (shard_a, shard_b, shard_c)


def solution(mesh):
    in_specs = (
        P("rows", "cols", None),
        P("rows", "cols"),
        P("cols", "rows"),
        P(("rows", "cols"), None),
    )
    out_specs = (P("rows", "cols"), P("cols", "rows"), P(("rows", "cols"), None))
    return jax.shard_map(
        per_device, mesh=mesh, in_specs=in_specs, out_specs=out_specs, check_vma=False
    )
```

profile of v0, /device:TPU:1, one launch (start us, length us, event | category | flops | bytes accessed | tf_op | source)
XLA Modules:
  0.0 2080.7 jit_solution(13962081747565695190)
XLA Ops:
  8.1 0.8 copy.9
  8.9 41.4 %all_gather.18 = f32[12,256]{0,1:T(8,128)S(1)} all-gather(f32[12,16]{0,1:T(8,128)S(1)} %copy.9), channel_id=1, replica_groups=mesh['rows'=16,'cols'=16] {'cols'}, dimensions={1}, use_global_device_ids=true | all-gather | bytes 13056 | tf_op jit(solution)/shard_map/all_gather | solution.py:30
  50.4 27.0 %all_gather.19 = f32[32,256]{0,1:T(8,128)S(1)} all-gather(f32[32,16]{0,1:T(8,128)} %param.6), channel_id=1, replica_groups=mesh['rows'=16,'cols'=16] {'rows'}, dimensions={1}, use_global_device_ids=true | all-gather | bytes 34816 | tf_op jit(solution)/shard_map/all_gather | solution.py:31
  77.6 592.7 %all-gather = f32[256,2,256]{2,1,0:T(2,128)S(1)} all-gather(f32[1,2,256]{2,1,0:T(2,128)} %bitcast.68), channel_id=1, replica_groups=mesh['rows'=16,'cols'=16] {'rows','cols'}, dimensions={0}, use_global_device_ids=true | all-gather | bytes 526336 | tf_op jit(solution)/shard_map/all_gather | solution.py:10
  670.7 0.9 fusion.7
  671.6 0.8 fusion.11
  673.3 1.2 copy.22
  674.6 2.6 fusion.12
  677.3 2.3 fusion.13
  679.6 214.6 %reduce-scatter.13.cloned.1.call-done = f32[16,12]{1,0:T(8,128)} async-done(((f32[256,12]{1,0:T(8,128)}), f32[16,12]{1,0:T(8,128)}) %reduce-scatter.13.cloned.1.call-update) | async-done | bytes 784
  895.1 35.0 %all_gather.22 = f32[12,256]{0,1:T(8,128)S(1)} all-gather(f32[12,16]{0,1:T(8,128)S(1)} %copy.12), channel_id=1, replica_groups=mesh['rows'=16,'cols'=16] {'cols'}, dimensions={1}, use_global_device_ids=true | all-gather | bytes 13056 | tf_op jit(solution)/shard_map/all_gather | solution.py:30
  930.1 26.0 %reduce-scatter.9.cloned.1.call-done = f32[32,16]{0,1:T(8,128)} async-done(((f32[32,256]{0,1:T(8,128)}), f32[32,16]{0,1:T(8,128)}) %reduce-scatter.9.cloned.1.call-update) | async-done | bytes 2064 | tf_op jit(solution)/shard_map/reduce_scatter | solution.py:52
  956.8 19.8 all_gather.21
  976.8 95.6 %all-reduce.5.cloned.1.call-done = f32[512,256]{1,0:T(8,128)} async-done(((f32[512,256]{1,0:T(8,128)}), f32[512,256]{1,0:T(8,128)}) %all-reduce.5.cloned.1.call-update) | async-done | bytes 524304
  1073.1 599.7 %all-gather.1 = f32[256,2,256]{2,1,0:T(2,128)S(1)} all-gather(f32[1,2,256]{2,1,0:T(2,128)S(1)} %fusion.10), channel_id=1, replica_groups=mesh['rows'=16,'cols'=16] {'rows','cols'}, dimensions={0}, use_global_device_ids=true | all-gather | bytes 526336 | tf_op jit(solution)/shard_map/all_gather | solution.py:10
  1673.1 0.9 fusion.6
  1675.9 1.2 copy.33
  1677.2 2.5 fusion.15
  1679.8 2.3 fusion.16
  1682.1 211.8 %reduce-scatter.15.cloned.1.call-done = f32[16,12]{1,0:T(8,128)} async-done(((f32[256,12]{1,0:T(8,128)}), f32[16,12]{1,0:T(8,128)}) %reduce-scatter.15.cloned.1.call-update) | async-done | bytes 784
  1895.3 60.0 %reduce-scatter.11.cloned.1.call-done = f32[32,16]{0,1:T(8,128)} async-done(((f32[32,256]{0,1:T(8,128)}), f32[32,16]{0,1:T(8,128)}) %reduce-scatter.11.cloned.1.call-update) | async-done | bytes 2064 | tf_op jit(solution)/shard_map/reduce_scatter | solution.py:52
  1955.3 1.3 multiply_subtract_fusion
  1956.6 115.7 %all-reduce.7.cloned.1.call-done = f32[512,256]{1,0:T(8,128)} async-done(((f32[512,256]{1,0:T(8,128)}), f32[512,256]{1,0:T(8,128)}) %all-reduce.7.cloned.1.call-update) | async-done | bytes 524304
  2072.3 1.3 fusion.8
  (52 shorter events, 7.9 us)
Async XLA Ops:
  8.0 662.7 %copy-start.7 = (f32[12,32,512]{2,1,0:T(8,128)S(1)}, f32[12,32,512]{2,1,0:T(8,128)}, u32[]{:S(2)}) copy-start(f32[12,32,512]{2,1,0:T(8,128)} %param.4) | copy-start | bytes 2359300
  8.0 886.2 %reduce-scatter.13.cloned.1.call-start = ((), (), s32[]{:S(2)}) async-start(), calls=%async_computation.6 | async-start | bytes 139264
  670.7 1.8 copy-start.2
  673.3 282.8 %reduce-scatter.9.cloned.1.call-start = ((), (), s32[]{:S(2)}) async-start(), calls=%async_computation.4 | async-start | bytes 139264 | tf_op jit(solution)/shard_map/reduce_scatter | solution.py:52
  674.5 2.7 copy-start.3
  674.6 220.4 %copy-start.5 = (f32[12,16]{1,0:T(8,128)S(1)}, f32[12,16]{1,0:T(8,128)}, u32[]{:S(2)}) copy-start(f32[12,16]{1,0:T(8,128)} %param.5) | copy-start | bytes 2308
  674.6 281.5 %copy-start.4 = (f32[32,16]{0,1:T(8,128)S(1)}, f32[32,16]{0,1:T(8,128)}, u32[]{:S(2)}) copy-start(f32[32,16]{0,1:T(8,128)} %param.6) | copy-start | bytes 6148
  677.2 395.2 %copy-start.6 = (f32[2,256]{1,0:T(2,128)S(1)}, f32[2,256]{1,0:T(2,128)}, u32[]{:S(2)}) copy-start(f32[2,256]{1,0:T(2,128)} %param.7) | copy-start | bytes 6148
  677.2 395.2 %all-reduce.5.cloned.1.call-start = ((), (), s32[]{:S(2)}) async-start(), calls=%async_computation.8 | async-start | bytes 1048576
  679.5 993.6 %copy-start.8 = (f32[12,32,512]{2,1,0:T(8,128)S(1)}, f32[12,32,512]{2,1,0:T(8,128)}, u32[]{:S(2)}) copy-start(f32[12,32,512]{2,1,0:T(8,128)} %param.4) | copy-start | bytes 2359300
  679.5 1214.4 %reduce-scatter.15.cloned.1.call-start = ((), (), s32[]{:S(2)}) async-start(), calls=%async_computation.7 | async-start | bytes 139264
  976.8 697.3 %copy-start = (f32[12,32,256]{2,1,0:T(8,128)}, f32[12,32,256]{2,1,0:T(8,128)S(1)}, u32[]{:S(2)}) copy-start(f32[12,32,256]{2,1,0:T(8,128)S(1)} %broadcast_multiply_fusion) | copy-start | bytes 1179652
  1675.7 279.6 %reduce-scatter.11.cloned.1.call-start = ((), (), s32[]{:S(2)}) async-start(), calls=%async_computation.5 | async-start | bytes 139264 | tf_op jit(solution)/shard_map/reduce_scatter | solution.py:52
  1677.2 2.6 copy-start.1
  1679.7 392.5 %all-reduce.7.cloned.1.call-start = ((), (), s32[]{:S(2)}) async-start(), calls=%async_computation.9 | async-start | bytes 1048576
Sparse Core Ops, SparseCore 0:
  673.4 220.7 reduce-scatter.12
  896.8 59.1 reduce-scatter.8
  1675.8 218.0 reduce-scatter.14
  1896.4 58.8 reduce-scatter.10
Sparse Core Ops, SparseCore 1:
  683.2 389.2 all-reduce.4
  1685.7 386.5 all-reduce.6
where the time goes:
time: 2080 us
  blocking collectives  1320 us (63%)
  waiting for transfers between devices  724 us (35%)
    all_gather x2, blocking collectives, gather_third(): return lax.all_gather(piece, ('rows', 'cols'), axis=0, tiled=True)  1190 us
    unnamed x10, waiting for transfers between devices  638 us
    reduce_scatter x2, waiting for transfers between devices, per_device(): lax.psum_scatter(term_b, 'rows', scatter_dimension=1, tiled=True)  86 us
    all_gather x2, blocking collectives, per_device(): whole_a = lax.all_gather(shard_a, 'cols', axis=1, tiled=True)  76.4 us
    all_gather x2, blocking collectives, per_device(): whole_b = lax.all_gather(shard_b, 'rows', axis=1, tiled=True)  46.9 us
  transfers between devices with their start and end apart: 6, of which 6 were waited for; matrix products, arithmetic and copies ran while one was open for 1% of the time, Pallas kernels for 0%

commit v1 on v0

v1 whole, which is shorter than its diff:
```python
import jax
import jax.numpy as jnp
from jax import lax
from jax.sharding import PartitionSpec as P

STEPS = 2


def exchange(parts, axis):
    return lax.all_to_all(parts, axis, 0, 0, tiled=True)


def per_device(tensor, first_factor, second_factor, third_factor):
    high = lax.Precision.HIGHEST
    n_rows, n_cols = lax.axis_size("rows"), lax.axis_size("cols")
    rows_dev, cols_dev, depth = tensor.shape
    size_i = rows_dev * n_rows
    size_j = cols_dev * n_cols
    rate_a = 4.0 / jnp.sqrt(jnp.float32(size_j * depth))
    rate_b = 4.0 / jnp.sqrt(jnp.float32(size_i * depth))
    rate_c = 4.0 / jnp.sqrt(jnp.float32(size_i * size_j))
    flat_target = tensor.reshape(-1, depth)
    shard_a, shard_b, shard_c = first_factor, second_factor, third_factor
    words_a, words_b = shard_a.size, shard_b.size
    rank = shard_c.shape[1]
    c_words = shard_c.size
    for _ in range(STEPS):
        mine = jnp.concatenate([shard_c.reshape(-1), shard_a.reshape(-1)])
        got = exchange(jnp.broadcast_to(mine[None], (n_cols, mine.size)), "cols")
        piece_c = got[:, :c_words].reshape(-1)
        whole_a = (
            got[:, c_words:].reshape(n_cols, rows_dev, -1).transpose(1, 0, 2).reshape(rows_dev, rank)
        )
        mine = jnp.concatenate([piece_c, shard_b.reshape(-1)])
        got = exchange(jnp.broadcast_to(mine[None], (n_rows, mine.size)), "rows")
        whole_c = got[:, : piece_c.size].reshape(depth, rank)
        whole_b = (
            got[:, piece_c.size :]
            .reshape(n_rows, cols_dev, -1)
            .transpose(1, 0, 2)
            .reshape(cols_dev, rank)
        )
        khatri = (whole_a[:, None, :] * whole_b[None, :, :]).reshape(-1, rank)
        model_tile = jnp.dot(khatri, whole_c.T, precision=high, preferred_element_type=jnp.float32)
        deriv = jax.nn.sigmoid(model_tile) - flat_target
        deriv_c = jnp.dot(
            deriv, whole_c, precision=high, preferred_element_type=jnp.float32
        ).reshape(rows_dev, cols_dev, -1)
        term_a = jnp.einsum("ijr,jr->ir", deriv_c, whole_b, precision=high)
        term_b = jnp.einsum("ijr,ir->jr", deriv_c, whole_a, precision=high)
        term_c = lax.dot_general(
            deriv,
            khatri,
            (((0,), (0,)), ((), ())),
            precision=high,
            preferred_element_type=jnp.float32,
        )
        send = jnp.concatenate(
            [
                term_c.reshape(n_rows, -1),
                term_b.reshape(cols_dev, n_rows, -1).transpose(1, 0, 2).reshape(n_rows, -1),
            ],
            axis=1,
        )
        got = exchange(send, "rows").sum(axis=0)
        part_c = got[: n_cols * c_words]
        shard_b = shard_b - rate_b * got[n_cols * c_words :].reshape(shard_b.shape)
        send = jnp.concatenate(
            [
                part_c.reshape(n_cols, -1),
                term_a.reshape(rows_dev, n_cols, -1).transpose(1, 0, 2).reshape(n_cols, -1),
            ],
            axis=1,
        )
        got = exchange(send, "cols").sum(axis=0)
        shard_c = shard_c - rate_c * got[:c_words].reshape(shard_c.shape)
        shard_a = shard_a - rate_a * got[c_words:].reshape(shard_a.shape)
    return (shard_a, shard_b, shard_c)


def solution(mesh):
    in_specs = (
        P("rows", "cols", None),
        P("rows", "cols"),
        P("cols", "rows"),
        P(("rows", "cols"), None),
    )
    out_specs = (P("rows", "cols"), P("cols", "rows"), P(("rows", "cols"), None))
    return jax.shard_map(
        per_device, mesh=mesh, in_specs=in_specs, out_specs=out_specs, check_vma=False
    )
```

time: 2080 us -> 142 us (0.07)
  blocking collectives: 1320 us -> 11.6 us
  waiting for transfers between devices: 724 us -> 65.5 us
  starting transfers between devices: 0.43 us -> 41.7 us
    all_gather x6 -> x0, blocking collectives: 1320 us -> none  [the longest x2 1190 us: gather_third(): return lax.all_gather(piece, ('rows', 'cols'), axis=0, tiled=True)]
    unnamed x10 -> x0, waiting for transfers between devices: 638 us -> none
    reduce_scatter x2 -> x0, waiting for transfers between devices: 86 us -> none  [per_device(): lax.psum_scatter(term_b, 'rows', scatter_dimension=1, tiled=True)]
    all_to_all x0 -> x7, waiting for transfers between devices: none -> 65.5 us  [exchange(): return lax.all_to_all(parts, axis, 0, 0, tiled=True)]
    all_to_all x0 -> x7, starting transfers between devices: none -> 41.7 us  [exchange(): return lax.all_to_all(parts, axis, 0, 0, tiled=True)]
  transfers between devices with their start and end apart: 6 -> 7, of which waited for: 6 -> 7; matrix products, arithmetic and copies ran while one was open for 1% -> 1% of each run, Pallas kernels for 0% -> 0%
where the time goes in v1:
time: 142 us
  waiting for transfers between devices  65.5 us (46%)
  starting transfers between devices  41.7 us (29%)
  local copies, waits for them, and re-layouts  13.1 us (9%)
  blocking collectives  11.6 us (8%)
  matrix products  6.32 us (4%)
  other arithmetic  2.31 us (2%)
    all_to_all x7, waiting for transfers between devices, exchange(): return lax.all_to_all(parts, axis, 0, 0, tiled=True)  65.5 us
    all_to_all x7, starting transfers between devices, exchange(): return lax.all_to_all(parts, axis, 0, 0, tiled=True)  41.7 us
    all_to_all x1, blocking collectives, exchange(): return lax.all_to_all(parts, axis, 0, 0, tiled=True)  11.6 us
    all_to_all x4, local copies, waits for them, and re-layouts, exchange(): return lax.all_to_all(parts, axis, 0, 0, tiled=True)  3.03 us
    dot_general x2, matrix products, per_device(): lax.dot_general(deriv, khatri, (((0,), (0,)), ((), ())), precision=high,...  2.86 us
  transfers between devices with their start and end apart: 7, of which 7 were waited for; matrix products, arithmetic and copies ran while one was open for 1% of the time, Pallas kernels for 0%

profile of v1, /device:TPU:1, one launch (start us, length us, event | category | flops | bytes accessed | tf_op | source)
XLA Modules:
  0.0 141.6 jit_solution(14058277893729008743)
XLA Ops:
  2.1 11.9 %all-to-all-start = ((f32[16,1,704]{2,1,0:T(1,128)}), f32[16,1,704]{2,1,0:T(1,128)S(1)}, u32[]{:S(2)}, u32[]{:S(2)}) async-start(f32[16,1,704]{2,1,0:T(1,128)} %broadcast_in_dim.8), calls=%async_computation | async-start | bytes 98304 | tf_op jit(solution)/shard_map/all_to_all | solution.py:10
  14.2 8.7 %all-to-all-done = f32[16,1,704]{2,1,0:T(1,128)S(1)} async-done(((f32[16,1,704]{2,1,0:T(1,128)}), f32[16,1,704]{2,1,0:T(1,128)S(1)}, u32[]{:S(2)}, u32[]{:S(2)}) %all-to-all-start) | async-done | bytes 45088 | tf_op jit(solution)/shard_map/all_to_all | solution.py:10
  22.9 1.1 broadcast_in_dim.9
  24.0 6.8 %all-to-all-start.1 = ((f32[16,1,8704]{2,1,0:T(1,128)}), f32[16,1,8704]{2,1,0:T(1,128)S(1)}, u32[]{:S(2)}, u32[]{:S(2)}) async-start(f32[16,1,8704]{2,1,0:T(1,128)} %broadcast_in_dim.9), calls=%async_computation.1 | async-start | bytes 1114112 | tf_op jit(solution)/shard_map/all_to_all | solution.py:10
  31.1 9.9 %all-to-all-done.1 = f32[16,1,8704]{2,1,0:T(1,128)S(1)} async-done(((f32[16,1,8704]{2,1,0:T(1,128)}), f32[16,1,8704]{2,1,0:T(1,128)S(1)}, u32[]{:S(2)}, u32[]{:S(2)}) %all-to-all-start.1) | async-done | bytes 557088 | tf_op jit(solution)/shard_map/all_to_all | solution.py:10
  42.5 0.9 fusion.7
  43.4 1.4 %fusion.8 = f32[512,256]{1,0:T(8,128)S(1)} fusion(f32[384,512]{1,0:T(8,128)S(1)} %fusion.7, f32[384,256]{1,0:T(8,128)S(1)} %bitcast.82), kind=kOutput, calls=%fused_computation.36 | convolution fusion | flops 603979776 | bytes 1703936 | tf_op jit(solution)/shard_map/dot_general | solution.py:51
  44.8 0.8 multiply_reduce_fusion.2
  46.2 1.2 all_to_all.52
  47.4 4.5 %all-to-all-start.2 = ((f32[16,1,8704]{2,1,0:T(1,128)}), f32[16,1,8704]{2,1,0:T(1,128)S(1)}, u32[]{:S(2)}, u32[]{:S(2)}) async-start(f32[16,1,8704]{2,1,0:T(1,128)} %all_to_all.52), calls=%async_computation.2 | async-start | bytes 1114112 | tf_op jit(solution)/shard_map/all_to_all | solution.py:10
  52.2 10.0 %all-to-all-done.2 = f32[16,1,8704]{2,1,0:T(1,128)S(1)} async-done(((f32[16,1,8704]{2,1,0:T(1,128)}), f32[16,1,8704]{2,1,0:T(1,128)S(1)}, u32[]{:S(2)}, u32[]{:S(2)}) %all-to-all-start.2) | async-done | bytes 557088 | tf_op jit(solution)/shard_map/all_to_all | solution.py:10
  62.6 11.6 %all_to_all.72 = f32[16,1,704]{2,1,0:T(1,128)S(1)} all-to-all(f32[16,1,704]{2,1,0:T(1,128)S(1)} %all_to_all.54), channel_id=1, replica_groups=mesh['rows'=16,'cols'=16] {'cols'}, dimensions={0} | all-to-all | bytes 90112 | tf_op jit(solution)/shard_map/all_to_all | solution.py:10
  75.7 3.5 %all-to-all-start.4 = ((f32[16,1,704]{2,1,0:T(1,128)}), f32[16,1,704]{2,1,0:T(1,128)S(1)}, u32[]{:S(2)}, u32[]{:S(2)}) async-start(f32[16,1,704]{2,1,0:T(1,128)} %broadcast_in_dim.10), calls=%async_computation.4 | async-start | bytes 98304 | tf_op jit(solution)/shard_map/all_to_all | solution.py:10
  79.4 8.7 %all-to-all-done.4 = f32[16,1,704]{2,1,0:T(1,128)S(1)} async-done(((f32[16,1,704]{2,1,0:T(1,128)}), f32[16,1,704]{2,1,0:T(1,128)S(1)}, u32[]{:S(2)}, u32[]{:S(2)}) %all-to-all-start.4) | async-done | bytes 45088 | tf_op jit(solution)/shard_map/all_to_all | solution.py:10
  88.1 1.1 broadcast_in_dim.11
  89.2 6.9 %all-to-all-start.5 = ((f32[16,1,8704]{2,1,0:T(1,128)}), f32[16,1,8704]{2,1,0:T(1,128)S(1)}, u32[]{:S(2)}, u32[]{:S(2)}) async-start(f32[16,1,8704]{2,1,0:T(1,128)} %broadcast_in_dim.11), calls=%async_computation.5 | async-start | bytes 1114112 | tf_op jit(solution)/shard_map/all_to_all | solution.py:10
  96.3 10.0 %all-to-all-done.5 = f32[16,1,8704]{2,1,0:T(1,128)S(1)} async-done(((f32[16,1,8704]{2,1,0:T(1,128)}), f32[16,1,8704]{2,1,0:T(1,128)S(1)}, u32[]{:S(2)}, u32[]{:S(2)}) %all-to-all-start.5) | async-done | bytes 557088 | tf_op jit(solution)/shard_map/all_to_all | solution.py:10
  107.1 0.9 fusion.6
  108.0 1.4 %fusion.9 = f32[512,256]{1,0:T(8,128)S(1)} fusion(f32[384,512]{1,0:T(8,128)S(1)} %fusion.6, f32[384,256]{1,0:T(8,128)S(1)} %bitcast.84), kind=kOutput, calls=%fused_computation.37 | convolution fusion | flops 603979776 | bytes 1703936 | tf_op jit(solution)/shard_map/dot_general | solution.py:51
  110.9 1.2 all_to_all.60
  112.0 4.5 %all-to-all-start.6 = ((f32[16,1,8704]{2,1,0:T(1,128)}), f32[16,1,8704]{2,1,0:T(1,128)S(1)}, u32[]{:S(2)}, u32[]{:S(2)}) async-start(f32[16,1,8704]{2,1,0:T(1,128)} %all_to_all.60), calls=%async_computation.6 | async-start | bytes 1114112 | tf_op jit(solution)/shard_map/all_to_all | solution.py:10
  116.8 10.0 %all-to-all-done.6 = f32[16,1,8704]{2,1,0:T(1,128)S(1)} async-done(((f32[16,1,8704]{2,1,0:T(1,128)}), f32[16,1,8704]{2,1,0:T(1,128)S(1)}, u32[]{:S(2)}, u32[]{:S(2)}) %all-to-all-start.6) | async-done | bytes 557088 | tf_op jit(solution)/shard_map/all_to_all | solution.py:10
  127.9 3.5 %all-to-all-start.7 = ((f32[16,1,704]{2,1,0:T(1,128)}), f32[16,1,704]{2,1,0:T(1,128)S(1)}, u32[]{:S(2)}, u32[]{:S(2)}) async-start(f32[16,1,704]{2,1,0:T(1,128)} %all_to_all.62), calls=%async_computation.7 | async-start | bytes 98304 | tf_op jit(solution)/shard_map/all_to_all | solution.py:10
  132.2 8.1 %all-to-all-done.7 = f32[16,1,704]{2,1,0:T(1,128)S(1)} async-done(((f32[16,1,704]{2,1,0:T(1,128)}), f32[16,1,704]{2,1,0:T(1,128)S(1)}, u32[]{:S(2)}, u32[]{:S(2)}) %all-to-all-start.7) | async-done | bytes 45088 | tf_op jit(solution)/shard_map/all_to_all | solution.py:10
  (105 shorter events, 11.7 us)
Async XLA Ops:
  0.6 0.8 copy-start.2
  2.1 11.9 %copy-start.1 = (f32[32,16]{0,1:T(8,128)S(1)}, f32[32,16]{0,1:T(8,128)}, u32[]{:S(2)}) copy-start(f32[32,16]{0,1:T(8,128)} %param.6) | copy-start | bytes 6148
  2.1 20.8 %all-to-all-start = ((f32[16,1,704]{2,1,0:T(1,128)}), f32[16,1,704]{2,1,0:T(1,128)S(1)}, u32[]{:S(2)}, u32[]{:S(2)}) async-start(f32[16,1,704]{2,1,0:T(1,128)} %broadcast_in_dim.8), calls=%async_computation | async-start | bytes 98304 | tf_op jit(solution)/shard_map/all_to_all | solution.py:10
  24.0 17.0 %all-to-all-start.1 = ((f32[16,1,8704]{2,1,0:T(1,128)}), f32[16,1,8704]{2,1,0:T(1,128)S(1)}, u32[]{:S(2)}, u32[]{:S(2)}) async-start(f32[16,1,8704]{2,1,0:T(1,128)} %broadcast_in_dim.9), calls=%async_computation.1 | async-start | bytes 1114112 | tf_op jit(solution)/shard_map/all_to_all | solution.py:10
  41.3 1.1 copy-start.3
  47.4 14.8 %all-to-all-start.2 = ((f32[16,1,8704]{2,1,0:T(1,128)}), f32[16,1,8704]{2,1,0:T(1,128)S(1)}, u32[]{:S(2)}, u32[]{:S(2)}) async-start(f32[16,1,8704]{2,1,0:T(1,128)} %all_to_all.52), calls=%async_computation.2 | async-start | bytes 1114112 | tf_op jit(solution)/shard_map/all_to_all | solution.py:10
  74.3 0.7 copy-start
  75.7 12.3 %all-to-all-start.4 = ((f32[16,1,704]{2,1,0:T(1,128)}), f32[16,1,704]{2,1,0:T(1,128)S(1)}, u32[]{:S(2)}, u32[]{:S(2)}) async-start(f32[16,1,704]{2,1,0:T(1,128)} %broadcast_in_dim.10), calls=%async_computation.4 | async-start | bytes 98304 | tf_op jit(solution)/shard_map/all_to_all | solution.py:10
  89.2 17.2 %all-to-all-start.5 = ((f32[16,1,8704]{2,1,0:T(1,128)}), f32[16,1,8704]{2,1,0:T(1,128)S(1)}, u32[]{:S(2)}, u32[]{:S(2)}) async-start(f32[16,1,8704]{2,1,0:T(1,128)} %broadcast_in_dim.11), calls=%async_computation.5 | async-start | bytes 1114112 | tf_op jit(solution)/shard_map/all_to_all | solution.py:10
  112.0 14.8 %all-to-all-start.6 = ((f32[16,1,8704]{2,1,0:T(1,128)}), f32[16,1,8704]{2,1,0:T(1,128)S(1)}, u32[]{:S(2)}, u32[]{:S(2)}) async-start(f32[16,1,8704]{2,1,0:T(1,128)} %all_to_all.60), calls=%async_computation.6 | async-start | bytes 1114112 | tf_op jit(solution)/shard_map/all_to_all | solution.py:10
  127.9 12.4 %all-to-all-start.7 = ((f32[16,1,704]{2,1,0:T(1,128)}), f32[16,1,704]{2,1,0:T(1,128)S(1)}, u32[]{:S(2)}, u32[]{:S(2)}) async-start(f32[16,1,704]{2,1,0:T(1,128)} %all_to_all.62), calls=%async_computation.7 | async-start | bytes 98304 | tf_op jit(solution)/shard_map/all_to_all | solution.py:10

commit v2 on v0

v2 whole, which is shorter than its diff:
```python
import jax
import jax.numpy as jnp
import numpy as np
from jax import lax
from jax.sharding import Mesh, PartitionSpec as P

STEPS = 2
XY = ("x", "y")
Z = ("zl", "zh")
HIGH = lax.Precision.HIGHEST


def exchange(parts, axis):
    return lax.all_to_all(parts, axis, 0, 0, tiled=True)


def swap(value):
    return lax.ppermute(value, "core", [(0, 1), (1, 0)])


def spread(block, count):
    return jnp.broadcast_to(block[None], (count,) + block.shape)


def fold(ab):
    return ab.reshape(4, 16, 64).transpose(1, 0, 2).reshape(16, 256)


def unfold(folded):
    lead = folded.shape[:-2]
    n = len(lead)
    split = folded.reshape(lead + (16, 4, 64))
    return split.transpose(tuple(range(n)) + (n + 1, n, n + 2)).reshape(lead + (64, 64))


def join_ab(a_t, b_t):
    return jnp.concatenate([a_t, jnp.zeros((a_t.shape[0], 8), jnp.float32), b_t], axis=1)


def per_device(tensor, first_factor, second_factor, third_factor):
    zl, x, core, zh, y = (lax.axis_index(n) for n in ("zl", "x", "core", "zh", "y"))
    n_i, n_j, depth = tensor.shape
    rank = third_factor.shape[1]
    size_i, size_j = n_i * 16, n_j * 16
    rate_a = 4.0 / jnp.sqrt(jnp.float32(size_j * depth))
    rate_b = 4.0 / jnp.sqrt(jnp.float32(size_i * depth))
    rate_c = 4.0 / jnp.sqrt(jnp.float32(size_i * size_j))

    flat = tensor.reshape(-1, depth)
    spot = lax.broadcasted_iota(jnp.int32, (depth, depth), 1)
    half = (spot // 256) ^ core
    xs, ys, zls, zhs, us = (
        (spot // 64) % 4,
        (spot // 16) % 4,
        (spot // 8) % 2,
        (spot // 2) % 4,
        spot % 2,
    )
    source = zls * 256 + xs * 64 + half * 32 + zhs * 8 + ys * 2 + us
    pick = (lax.broadcasted_iota(jnp.int32, (depth, depth), 0) == source).astype(jnp.float32)
    kept = jnp.dot(flat, pick[:, :256], precision=HIGH)
    sent = jnp.dot(flat, pick[:, 256:], precision=HIGH)
    target = jnp.concatenate([kept, swap(sent)], axis=0)

    a_t, b_t = first_factor.T, second_factor.T
    other = swap(jnp.concatenate([a_t, b_t], axis=1))
    a24 = jnp.concatenate([a_t, other[:, :n_i]], axis=1)
    b_other = other[:, n_i:]
    b32 = jnp.where(core == 0, jnp.concatenate([b_t, b_other]), jnp.concatenate([b_other, b_t]))
    ab = join_ab(jnp.concatenate([a24, a24]), b32)
    ab = ab.reshape(2, 16, 64).transpose(1, 0, 2).reshape(8, 256)
    c_pad = jnp.concatenate([third_factor, jnp.zeros((6, rank), jnp.float32)])
    got = exchange(spread(jnp.concatenate([c_pad, ab]), 8).reshape(-1, rank), Z)
    got = got.reshape(2, 4, 16, rank)
    block_c = got[:, :, :2].reshape(16, rank)
    ab = got[:, :, 8:].reshape(2, 4, 16, 2, 64).transpose(0, 1, 3, 2, 4).reshape(2, 4, 32, 64)
    block_a = lax.dynamic_index_in_dim(ab, zl, 0, False)[:, :16, :24].reshape(64, 24)
    block_b = lax.dynamic_index_in_dim(ab, zh, 1, False)[:, :, 32:].reshape(64, n_j)

    for step_index in range(STEPS):
        mine = jnp.concatenate([block_c, fold(join_ab(block_a, block_b))])
        got = exchange(spread(mine, 16).reshape(-1, rank), XY).reshape(4, 4, 32, rank)
        c = got[:, :, :16].reshape(256, rank)
        ab = unfold(got[:, :, 16:])
        a_all = lax.dynamic_index_in_dim(ab, x, 0, False)[:, :, :24]
        a_all = a_all.reshape(4, 4, 16, 24).transpose(1, 0, 2, 3).reshape(rank, 24).T
        b_all = lax.dynamic_index_in_dim(ab, y, 1, False)[:, :, 32:]
        b_all = b_all.reshape(4, 2, 32, n_j).transpose(1, 0, 2, 3).reshape(rank, n_j).T
        khatri = (a_all[:, None, :] * b_all[None, :, :]).reshape(-1, rank)
        model = jnp.dot(khatri, c.T, precision=HIGH, preferred_element_type=jnp.float32)
        deriv = jax.nn.sigmoid(model) - target
        deriv_c = jnp.dot(deriv, c, precision=HIGH, preferred_element_type=jnp.float32)
        deriv_c = deriv_c.reshape(24, n_j, rank)
        grad_a = jnp.sum(deriv_c * b_all[None], axis=1)
        grad_b = jnp.sum(deriv_c * a_all[:, None], axis=0)
        grad_c = lax.dot_general(
            deriv,
            khatri,
            (((0,), (0,)), ((), ())),
            precision=HIGH,
            preferred_element_type=jnp.float32,
        )
        send_a = grad_a.T.reshape(4, 4, 16, 24).transpose(1, 0, 2, 3).reshape(1, 4, 64, 24)
        send_b = grad_b.T.reshape(2, 4, 32, n_j).transpose(1, 0, 2, 3).reshape(4, 1, 64, n_j)
        send = jnp.concatenate(
            [
                jnp.broadcast_to(send_a, (4, 4, 64, 24)),
                jnp.zeros((4, 4, 64, 8), jnp.float32),
                jnp.broadcast_to(send_b, (4, 4, 64, n_j)),
            ],
            axis=3,
        )
        send = send.reshape(4, 4, 4, 16, 64).transpose(0, 1, 3, 2, 4).reshape(4, 4, 16, rank)
        send = jnp.concatenate([grad_c.reshape(4, 4, 16, rank), send], axis=2)
        got = exchange(send.reshape(-1, rank), XY).reshape(4, 4, 32, rank)
        part_c = got[:, :, :16].sum(axis=(0, 1))
        ab = unfold(got[:, :, 16:])
        part_a = lax.dynamic_index_in_dim(ab, x, 0, False)[:, :, :24].sum(axis=0)
        part_b = lax.dynamic_index_in_dim(ab, y, 1, False)[:, :, 32:].sum(axis=0)
        if step_index < STEPS - 1:
            mine = jnp.concatenate([part_c, fold(join_ab(part_a, part_b))])
            got = exchange(spread(mine, 8).reshape(-1, rank), Z).reshape(2, 4, 32, rank)
            block_c = block_c - rate_c * got[:, :, :16].sum(axis=(0, 1))
            ab = unfold(got[:, :, 16:])
            part_a = lax.dynamic_index_in_dim(ab, zl, 0, False)[:, :, :24].sum(axis=0)
            part_b = lax.dynamic_index_in_dim(ab, zh, 1, False)[:, :, 32:].sum(axis=0)
            other = swap(join_ab(part_a, part_b))
            other_a = jnp.concatenate([other[:, 12:24], other[:, :12]], axis=1)
            block_a = block_a - rate_a * (part_a + other_a)
            block_b = block_b - rate_b * (part_b + other[:, 32:])

    send_a = part_a.reshape(1, 4, 16, 24)
    send_b = part_b.reshape(2, 1, 32, n_j)
    send = jnp.concatenate(
        [
            jnp.broadcast_to(jnp.concatenate([send_a, send_a], axis=2), (2, 4, 32, 24)),
            jnp.zeros((2, 4, 32, 8), jnp.float32),
            jnp.broadcast_to(send_b, (2, 4, 32, n_j)),
        ],
        axis=3,
    )
    send = send.reshape(2, 4, 2, 16, 64).transpose(0, 1, 3, 2, 4).reshape(2, 4, 8, rank)
    send_c = jnp.concatenate(
        [part_c.reshape(2, 4, 2, rank), jnp.zeros((2, 4, 6, rank), jnp.float32)], axis=2
    )
    send = jnp.concatenate([send_c, send], axis=2)
    got = exchange(send.reshape(-1, rank), Z).reshape(2, 4, 16, rank)
    grad_c = got[:, :, :2].sum(axis=(0, 1))
    ab = got[:, :, 8:].reshape(2, 4, 16, 2, 64).transpose(0, 1, 3, 2, 4).reshape(2, 4, 32, 64)
    part_a = lax.dynamic_index_in_dim(ab, zl, 0, False)[:, :16, :24].sum(axis=0)
    part_b = lax.dynamic_index_in_dim(ab, zh, 1, False)[:, :, 32:].sum(axis=0)
    part_b = part_b.reshape(2, 16, n_j)
    own_b = lax.dynamic_index_in_dim(part_b, core, 0, False)
    away_b = lax.dynamic_index_in_dim(part_b, 1 - core, 0, False)
    other = swap(jnp.concatenate([part_a[:, 12:], away_b], axis=1))
    old_a = lax.dynamic_index_in_dim(block_a.reshape(4, 16, 24), zh, 0, False)[:, :n_i]
    old_b = lax.dynamic_index_in_dim(block_b.reshape(4, 16, n_j), zl * 2 + core, 0, False)
    old_c = lax.dynamic_index_in_dim(block_c.reshape(8, 2, rank), zl * 4 + zh, 0, False)
    new_a = old_a - rate_a * (part_a[:, :n_i] + other[:, :n_i])
    new_b = old_b - rate_b * (own_b + other[:, n_i:])
    new_c = old_c - rate_c * grad_c
    return (new_a.T, new_b.T, new_c)


def solution(mesh):
    fine = Mesh(mesh.devices.reshape(2, 4, 2, 4, 4), ("zl", "x", "core", "zh", "y"))
    rows, cols = ("zl", "x", "core"), ("zh", "y")
    in_specs = (P(rows, cols, None), P(rows, cols), P(cols, rows), P(rows + cols, None))
    out_specs = (P(rows, cols), P(cols, rows), P(rows + cols, None))
    return jax.shard_map(
        per_device, mesh=fine, in_specs=in_specs, out_specs=out_specs, check_vma=False
    )
```

time: 2080 us -> 138 us (0.07)
  blocking collectives: 1320 us -> 50.4 us
  waiting for transfers between devices: 724 us -> 19.8 us
  starting transfers between devices: 0.43 us -> 31.1 us
    all_gather x6 -> x0, blocking collectives: 1320 us -> none  [the longest x2 1190 us: gather_third(): return lax.all_gather(piece, ('rows', 'cols'), axis=0, tiled=True)]
    unnamed x10 -> x0, waiting for transfers between devices: 638 us -> none
    reduce_scatter x2 -> x0, waiting for transfers between devices: 86 us -> none  [per_device(): lax.psum_scatter(term_b, 'rows', scatter_dimension=1, tiled=True)]
    all_to_all x0 -> x4, blocking collectives: none -> 50.4 us  [exchange(): return lax.all_to_all(parts, axis, 0, 0, tiled=True)]
  transfers between devices with their start and end apart: 6 -> 7, of which waited for: 6 -> 5; matrix products, arithmetic and copies ran while one was open for 1% -> 3% of each run, Pallas kernels for 0% -> 0%
where the time goes in v2:
time: 138 us; the launch traced here: 136 us
  blocking collectives  50.4 us (37%)
  starting transfers between devices  31.1 us (23%)
  waiting for transfers between devices  19.8 us (14%)
  local copies, waits for them, and re-layouts  17.1 us (12%)
  matrix products  10.1 us (7%)
  other arithmetic  6.43 us (5%)
  between operations  1.51 us (1%)
    all_to_all x4, blocking collectives, exchange(): return lax.all_to_all(parts, axis, 0, 0, tiled=True)  50.4 us
    all_to_all x3, waiting for transfers between devices, exchange(): return lax.all_to_all(parts, axis, 0, 0, tiled=True)  19 us
    all_to_all x3, starting transfers between devices, exchange(): return lax.all_to_all(parts, axis, 0, 0, tiled=True)  16.6 us
    ppermute x4, starting transfers between devices, swap(): return lax.ppermute(value, 'core', [(0, 1), (1, 0)])  14.5 us
    unnamed x28, local copies, waits for them, and re-layouts  6.65 us
    dot_general x2, matrix products, per_device(): jnp.dot(khatri, c.T, precision=HIGH, preferred_element_type=jnp.float32)  3.7 us
    dot_general x2, matrix products, per_device(): jnp.dot(deriv, c, precision=HIGH, preferred_element_type=jnp.float32)  3.63 us
  transfers between devices with their start and end apart: 7, of which 5 were waited for; matrix products, arithmetic and copies ran while one was open for 3% of the time, Pallas kernels for 0%

profile of v2, /device:TPU:1, one launch (start us, length us, event | category | flops | bytes accessed | tf_op | source)
XLA Modules:
  0.0 136.5 jit_solution(18051822944093552020)
XLA Ops:
  0.7 0.8 copy.132
  1.6 3.3 %collective-permute-start = (f32[16,44]{1,0:T(8,128)S(1)}, f32[16,44]{1,0:T(8,128)S(1)}, u32[]{:S(2)}, u32[]{:S(2)}) collective-permute-start(f32[16,44]{1,0:T(8,128)S(1)} %pad_maximum_fusion.14), channel_id=1, source_target_pairs={{0,16},{16,0},{1,17},{17,1},{2,18},{18,2},{3,19},{19,3},{4,20},{20... | collective-permute-start | bytes 8456 | tf_op jit(solution)/shard_map/ppermute | solution.py:18
  7.4 6.5 %all-to-all-start = ((f32[8,16,256]{2,1,0:T(8,128)}), f32[8,16,256]{2,1,0:T(8,128)S(1)}, u32[]{:S(2)}, u32[]{:S(2)}) async-start(f32[8,16,256]{2,1,0:T(8,128)} %broadcast_in_dim.42), calls=%async_computation | async-start | bytes 262144 | tf_op jit(solution)/shard_map/all_to_all | solution.py:14
  14.0 6.8 %all-to-all-done = f32[8,16,256]{2,1,0:T(8,128)S(1)} async-done(((f32[8,16,256]{2,1,0:T(8,128)}), f32[8,16,256]{2,1,0:T(8,128)S(1)}, u32[]{:S(2)}, u32[]{:S(2)}) %all-to-all-start) | async-done | bytes 131104 | tf_op jit(solution)/shard_map/all_to_all | solution.py:14
  22.0 0.8 broadcast_in_dim.43
  22.8 6.8 %all-to-all-start.1 = ((f32[16,32,256]{2,1,0:T(8,128)}), f32[16,32,256]{2,1,0:T(8,128)S(1)}, u32[]{:S(2)}, u32[]{:S(2)}) async-start(f32[16,32,256]{2,1,0:T(8,128)} %broadcast_in_dim.43), calls=%async_computation.1 | async-start | bytes 1048576 | tf_op jit(solution)/shard_map/all_to_all | solution.py:14
  30.2 2.0 %collective-permute-start.1 = (f32[384,256]{1,0:T(8,128)S(1)}, f32[384,256]{1,0:T(8,128)}, u32[]{:S(2)}, u32[]{:S(2)}) collective-permute-start(f32[384,256]{1,0:T(8,128)S(1)} %convolution_bitcast_fusion), channel_id=1, source_target_pairs={{0,16},{16,0},{1,17},{17,1},{2,18},{18,2},{3,19},{19,3},{4,20},{20... | collective-permute-start | bytes 1179656 | tf_op jit(solution)/shard_map/ppermute | solution.py:18
  32.8 6.0 %all-to-all-done.1 = f32[16,32,256]{2,1,0:T(8,128)S(1)} async-done(((f32[16,32,256]{2,1,0:T(8,128)}), f32[16,32,256]{2,1,0:T(8,128)S(1)}, u32[]{:S(2)}, u32[]{:S(2)}) %all-to-all-start.1) | async-done | bytes 524320 | tf_op jit(solution)/shard_map/all_to_all | solution.py:14
  40.1 1.9 %fusion.4 = f32[768,256]{1,0:T(8,128)S(1)} fusion(f32[768,256]{1,0:T(8,128)S(1)} %bitcast.201, f32[256,256]{1,0:T(8,128)S(1)} %bitcast.231, f32[384,256]{1,0:T(8,128)} %collective-permute-done.1, f32[384,256]{1,0:T(8,128)S(1)} %convolution_bitcast_fusion.1), kind=kOutput, calls=%fused_computation.26 | convolution fusion | flops 604962816 | bytes 2621440 | tf_op jit(solution)/shard_map/dot_general | solution.py:90
  42.2 1.4 %multiply_reduce_fusion.3 = (f32[24,256]{1,0:T(8,128)}, f32[32,256]{1,0:T(8,128)}) fusion(f32[32,256]{1,0:T(8,128)S(1)} %bitcast.264, f32[24,256]{1,0:T(8,128)S(1)} %bitcast.271, f32[24,32,256]{2,1,0:T(8,128)S(1)} %bitcast.210, f32[256,256,1]{1,0,2:T(8,128)S(1)} %bitcast.232), kind=kOutput, calls=%fused_computation.50 | convolution fusion | flops 604751872 | bytes 1163264 | tf_op jit(solution)/shard_map/dot_general | solution.py:92
  43.7 0.9 reshape.314
  47.3 12.1 %all_to_all.42 = f32[16,32,256]{2,1,0:T(8,128)S(1)} all-to-all(f32[16,32,256]{2,1,0:T(8,128)S(1)} %pad_maximum_fusion.2), channel_id=1, replica_groups=mesh['zl'=2,'x'=4,'core'=2,'zh'=4,'y'=4] {'x','y'}, dimensions={0} | all-to-all | bytes 1048576 | tf_op jit(solution)/shard_map/all_to_all | solution.py:14
  60.2 12.2 %all_to_all.43 = f32[8,32,256]{2,1,0:T(8,128)S(1)} all-to-all(f32[8,32,256]{2,1,0:T(8,128)S(1)} %broadcast_in_dim.94), channel_id=1, replica_groups=mesh['zl'=2,'x'=4,'core'=2,'zh'=4,'y'=4] {'zl','zh'}, dimensions={0} | all-to-all | bytes 524288 | tf_op jit(solution)/shard_map/all_to_all | solution.py:14
  72.8 4.7 %collective-permute-start.2 = (f32[64,64]{1,0:T(8,128)S(1)}, f32[64,64]{1,0:T(8,128)S(1)}, u32[]{:S(2)}, u32[]{:S(2)}) collective-permute-start(f32[64,64]{1,0:T(8,128)S(1)} %pad_maximum_fusion.10), channel_id=1, source_target_pairs={{0,16},{16,0},{1,17},{17,1},{2,18},{18,2},{3,19},{19,3},{4,20},{20... | collective-permute-start | bytes 49160 | tf_op jit(solution)/shard_map/ppermute | solution.py:18
  79.8 13.4 %all_to_all.44 = f32[16,32,256]{2,1,0:T(8,128)S(1)} all-to-all(f32[16,32,256]{2,1,0:T(8,128)S(1)} %broadcast_in_dim.95), channel_id=1, replica_groups=mesh['zl'=2,'x'=4,'core'=2,'zh'=4,'y'=4] {'x','y'}, dimensions={0} | all-to-all | bytes 1048576 | tf_op jit(solution)/shard_map/all_to_all | solution.py:14
  95.4 1.9 %fusion.7 = f32[768,256]{1,0:T(8,128)S(1)} fusion(f32[768,256]{1,0:T(8,128)S(1)} %bitcast.203, f32[256,256]{1,0:T(8,128)S(1)} %bitcast.233, f32[384,256]{1,0:T(8,128)} %collective-permute-done.1, f32[384,256]{1,0:T(8,128)S(1)} %copy-done.2), kind=kOutput, calls=%fused_computation.29 | convolution fusion | flops 604962816 | bytes 2621440 | tf_op jit(solution)/shard_map/dot_general | solution.py:90
  97.6 2.2 %multiply_reduce_fusion.1 = (f32[24,256]{1,0:T(8,128)}, f32[32,256]{1,0:T(8,128)}) fusion(f32[32,256]{1,0:T(8,128)S(1)} %bitcast.266, f32[24,256]{1,0:T(8,128)} %bitcast.273, f32[24,32,256]{2,1,0:T(8,128)S(1)} %bitcast.208, f32[256,256,1]{1,0,2:T(8,128)S(1)} %bitcast.234), kind=kOutput, calls=%fused_computation.48 | convolution fusion | flops 604751872 | bytes 1163264 | tf_op jit(solution)/shard_map/dot_general | solution.py:92
  99.7 0.9 reshape.337
  103.4 12.7 %all_to_all.45 = f32[16,32,256]{2,1,0:T(8,128)S(1)} all-to-all(f32[16,32,256]{2,1,0:T(8,128)S(1)} %pad_maximum_fusion.4), channel_id=1, replica_groups=mesh['zl'=2,'x'=4,'core'=2,'zh'=4,'y'=4] {'x','y'}, dimensions={0} | all-to-all | bytes 1048576 | tf_op jit(solution)/shard_map/all_to_all | solution.py:14
  117.8 3.4 %all-to-all-start.6 = ((f32[8,16,256]{2,1,0:T(8,128)}), f32[8,16,256]{2,1,0:T(8,128)S(1)}, u32[]{:S(2)}, u32[]{:S(2)}) async-start(f32[8,16,256]{2,1,0:T(8,128)} %pad_maximum_fusion.6), calls=%async_computation.6 | async-start | bytes 262144 | tf_op jit(solution)/shard_map/all_to_all | solution.py:14
  122.0 6.1 %all-to-all-done.6 = f32[8,16,256]{2,1,0:T(8,128)S(1)} async-done(((f32[8,16,256]{2,1,0:T(8,128)}), f32[8,16,256]{2,1,0:T(8,128)S(1)}, u32[]{:S(2)}, u32[]{:S(2)}) %all-to-all-start.6) | async-done | bytes 131104 | tf_op jit(solution)/shard_map/all_to_all | solution.py:14
  128.6 4.6 %collective-permute-start.3 = (f32[16,44]{1,0:T(8,128)S(1)}, f32[16,44]{1,0:T(8,128)S(1)}, u32[]{:S(2)}, u32[]{:S(2)}) collective-permute-start(f32[16,44]{1,0:T(8,128)S(1)} %pad_maximum_fusion.15), channel_id=1, source_target_pairs={{0,16},{16,0},{1,17},{17,1},{2,18},{18,2},{3,19},{19,3},{4,20},{20... | collective-permute-start | bytes 8456 | tf_op jit(solution)/shard_map/ppermute | solution.py:18
  133.2 1.2 fusion.46
  135.1 1.4 %fusion.35 = f32[32,16]{0,1:T(8,128)} fusion(f32[16,44]{1,0:T(8,128)S(1)} %collective-permute-done.3, f32[2,16,32]{2,1,0:T(8,128)S(1)} %bitcast.287, s32[]{:T(128)S(6)} %select_n.116, f32[4,16,32]{2,1,0:T(8,128)} %bitcast.274, s32[]{:T(128)S(6)} %select_n.115), kind=kLoop, calls=%fused_computation.115 | loop fusion | flops 1536 | bytes 8200 | tf_op jit(solution)/shard_map/transpose | solution.py:162
  (174 shorter events, 21.1 us)
Async XLA Ops:
  0.6 28.9 %copy-start = (f32[12,32,512]{2,1,0:T(8,128)S(1)}, f32[12,32,512]{2,1,0:T(8,128)}, u32[]{:S(2)}) copy-start(f32[12,32,512]{2,1,0:T(8,128)} %param.4) | copy-start | bytes 2359300
  0.6 0.9 copy-start.11
  1.6 4.1 %collective-permute-start = (f32[16,44]{1,0:T(8,128)S(1)}, f32[16,44]{1,0:T(8,128)S(1)}, u32[]{:S(2)}, u32[]{:S(2)}) collective-permute-start(f32[16,44]{1,0:T(8,128)S(1)} %pad_maximum_fusion.14), channel_id=1, source_target_pairs={{0,16},{16,0},{1,17},{17,1},{2,18},{18,2},{3,19},{19,3},{4,20},{20... | collective-permute-start | bytes 8456 | tf_op jit(solution)/shard_map/ppermute | solution.py:18
  6.0 0.7 copy-start.12
  7.4 13.5 %all-to-all-start = ((f32[8,16,256]{2,1,0:T(8,128)}), f32[8,16,256]{2,1,0:T(8,128)S(1)}, u32[]{:S(2)}, u32[]{:S(2)}) async-start(f32[8,16,256]{2,1,0:T(8,128)} %broadcast_in_dim.42), calls=%async_computation | async-start | bytes 262144 | tf_op jit(solution)/shard_map/all_to_all | solution.py:14
  20.9 0.6 copy-start.9
  22.8 16.0 %all-to-all-start.1 = ((f32[16,32,256]{2,1,0:T(8,128)}), f32[16,32,256]{2,1,0:T(8,128)S(1)}, u32[]{:S(2)}, u32[]{:S(2)}) async-start(f32[16,32,256]{2,1,0:T(8,128)} %broadcast_in_dim.43), calls=%async_computation.1 | async-start | bytes 1048576 | tf_op jit(solution)/shard_map/all_to_all | solution.py:14
  30.2 9.9 %collective-permute-start.1 = (f32[384,256]{1,0:T(8,128)S(1)}, f32[384,256]{1,0:T(8,128)}, u32[]{:S(2)}, u32[]{:S(2)}) collective-permute-start(f32[384,256]{1,0:T(8,128)S(1)} %convolution_bitcast_fusion), channel_id=1, source_target_pairs={{0,16},{16,0},{1,17},{17,1},{2,18},{18,2},{3,19},{19,3},{4,20},{20... | collective-permute-start | bytes 1179656 | tf_op jit(solution)/shard_map/ppermute | solution.py:18
  32.8 7.3 %copy-start.1 = (f32[384,256]{1,0:T(8,128)}, f32[384,256]{1,0:T(8,128)S(1)}, u32[]{:S(2)}) copy-start(f32[384,256]{1,0:T(8,128)S(1)} %convolution_bitcast_fusion.1) | copy-start | bytes 1179652
  44.5 0.7 copy-start.7
  72.8 5.5 %collective-permute-start.2 = (f32[64,64]{1,0:T(8,128)S(1)}, f32[64,64]{1,0:T(8,128)S(1)}, u32[]{:S(2)}, u32[]{:S(2)}) collective-permute-start(f32[64,64]{1,0:T(8,128)S(1)} %pad_maximum_fusion.10), channel_id=1, source_target_pairs={{0,16},{16,0},{1,17},{17,1},{2,18},{18,2},{3,19},{19,3},{4,20},{20... | collective-permute-start | bytes 49160 | tf_op jit(solution)/shard_map/ppermute | solution.py:18
  78.4 0.6 copy-start.3
  79.1 0.6 copy-start.6
  94.4 0.6 copy-start.5
  94.4 1.0 copy-start.2
  100.6 0.7 copy-start.8
  117.8 10.3 %all-to-all-start.6 = ((f32[8,16,256]{2,1,0:T(8,128)}), f32[8,16,256]{2,1,0:T(8,128)S(1)}, u32[]{:S(2)}, u32[]{:S(2)}) async-start(f32[8,16,256]{2,1,0:T(8,128)} %pad_maximum_fusion.6), calls=%async_computation.6 | async-start | bytes 262144 | tf_op jit(solution)/shard_map/all_to_all | solution.py:14
  121.2 0.7 copy-start.10
  121.2 0.8 copy-start.4
  128.6 5.8 %collective-permute-start.3 = (f32[16,44]{1,0:T(8,128)S(1)}, f32[16,44]{1,0:T(8,128)S(1)}, u32[]{:S(2)}, u32[]{:S(2)}) collective-permute-start(f32[16,44]{1,0:T(8,128)S(1)} %pad_maximum_fusion.15), channel_id=1, source_target_pairs={{0,16},{16,0},{1,17},{17,1},{2,18},{18,2},{3,19},{19,3},{4,20},{20... | collective-permute-start | bytes 8456 | tf_op jit(solution)/shard_map/ppermute | solution.py:18

commit v3 on v0

v3 whole, which is shorter than its diff:
```python
import functools

import jax
import jax.numpy as jnp
from jax import lax
from jax.experimental import pallas as pl
from jax.experimental.pallas import tpu as pltpu
from jax.sharding import Mesh, PartitionSpec as P

XY = ("x", "y")
Z = ("zl", "zh")
HIGH = lax.Precision.HIGHEST
F32 = jnp.float32


def exchange(parts, axis):
    shape = parts.shape
    got = lax.all_to_all(parts.reshape(-1, shape[2]), axis, 0, 0, tiled=True)
    return got.reshape(shape)


def swap(value):
    return lax.ppermute(value, "core", [(0, 1), (1, 0)])


def call(body, outs, scratch, index, *operands):
    vmem = pl.BlockSpec(memory_space=pltpu.VMEM)
    return pl.pallas_call(
        body,
        out_shape=[jax.ShapeDtypeStruct(s, F32) for s in outs],
        in_specs=[pl.BlockSpec(memory_space=pltpu.SMEM)] + [vmem] * len(operands),
        out_specs=[vmem] * len(outs),
        scratch_shapes=[pltpu.VMEM(s, F32) for s in scratch],
        compiler_params=pltpu.CompilerParams(vmem_limit_bytes=40 * 1024 * 1024),
    )(index, *operands)


def lanes(rows=16):
    return lax.broadcasted_iota(jnp.int32, (rows, 128), 1)


def split(value):
    top = value.astype(jnp.bfloat16)
    return top, (value - top.astype(F32)).astype(jnp.bfloat16)


def product(left, right, dims):
    (lt, lb), (rt, rb) = left, right
    dot = functools.partial(
        lax.dot_general, dimension_numbers=(dims, ((), ())), preferred_element_type=F32
    )
    return dot(lt, rt) + (dot(lt, rb) + dot(lb, rt))


def slip_of(block, place, zl, zh):
    a = block[16:32, 0:128]
    b = block[16:32, 128:256]
    if zh:
        a = pltpu.roll(a, 128 - 32 * zh, 1)
    if not zl:
        b = pltpu.roll(b, 32, 1)
    at = lanes()
    second = (at // 32) % 2 == 1
    ab = jnp.where(at < 32, a, jnp.where(second, b, 0.0))
    c = block[2 * place : 2 * place + 2, :]
    return c, ab


def first_slip(index, a_ref, bt_ref, c_ref, out_ref, pad):
    core = index[2]
    pad[...] = jnp.zeros((128, 128), F32)
    pad[0:12, 0:16] = a_ref[...]
    at = pad[...].T[0:16, :]
    pad[32:48, 0:32] = bt_ref[...]
    b = pad[32:48, :]
    a = jnp.where(core == 0, at, pltpu.roll(at, 12, 1))
    b = jnp.where(core == 0, pltpu.roll(b, 32, 1), pltpu.roll(b, 96, 1))
    out_ref[0:8, :] = jnp.zeros((8, 128), F32)
    out_ref[0:2, :] = c_ref[:, 0:128]
    out_ref[2:4, :] = c_ref[:, 128:256]
    out_ref[8:24, :] = a + b


def first_pack(index, own_ref, other_ref, out_ref):
    ab = own_ref[8:24, :] + other_ref[8:24, :]
    c = own_ref[0:8, :]
    for p in range(8):
        out_ref[p, 0:8, :] = c
        out_ref[p, 8:24, :] = ab


def block_from_slips(index, got_ref, block_ref, out_ref):
    zl, zh = index[0], index[3]
    for p in range(8):
        block_ref[2 * p : 2 * p + 2, 0:128] = got_ref[p, 0:2, :]
        block_ref[2 * p : 2 * p + 2, 128:256] = got_ref[p, 2:4, :]
    at = lanes()
    a = jnp.zeros((16, 128), F32)
    for q in range(4):
        v = jnp.where(at < 32, got_ref[zl * 4 + q, 8:24, :], 0.0)
        a = a + (pltpu.roll(v, 32 * q, 1) if q else v)
    second = (at // 32) % 2 == 1
    low = jnp.where(second, got_ref[zh, 8:24, :], 0.0)
    high = jnp.where(second, got_ref[4 + zh, 8:24, :], 0.0)
    block_ref[16:32, 0:128] = a
    block_ref[16:32, 128:256] = pltpu.roll(low, 96, 1) + high
    block = block_ref[...]
    for p in range(16):
        out_ref[p] = block


def gradients(index, got_ref, target_ref, out_ref, turn, khatri, terms):
    x, y = index[1], index[4]
    for q in range(4):
        v = got_ref[x * 4 + q, 16:32, 0:128]
        turn[16 * q : 16 * q + 16, :] = v
        turn[64 + 16 * q : 80 + 16 * q, :] = pltpu.roll(v, 96, 1)
    turned = turn[...].T
    a = jnp.concatenate([turned[0:24], turned[64:88]], axis=1)
    for q in range(4):
        v = got_ref[q * 4 + y, 16:32, 128:256]
        turn[32 * q : 32 * q + 16, :] = v
        turn[32 * q + 16 : 32 * q + 32, :] = pltpu.roll(v, 64, 1)
    turned = turn[...].T
    b = jnp.concatenate([turned[0:32], turned[32:64]], axis=1)
    for i in range(24):
        khatri[32 * i : 32 * i + 32, :] = a[i : i + 1, :] * b
    c = split(got_ref[:, 0:16, :].reshape(256, 256))
    parts = split(khatri[...])
    model = product(parts, c, ((1,), (1,)))
    deriv = split(jax.nn.sigmoid(model) - target_ref[...])
    terms[...] = product(deriv, c, ((1,), (0,)))
    grad_c = product(deriv, parts, ((0,), (0,)))
    grad_b = jnp.zeros((32, 256), F32)
    turn[...] = jnp.zeros((128, 128), F32)
    for i in range(24):
        term = terms[32 * i : 32 * i + 32, :]
        grad_b = grad_b + term * a[i : i + 1, :]
        row = jnp.sum(term * b, axis=0, keepdims=True)
        turn[i : i + 1, :] = row[:, 0:128]
        turn[64 + i : 65 + i, :] = row[:, 128:256]
    turned = turn[...].T
    pieces_a = [
        turned[16 * q : 16 * q + 16] + pltpu.roll(turned[64 + 16 * q : 80 + 16 * q], 32, 1)
        for q in range(4)
    ]
    turn[...] = jnp.zeros((128, 128), F32)
    turn[0:32, :] = grad_b[:, 0:128]
    turn[32:64, :] = grad_b[:, 128:256]
    turned = turn[...].T
    pieces_b = [
        turned[32 * q : 32 * q + 16] + pltpu.roll(turned[32 * q + 16 : 32 * q + 32], 64, 1)
        for q in range(4)
    ]
    out_ref[:, 0:16, :] = grad_c.reshape(16, 16, 256)
    for p in range(16):
        out_ref[p, 16:32, 0:128] = pieces_a[p % 4]
        out_ref[p, 16:32, 128:256] = pieces_b[p // 4]


def sum_xy(index, got_ref):
    x, y = index[1], index[4]
    c = jnp.sum(got_ref[:, 0:16, :], axis=0)
    a = got_ref[x * 4, 16:32, 0:128]
    b = got_ref[y, 16:32, 128:256]
    for q in range(1, 4):
        a = a + got_ref[x * 4 + q, 16:32, 0:128]
        b = b + got_ref[q * 4 + y, 16:32, 128:256]
    return c, a, b


def middle_pack(index, got_ref, out_ref):
    c, a, b = sum_xy(index, got_ref)
    for p in range(8):
        out_ref[p, 0:16, :] = c
        out_ref[p, 16:32, 0:128] = a
        out_ref[p, 16:32, 128:256] = b


def middle_sum(index, got_ref, c_ref, ab_ref):
    zl, zh = index[0], index[3]
    c_ref[...] = jnp.sum(got_ref[:, 0:16, :], axis=0)
    a = got_ref[zl * 4, 16:32, 0:128]
    for q in range(1, 4):
        a = a + got_ref[zl * 4 + q, 16:32, 0:128]
    ab_ref[:, 0:128] = a
    ab_ref[:, 128:256] = got_ref[zh, 16:32, 128:256] + got_ref[4 + zh, 16:32, 128:256]


def middle_update(rates, index, block_ref, c_ref, ab_ref, other_ref, slip_ref, out_ref, new):
    rate_a, rate_b, rate_c = rates
    ab = ab_ref[...] + other_ref[...]
    new[0:16, :] = block_ref[0:16, :] - rate_c * c_ref[...]
    new[16:32, 0:128] = block_ref[16:32, 0:128] - rate_a * ab[:, 0:128]
    new[16:32, 128:256] = block_ref[16:32, 128:256] - rate_b * ab[:, 128:256]
    block = new[...]
    for p in range(16):
        out_ref[p] = block
    own = index[0] * 4 + index[3]
    c = jnp.zeros((2, 256), F32)
    ab = jnp.zeros((16, 128), F32)
    for p in range(8):
        c_p, ab_p = slip_of(block, p, p // 4, p % 4)
        c = jnp.where(own == p, c_p, c)
        ab = jnp.where(own == p, ab_p, ab)
    slip_ref[0:8, :] = jnp.zeros((8, 128), F32)
    slip_ref[0:2, :] = c[:, 0:128]
    slip_ref[2:4, :] = c[:, 128:256]
    slip_ref[8:24, :] = ab


def last_pack(index, got_ref, out_ref, new):
    c, a, b = sum_xy(index, got_ref)
    new[0:16, :] = c
    new[16:32, 0:128] = a
    new[16:32, 128:256] = b
    block = new[...]
    for p in range(8):
        c_p, ab_p = slip_of(block, p, p // 4, p % 4)
        out_ref[p, 0:8, :] = jnp.zeros((8, 128), F32)
        out_ref[p, 0:2, :] = c_p[:, 0:128]
        out_ref[p, 2:4, :] = c_p[:, 128:256]
        out_ref[p, 8:24, :] = ab_p


def last_sum(index, got_ref, slip_ref):
    zl, zh = index[0], index[3]
    c = got_ref[0, 0:8, :]
    for p in range(1, 8):
        c = c + got_ref[p, 0:8, :]
    a = got_ref[zl * 4, 8:24, :]
    for q in range(1, 4):
        a = a + got_ref[zl * 4 + q, 8:24, :]
    b = got_ref[zh, 8:24, :] + got_ref[4 + zh, 8:24, :]
    slip_ref[0:8, :] = c
    slip_ref[8:24, :] = jnp.where(lanes() < 32, a, b)


def last_update(rates, index, old_ref, grad_ref, other_ref, a_ref, bt_ref, c_ref, pad):
    rate_a, rate_b, rate_c = rates
    core = index[2]
    c = old_ref[0:8, :] - rate_c * grad_ref[0:8, :]
    c_ref[:, 0:128] = c[0:2, :]
    c_ref[:, 128:256] = c[2:4, :]
    rate = jnp.where(lanes() < 32, rate_a, rate_b)
    ab = old_ref[8:24, :] - rate * (grad_ref[8:24, :] + other_ref[8:24, :])
    b = jnp.where(core == 0, pltpu.roll(ab, 96, 1), pltpu.roll(ab, 32, 1))
    bt_ref[...] = b[:, 0:32]
    pad[...] = jnp.zeros((128, 128), F32)
    pad[0:16, :] = jnp.where(core == 0, ab, pltpu.roll(ab, 116, 1))
    turned = pad[...].T
    a_ref[...] = turned[0:12, 0:16]


def arrange_target(tensor, core):
    depth = tensor.shape[2]
    flat = tensor.reshape(-1, depth)
    spot = lax.broadcasted_iota(jnp.int32, (depth, depth), 1)
    half = (spot // 256) ^ core
    xs, ys = (spot // 64) % 4, (spot // 16) % 4
    zls, zhs, us = (spot // 8) % 2, (spot // 2) % 4, spot % 2
    source = zls * 256 + xs * 64 + half * 32 + zhs * 8 + ys * 2 + us
    pick = (lax.broadcasted_iota(jnp.int32, (depth, depth), 0) == source).astype(F32)
    kept = jnp.dot(flat, pick[:, :256], precision=HIGH)
    came = swap(jnp.dot(flat, pick[:, 256:], precision=HIGH))
    return jnp.concatenate(
        [jnp.where(core == 0, kept, came), jnp.where(core == 0, came, kept)], axis=0
    )


def per_device(tensor, first_factor, second_factor, third_factor):
    index = jnp.stack([lax.axis_index(n) for n in ("zl", "x", "core", "zh", "y")])
    n_i, n_j, depth = tensor.shape
    size_i, size_j = n_i * 16, n_j * 16
    rates = tuple(4.0 / float(n) ** 0.5 for n in (size_j * depth, size_i * depth, size_i * size_j))
    wide = (16, 32, 256)
    square = (128, 128)

    (slip,) = call(first_slip, [(24, 128)], [square], index, first_factor, second_factor.T, third_factor)
    (send,) = call(first_pack, [(8, 24, 128)], [], index, slip, swap(slip))
    got = exchange(send, Z)
    target = arrange_target(tensor, index[2])
    block, send = call(block_from_slips, [(32, 256), wide], [], index, got)
    grads_scratch = [square, (768, 256), (768, 256)]

    (send,) = call(gradients, [wide], grads_scratch, index, exchange(send, XY), target)
    (send,) = call(middle_pack, [(8, 32, 256)], [], index, exchange(send, XY))
    grad_c, grad_ab = call(middle_sum, [(16, 256), (16, 256)], [], index, exchange(send, Z))
    slip, send = call(
        functools.partial(middle_update, rates),
        [(24, 128), wide],
        [(32, 256)],
        index,
        block,
        grad_c,
        grad_ab,
        swap(grad_ab),
    )
    (send,) = call(gradients, [wide], grads_scratch, index, exchange(send, XY), target)
    (send,) = call(last_pack, [(8, 24, 128)], [(32, 256)], index, exchange(send, XY))
    (grad,) = call(last_sum, [(24, 128)], [], index, exchange(send, Z))
    new_a, new_bt, new_c = call(
        functools.partial(last_update, rates),
        [(n_i, 16), (16, n_j), third_factor.shape],
        [square],
        index,
        slip,
        grad,
        swap(grad),
    )
    return (new_a, new_bt.T, new_c)


def solution(mesh):
    fine = Mesh(mesh.devices.reshape(2, 4, 2, 4, 4), ("zl", "x", "core", "zh", "y"))
    rows, cols = ("zl", "x", "core"), ("zh", "y")
    in_specs = (P(rows, cols, None), P(rows, cols), P(cols, rows), P(rows + cols, None))
    out_specs = (P(rows, cols), P(cols, rows), P(rows + cols, None))
    return jax.shard_map(
        per_device, mesh=fine, in_specs=in_specs, out_specs=out_specs, check_vma=False
    )
```

time: 2080 us -> 120 us (0.06)
  blocking collectives: 1320 us -> 73.3 us
  waiting for transfers between devices: 724 us -> 11.2 us
    all_gather x6 -> x0, blocking collectives: 1320 us -> none  [the longest x2 1190 us: gather_third(): return lax.all_gather(piece, ('rows', 'cols'), axis=0, tiled=True)]
    unnamed x10 -> x0, waiting for transfers between devices: 638 us -> none
    reduce_scatter x2 -> x0, waiting for transfers between devices: 86 us -> none  [per_device(): lax.psum_scatter(term_b, 'rows', scatter_dimension=1, tiled=True)]
    all_to_all x0 -> x6, blocking collectives: none -> 73.3 us  [exchange(): got = lax.all_to_all(parts.reshape(-1, shape[2]), axis, 0, 0, tiled=True)]
  transfers between devices with their start and end apart: 6 -> 5, of which waited for: 6 -> 4; matrix products, arithmetic and copies ran while one was open for 1% -> 1% of each run, Pallas kernels for 0% -> 2%
where the time goes in v3:
time: 120 us; the launch traced here: 119 us
  blocking collectives  73.3 us (61%)
  starting transfers between devices  19.6 us (16%)
  Pallas kernels  11.6 us (10%)
  waiting for transfers between devices  11.2 us (9%)
  local copies, waits for them, and re-layouts  1.52 us (1%)
    all_to_all x6, blocking collectives, exchange(): got = lax.all_to_all(parts.reshape(-1, shape[2]), axis, 0, 0, tiled=True)  73.3 us
    ppermute x4, starting transfers between devices, swap(): return lax.ppermute(value, 'core', [(0, 1), (1, 0)])  12.8 us
    pallas_call x11, Pallas kernels, call(): pl.pallas_call(body, out_shape=[jax.ShapeDtypeStruct(s, F32) for s in out...  11.6 us
    all_to_all x1, waiting for transfers between devices, exchange(): got = lax.all_to_all(parts.reshape(-1, shape[2]), axis, 0, 0, tiled=True)  8.33 us
    all_to_all x1, starting transfers between devices, exchange(): got = lax.all_to_all(parts.reshape(-1, shape[2]), axis, 0, 0, tiled=True)  6.75 us
    ppermute x4, waiting for transfers between devices, swap(): return lax.ppermute(value, 'core', [(0, 1), (1, 0)])  2.83 us
  transfers between devices with their start and end apart: 5, of which 4 were waited for; matrix products, arithmetic and copies ran while one was open for 1% of the time, Pallas kernels for 2%

profile of v3, /device:TPU:1, one launch (start us, length us, event | category | flops | bytes accessed | tf_op | source)
XLA Modules:
  0.0 119.4 jit_solution(10860653608873494341)
XLA Ops:
  1.0 0.8 copy-done
  2.3 3.3 %collective-permute-start.1 = (f32[384,256]{1,0:T(8,128)S(1)}, f32[384,256]{1,0:T(8,128)S(1)}, u32[]{:S(2)}, u32[]{:S(2)}) collective-permute-start(f32[384,256]{1,0:T(8,128)S(1)} %convolution_bitcast_fusion), channel_id=1, source_target_pairs={{0,16},{16,0},{1,17},{17,1},{2,18},{18,2},{3,19},{19,3},{4,20},{20... | collective-permute-start | bytes 1179656 | tf_op jit(solution)/shard_map/ppermute | solution.py:23
  5.8 0.6 copy-done.3
  6.4 0.7 shard_map.67.own_ref
  7.1 1.2 collective-permute-done.other_ref
  8.8 13.2 %all_to_all.42.got_ref = f32[8,24,128]{2,1,0:T(8,128)S(1)} all-to-all(f32[8,24,128]{2,1,0:T(8,128)S(1)} %shard_map.68), channel_id=1, replica_groups=mesh['zl'=2,'x'=4,'core'=2,'zh'=4,'y'=4] {'zl','zh'}, dimensions={0} | all-to-all | bytes 196608 | tf_op jit(solution)/shard_map/all_to_all | solution.py:18
  22.0 1.4 %shard_map.69 = (f32[32,256]{1,0:T(8,128)S(1)}, f32[16,32,256]{2,1,0:T(8,128)}) custom-call(s32[5]{0:T(128)S(1)} %stack.23.index, f32[8,24,128]{2,1,0:T(8,128)S(1)} %all_to_all.42.got_ref), custom_call_target="tpu_custom_call" | custom-call | tf_op jit(solution)/shard_map/pallas_call | solution.py:28
  23.4 6.8 %all-to-all-start.1 = ((f32[16,32,256]{2,1,0:T(8,128)}), f32[16,32,256]{2,1,0:T(8,128)S(1)}, u32[]{:S(2)}, u32[]{:S(2)}) async-start(f32[16,32,256]{2,1,0:T(8,128)} %get-tuple-element.13), calls=%async_computation.1 | async-start | bytes 1048576 | tf_op jit(solution)/shard_map/all_to_all | solution.py:18
  30.2 0.6 broadcast_select_fusion.1
  30.9 8.3 %all-to-all-done.1.got_ref = f32[16,32,256]{2,1,0:T(8,128)S(1)} async-done(((f32[16,32,256]{2,1,0:T(8,128)}), f32[16,32,256]{2,1,0:T(8,128)S(1)}, u32[]{:S(2)}, u32[]{:S(2)}) %all-to-all-start.1) | async-done | bytes 524320 | tf_op jit(solution)/shard_map/all_to_all | solution.py:18
  39.2 2.4 %shard_map.70 = f32[16,32,256]{2,1,0:T(8,128)S(1)} custom-call(s32[5]{0:T(128)S(1)} %stack.23.index, f32[16,32,256]{2,1,0:T(8,128)S(1)} %all-to-all-done.1.got_ref, f32[768,256]{1,0:T(8,128)S(1)} %pad_maximum_fusion.target_ref), custom_call_target="tpu_custom_call" | custom-call | tf_op jit(solution)/shard_map/pallas_call | solution.py:28
  41.6 12.8 %all_to_all.43.got_ref = f32[16,32,256]{2,1,0:T(8,128)S(1)} all-to-all(f32[16,32,256]{2,1,0:T(8,128)S(1)} %shard_map.70), channel_id=1, replica_groups=mesh['zl'=2,'x'=4,'core'=2,'zh'=4,'y'=4] {'x','y'}, dimensions={0} | all-to-all | bytes 1048576 | tf_op jit(solution)/shard_map/all_to_all | solution.py:18
  54.9 11.4 %all_to_all.44.got_ref = f32[8,32,256]{2,1,0:T(8,128)S(1)} all-to-all(f32[8,32,256]{2,1,0:T(8,128)S(1)} %shard_map.71), channel_id=1, replica_groups=mesh['zl'=2,'x'=4,'core'=2,'zh'=4,'y'=4] {'zl','zh'}, dimensions={0} | all-to-all | bytes 524288 | tf_op jit(solution)/shard_map/all_to_all | solution.py:18
  66.9 4.8 %collective-permute-start.2 = (f32[16,256]{1,0:T(8,128)S(1)}, f32[16,256]{1,0:T(8,128)S(1)}, u32[]{:S(2)}, u32[]{:S(2)}) collective-permute-start(f32[16,256]{1,0:T(8,128)S(1)} %get-tuple-element.15.ab_ref), channel_id=1, source_target_pairs={{0,16},{16,0},{1,17},{17,1},{2,18},{18,2},{3,19},{19,3},{4,20},{20... | collective-permute-start | bytes 49160 | tf_op jit(solution)/shard_map/ppermute | solution.py:23
  71.7 0.8 collective-permute-done.2.other_ref
  72.5 0.6 shard_map.73
  73.1 13.3 %all_to_all.45.got_ref = f32[16,32,256]{2,1,0:T(8,128)S(1)} all-to-all(f32[16,32,256]{2,1,0:T(8,128)S(1)} %get-tuple-element.17), channel_id=1, replica_groups=mesh['zl'=2,'x'=4,'core'=2,'zh'=4,'y'=4] {'x','y'}, dimensions={0} | all-to-all | bytes 1048576 | tf_op jit(solution)/shard_map/all_to_all | solution.py:18
  86.5 2.4 %shard_map.74 = f32[16,32,256]{2,1,0:T(8,128)S(1)} custom-call(s32[5]{0:T(128)S(1)} %stack.23.index, f32[16,32,256]{2,1,0:T(8,128)S(1)} %all_to_all.45.got_ref, f32[768,256]{1,0:T(8,128)S(1)} %pad_maximum_fusion.target_ref), custom_call_target="tpu_custom_call" | custom-call | tf_op jit(solution)/shard_map/pallas_call | solution.py:28
  88.8 12.7 %all_to_all.46.got_ref = f32[16,32,256]{2,1,0:T(8,128)S(1)} all-to-all(f32[16,32,256]{2,1,0:T(8,128)S(1)} %shard_map.74), channel_id=1, replica_groups=mesh['zl'=2,'x'=4,'core'=2,'zh'=4,'y'=4] {'x','y'}, dimensions={0} | all-to-all | bytes 1048576 | tf_op jit(solution)/shard_map/all_to_all | solution.py:18
  101.5 0.6 shard_map.75
  102.2 9.9 %all_to_all.47.got_ref = f32[8,24,128]{2,1,0:T(8,128)S(1)} all-to-all(f32[8,24,128]{2,1,0:T(8,128)S(1)} %shard_map.75), channel_id=1, replica_groups=mesh['zl'=2,'x'=4,'core'=2,'zh'=4,'y'=4] {'zl','zh'}, dimensions={0} | all-to-all | bytes 196608 | tf_op jit(solution)/shard_map/all_to_all | solution.py:18
  112.6 4.7 %collective-permute-start.3 = (f32[24,128]{1,0:T(8,128)S(1)}, f32[24,128]{1,0:T(8,128)S(1)}, u32[]{:S(2)}, u32[]{:S(2)}) collective-permute-start(f32[24,128]{1,0:T(8,128)S(1)} %shard_map.76.grad_ref), channel_id=1, source_target_pairs={{0,16},{16,0},{1,17},{17,1},{2,18},{18,2},{3,19},{19,3},{4,20},{20... | collective-permute-start | bytes 36872 | tf_op jit(solution)/shard_map/ppermute | solution.py:23
  117.3 0.8 collective-permute-done.3.other_ref
  118.1 1.3 %shard_map.77 = (f32[12,16]{1,0:T(8,128)}, f32[16,32]{1,0:T(8,128)}, f32[2,256]{1,0:T(2,128)}) custom-call(s32[5]{0:T(128)S(1)} %stack.23.index, f32[24,128]{1,0:T(8,128)S(1)} %get-tuple-element.16.old_ref, f32[24,128]{1,0:T(8,128)S(1)} %shard_map.76.grad_ref, f32[24,128]{1,0:T(8,128)S(1)} %collective-permute-done.3.other_ref), custom_call_target="tpu_custom_call" | custom-call | tf_op jit(solution)/shard_map/pallas_call | solution.py:28
  (25 shorter events, 3.3 us)
Async XLA Ops:
  0.6 1.1 copy-start
  2.3 27.9 %collective-permute-start.1 = (f32[384,256]{1,0:T(8,128)S(1)}, f32[384,256]{1,0:T(8,128)S(1)}, u32[]{:S(2)}, u32[]{:S(2)}) collective-permute-start(f32[384,256]{1,0:T(8,128)S(1)} %convolution_bitcast_fusion), channel_id=1, source_target_pairs={{0,16},{16,0},{1,17},{17,1},{2,18},{18,2},{3,19},{19,3},{4,20},{20... | collective-permute-start | bytes 1179656 | tf_op jit(solution)/shard_map/ppermute | solution.py:23
  5.7 0.7 copy-start.3
  5.7 0.7 copy-start.1
  5.7 0.7 copy-start.2
  7.1 1.2 %collective-permute-start = (f32[24,128]{1,0:T(8,128)S(1)}, f32[24,128]{1,0:T(8,128)S(1)}, u32[]{:S(2)}, u32[]{:S(2)}) collective-permute-start(f32[24,128]{1,0:T(8,128)S(1)} %shard_map.67.own_ref), channel_id=1, source_target_pairs={{0,16},{16,0},{1,17},{17,1},{2,18},{18,2},{3,19},{19,3},{4,20},{20... | collective-permute-start | bytes 36872 | tf_op jit(solution)/shard_map/ppermute | solution.py:23
  23.4 15.8 %all-to-all-start.1 = ((f32[16,32,256]{2,1,0:T(8,128)}), f32[16,32,256]{2,1,0:T(8,128)S(1)}, u32[]{:S(2)}, u32[]{:S(2)}) async-start(f32[16,32,256]{2,1,0:T(8,128)} %get-tuple-element.13), calls=%async_computation.1 | async-start | bytes 1048576 | tf_op jit(solution)/shard_map/all_to_all | solution.py:18
  66.9 5.6 %collective-permute-start.2 = (f32[16,256]{1,0:T(8,128)S(1)}, f32[16,256]{1,0:T(8,128)S(1)}, u32[]{:S(2)}, u32[]{:S(2)}) collective-permute-start(f32[16,256]{1,0:T(8,128)S(1)} %get-tuple-element.15.ab_ref), channel_id=1, source_target_pairs={{0,16},{16,0},{1,17},{17,1},{2,18},{18,2},{3,19},{19,3},{4,20},{20... | collective-permute-start | bytes 49160 | tf_op jit(solution)/shard_map/ppermute | solution.py:23
  112.6 5.5 %collective-permute-start.3 = (f32[24,128]{1,0:T(8,128)S(1)}, f32[24,128]{1,0:T(8,128)S(1)}, u32[]{:S(2)}, u32[]{:S(2)}) collective-permute-start(f32[24,128]{1,0:T(8,128)S(1)} %shard_map.76.grad_ref), channel_id=1, source_target_pairs={{0,16},{16,0},{1,17},{17,1},{2,18},{18,2},{3,19},{19,3},{4,20},{20... | collective-permute-start | bytes 36872 | tf_op jit(solution)/shard_map/ppermute | solution.py:23

commit v4 on v3

--- a/solution.py
+++ b/solution.py
@@ -50,6 +50,22 @@
         lax.dot_general, dimension_numbers=(dims, ((), ())), preferred_element_type=F32
     )
     return dot(lt, rt) + (dot(lt, rb) + dot(lb, rt))
+
+
+def fill_slot(ref, p, value):
+    ref[p, 16:24, 0:128] = value[0:8]
+    ref[p, 16:24, 128:256] = value[8:16]
+
+
+def slot(ref, p):
+    v = ref[p, 16:24, :]
+    return jnp.concatenate([v[:, 0:128], v[:, 128:256]], axis=0)
+
+
+def send_block(block, out_ref, x):
+    for p in range(16):
+        out_ref[p, 0:16, :] = block[0:16]
+        fill_slot(out_ref, p, jnp.where(x == p // 4, block[16:32, 0:128], block[16:32, 128:256]))
 
 
 def slip_of(block, place, zl, zh):
@@ -89,8 +105,9 @@
         out_ref[p, 8:24, :] = ab
 
 
-def block_from_slips(index, got_ref, block_ref, out_ref):
+def block_from_slips(index, got_ref, block_ref, out_ref, core_ref):
     zl, zh = index[0], index[3]
+    core_ref[...] = jnp.full((8, 128), index[2], jnp.int32).astype(F32)
     for p in range(8):
         block_ref[2 * p : 2 * p + 2, 0:128] = got_ref[p, 0:2, :]
         block_ref[2 * p : 2 * p + 2, 128:256] = got_ref[p, 2:4, :]
@@ -104,41 +121,45 @@
     high = jnp.where(second, got_ref[4 + zh, 8:24, :], 0.0)
     block_ref[16:32, 0:128] = a
     block_ref[16:32, 128:256] = pltpu.roll(low, 96, 1) + high
-    block = block_ref[...]
-    for p in range(16):
-        out_ref[p] = block
-
-
-def gradients(index, got_ref, target_ref, out_ref, turn, khatri, terms):
-    x, y = index[1], index[4]
-    for q in range(4):
-        v = got_ref[x * 4 + q, 16:32, 0:128]
+    send_block(block_ref[...], out_ref, index[1])
+
+
+def gradients(
+    index, got_ref, block_ref, kept_ref, came_ref, out_ref, own_ref, turn, khatri, terms, first
+):
+    x, core, y = index[1], index[2], index[4]
+    order = [i + 12 * core if i < 12 else i - 12 * core for i in range(24)]
+    for q in range(4):
+        v = jnp.where(y == q, block_ref[16:32, 0:128], slot(got_ref, x * 4 + q))
         turn[16 * q : 16 * q + 16, :] = v
         turn[64 + 16 * q : 80 + 16 * q, :] = pltpu.roll(v, 96, 1)
     turned = turn[...].T
-    a = jnp.concatenate([turned[0:24], turned[64:88]], axis=1)
-    for q in range(4):
-        v = got_ref[q * 4 + y, 16:32, 128:256]
+    first[:, 0:128] = turned[0:24]
+    first[:, 128:256] = turned[64:88]
+    a = [first[pl.ds(i, 1), :] for i in order]
+    for q in range(4):
+        v = jnp.where(x == q, block_ref[16:32, 128:256], slot(got_ref, q * 4 + y))
         turn[32 * q : 32 * q + 16, :] = v
         turn[32 * q + 16 : 32 * q + 32, :] = pltpu.roll(v, 64, 1)
     turned = turn[...].T
     b = jnp.concatenate([turned[0:32], turned[32:64]], axis=1)
     for i in range(24):
-        khatri[32 * i : 32 * i + 32, :] = a[i : i + 1, :] * b
+        khatri[32 * i : 32 * i + 32, :] = a[i] * b
     c = split(got_ref[:, 0:16, :].reshape(256, 256))
     parts = split(khatri[...])
     model = product(parts, c, ((1,), (1,)))
-    deriv = split(jax.nn.sigmoid(model) - target_ref[...])
+    target = jnp.concatenate([kept_ref[...], came_ref[...]], axis=0)
+    deriv = split(jax.nn.sigmoid(model) - target)
     terms[...] = product(deriv, c, ((1,), (0,)))
     grad_c = product(deriv, parts, ((0,), (0,)))
     grad_b = jnp.zeros((32, 256), F32)
     turn[...] = jnp.zeros((128, 128), F32)
     for i in range(24):
         term = terms[32 * i : 32 * i + 32, :]
-        grad_b = grad_b + term * a[i : i + 1, :]
+        grad_b = grad_b + term * a[i]
         row = jnp.sum(term * b, axis=0, keepdims=True)
-        turn[i : i + 1, :] = row[:, 0:128]
-        turn[64 + i : 65 + i, :] = row[:, 128:256]
+        turn[pl.ds(order[i], 1), :] = row[:, 0:128]
+        turn[pl.ds(order[i] + 64, 1), :] = row[:, 128:256]
     turned = turn[...].T
     pieces_a = [
         turned[16 * q : 16 * q + 16] + pltpu.roll(turned[64 + 16 * q : 80 + 16 * q], 32, 1)
@@ -154,48 +175,53 @@
     ]
     out_ref[:, 0:16, :] = grad_c.reshape(16, 16, 256)
     for p in range(16):
-        out_ref[p, 16:32, 0:128] = pieces_a[p % 4]
-        out_ref[p, 16:32, 128:256] = pieces_b[p // 4]
-
-
-def sum_xy(index, got_ref):
+        fill_slot(out_ref, p, jnp.where(x == p // 4, pieces_a[p % 4], pieces_b[p // 4]))
+    own_a, own_b = pieces_a[0], pieces_b[0]
+    for q in range(1, 4):
+        own_a = jnp.where(y == q, pieces_a[q], own_a)
+        own_b = jnp.where(x == q, pieces_b[q], own_b)
+    own_ref[:, 0:128] = own_a
+    own_ref[:, 128:256] = own_b
+
+
+def sum_xy(index, got_ref, own_ref):
     x, y = index[1], index[4]
     c = jnp.sum(got_ref[:, 0:16, :], axis=0)
-    a = got_ref[x * 4, 16:32, 0:128]
-    b = got_ref[y, 16:32, 128:256]
-    for q in range(1, 4):
-        a = a + got_ref[x * 4 + q, 16:32, 0:128]
-        b = b + got_ref[q * 4 + y, 16:32, 128:256]
+    a, b = own_ref[:, 0:128], own_ref[:, 128:256]
+    for q in range(4):
+        a = a + jnp.where(y == q, 0.0, slot(got_ref, x * 4 + q))
+        b = b + jnp.where(x == q, 0.0, slot(got_ref, q * 4 + y))
     return c, a, b
 
 
-def middle_pack(index, got_ref, out_ref):
-    c, a, b = sum_xy(index, got_ref)
+def middle_pack(index, got_ref, own_ref, out_ref, sum_ref):
+    c, a, b = sum_xy(index, got_ref, own_ref)
     for p in range(8):
         out_ref[p, 0:16, :] = c
-        out_ref[p, 16:32, 0:128] = a
-        out_ref[p, 16:32, 128:256] = b
-
-
-def middle_sum(index, got_ref, c_ref, ab_ref):
+        fill_slot(out_ref, p, jnp.where(index[0] == p // 4, a, b))
+    sum_ref[:, 0:128] = a
+    sum_ref[:, 128:256] = b
+
+
+def middle_sum(index, got_ref, own_ref, c_ref, ab_ref):
     zl, zh = index[0], index[3]
     c_ref[...] = jnp.sum(got_ref[:, 0:16, :], axis=0)
-    a = got_ref[zl * 4, 16:32, 0:128]
-    for q in range(1, 4):
-        a = a + got_ref[zl * 4 + q, 16:32, 0:128]
+    a = own_ref[:, 0:128]
+    for q in range(4):
+        a = a + jnp.where(zh == q, 0.0, slot(got_ref, zl * 4 + q))
     ab_ref[:, 0:128] = a
-    ab_ref[:, 128:256] = got_ref[zh, 16:32, 128:256] + got_ref[4 + zh, 16:32, 128:256]
-
-
-def middle_update(rates, index, block_ref, c_ref, ab_ref, other_ref, slip_ref, out_ref, new):
+    ab_ref[:, 128:256] = own_ref[:, 128:256] + slot(got_ref, (1 - zl) * 4 + zh)
+
+
+def middle_update(rates, index, block_ref, c_ref, ab_ref, other_ref, slip_ref, block_out, out_ref, new):
     rate_a, rate_b, rate_c = rates
     ab = ab_ref[...] + other_ref[...]
     new[0:16, :] = block_ref[0:16, :] - rate_c * c_ref[...]
     new[16:32, 0:128] = block_ref[16:32, 0:128] - rate_a * ab[:, 0:128]
     new[16:32, 128:256] = block_ref[16:32, 128:256] - rate_b * ab[:, 128:256]
     block = new[...]
-    for p in range(16):
-        out_ref[p] = block
+    block_out[...] = block
+    send_block(block, out_ref, index[1])
     own = index[0] * 4 + index[3]
     c = jnp.zeros((2, 256), F32)
     ab = jnp.zeros((16, 128), F32)
@@ -209,8 +235,8 @@
     slip_ref[8:24, :] = ab
 
 
-def last_pack(index, got_ref, out_ref, new):
-    c, a, b = sum_xy(index, got_ref)
+def last_pack(index, got_ref, own_ref, out_ref, new):
+    c, a, b = sum_xy(index, got_ref, own_ref)
     new[0:16, :] = c
     new[16:32, 0:128] = a
     new[16:32, 128:256] = b
@@ -252,20 +278,16 @@
     a_ref[...] = turned[0:12, 0:16]
 
 
-def arrange_target(tensor, core):
-    depth = tensor.shape[2]
-    flat = tensor.reshape(-1, depth)
-    spot = lax.broadcasted_iota(jnp.int32, (depth, depth), 1)
-    half = (spot // 256) ^ core
-    xs, ys = (spot // 64) % 4, (spot // 16) % 4
+def arrange(flats, core):
+    depth = flats[0].shape[1]
+    spot = lax.broadcasted_iota(jnp.int32, (depth, depth // 2), 1)
+    half = jnp.where(core == 0.0, 0, 32)
+    xs, ys = spot // 64, (spot // 16) % 4
     zls, zhs, us = (spot // 8) % 2, (spot // 2) % 4, spot % 2
-    source = zls * 256 + xs * 64 + half * 32 + zhs * 8 + ys * 2 + us
-    pick = (lax.broadcasted_iota(jnp.int32, (depth, depth), 0) == source).astype(F32)
-    kept = jnp.dot(flat, pick[:, :256], precision=HIGH)
-    came = swap(jnp.dot(flat, pick[:, 256:], precision=HIGH))
-    return jnp.concatenate(
-        [jnp.where(core == 0, kept, came), jnp.where(core == 0, came, kept)], axis=0
-    )
+    source = zls * 256 + xs * 64 + half + zhs * 8 + ys * 2 + us
+    here = lax.broadcasted_iota(jnp.int32, (depth, depth // 2), 0)
+    pick = (here == source).astype(F32)
+    return [jnp.dot(flat, pick, precision=HIGH) for flat in flats]
 
 
 def per_device(tensor, first_factor, second_factor, third_factor):
@@ -273,22 +295,27 @@
     n_i, n_j, depth = tensor.shape
     size_i, size_j = n_i * 16, n_j * 16
     rates = tuple(4.0 / float(n) ** 0.5 for n in (size_j * depth, size_i * depth, size_i * size_j))
-    wide = (16, 32, 256)
-    square = (128, 128)
-
+    wide = (16, 24, 256)
+    square, pair = (128, 128), (16, 256)
+
+    flat = tensor.reshape(-1, depth)
+    flat_other = swap(flat)
     (slip,) = call(first_slip, [(24, 128)], [square], index, first_factor, second_factor.T, third_factor)
     (send,) = call(first_pack, [(8, 24, 128)], [], index, slip, swap(slip))
-    got = exchange(send, Z)
-    target = arrange_target(tensor, index[2])
-    block, send = call(block_from_slips, [(32, 256), wide], [], index, got)
-    grads_scratch = [square, (768, 256), (768, 256)]
-
-    (send,) = call(gradients, [wide], grads_scratch, index, exchange(send, XY), target)
-    (send,) = call(middle_pack, [(8, 32, 256)], [], index, exchange(send, XY))
-    grad_c, grad_ab = call(middle_sum, [(16, 256), (16, 256)], [], index, exchange(send, Z))
-    slip, send = call(
+    block, send, core = call(
+        block_from_slips, [(32, 256), wide, (8, 128)], [], index, exchange(send, Z)
+    )
+    targets = arrange((flat, flat_other), core[0, 0])
+    step = functools.partial(
+        call, gradients, [wide, pair], [square, (768, 256), (768, 256), (24, 256)], index
+    )
+
+    send, own = step(exchange(send, XY), block, *targets)
+    send, own = call(middle_pack, [(8, 24, 256), pair], [], index, exchange(send, XY), own)
+    grad_c, grad_ab = call(middle_sum, [pair, pair], [], index, exchange(send, Z), own)
+    slip, block, send = call(
         functools.partial(middle_update, rates),
-        [(24, 128), wide],
+        [(24, 128), (32, 256), wide],
         [(32, 256)],
         index,
         block,
@@ -296,8 +323,8 @@
         grad_ab,
         swap(grad_ab),
     )
-    (send,) = call(gradients, [wide], grads_scratch, index, exchange(send, XY), target)
-    (send,) = call(last_pack, [(8, 24, 128)], [(32, 256)], index, exchange(send, XY))
+    send, own = step(exchange(send, XY), block, *targets)
+    (send,) = call(last_pack, [(8, 24, 128)], [(32, 256)], index, exchange(send, XY), own)
     (grad,) = call(last_sum, [(24, 128)], [], index, exchange(send, Z))
     new_a, new_bt, new_c = call(
         functools.partial(last_update, rates),

time: 120 us -> 113 us (0.942)
  blocking collectives: 73.3 us -> 54.6 us
  starting transfers between devices: 19.6 us -> 26.2 us
  waiting for transfers between devices: 11.2 us -> 15.6 us
    all_to_all x6 -> x5, blocking collectives: 73.3 us -> 54.6 us  [exchange(): got = lax.all_to_all(parts.reshape(-1, shape[2]), axis, 0, 0, tiled=True)]
    all_to_all x1 -> x2, starting transfers between devices: 6.75 us -> 13.2 us  [exchange(): got = lax.all_to_all(parts.reshape(-1, shape[2]), axis, 0, 0, tiled=True)]
    all_to_all x1 -> x2, waiting for transfers between devices: 8.33 us -> 13.2 us  [exchange(): got = lax.all_to_all(parts.reshape(-1, shape[2]), axis, 0, 0, tiled=True)]
  transfers between devices with their start and end apart: 5 -> 6, of which waited for: 4 -> 5; matrix products, arithmetic and copies ran while one was open for 1% -> 2% of each run, Pallas kernels for 2% -> 2%
where the time goes in v4:
time: 113 us; the launch traced here: 112 us
  blocking collectives  54.6 us (48%)
  starting transfers between devices  26.2 us (23%)
  waiting for transfers between devices  15.6 us (14%)
  Pallas kernels  12.2 us (11%)
  between operations  1.44 us (1%)
  local copies, waits for them, and re-layouts  1.21 us (1%)
  matrix products  1.15 us (1%)
    all_to_all x5, blocking collectives, exchange(): got = lax.all_to_all(parts.reshape(-1, shape[2]), axis, 0, 0, tiled=True)  54.6 us
    all_to_all x2, waiting for transfers between devices, exchange(): got = lax.all_to_all(parts.reshape(-1, shape[2]), axis, 0, 0, tiled=True)  13.2 us
    all_to_all x2, starting transfers between devices, exchange(): got = lax.all_to_all(parts.reshape(-1, shape[2]), axis, 0, 0, tiled=True)  13.2 us
    ppermute x4, starting transfers between devices, swap(): return lax.ppermute(value, 'core', [(0, 1), (1, 0)])  13 us
    pallas_call x11, Pallas kernels, call(): pl.pallas_call(body, out_shape=[jax.ShapeDtypeStruct(s, F32) for s in out...  12.2 us
    ppermute x4, waiting for transfers between devices, swap(): return lax.ppermute(value, 'core', [(0, 1), (1, 0)])  2.36 us
  transfers between devices with their start and end apart: 6, of which 5 were waited for; matrix products, arithmetic and copies ran while one was open for 2% of the time, Pallas kernels for 2%

profile of v4, /device:TPU:1, one launch (start us, length us, event | category | flops | bytes accessed | tf_op | source)
XLA Modules:
  0.0 112.3 jit_solution(3974126502582456878)
XLA Ops:
  1.4 0.7 shard_map.67.own_ref
  2.0 3.3 %collective-permute-start = (f32[24,128]{1,0:T(8,128)S(1)}, f32[24,128]{1,0:T(8,128)S(1)}, u32[]{:S(2)}, u32[]{:S(2)}) collective-permute-start(f32[24,128]{1,0:T(8,128)S(1)} %shard_map.67.own_ref), channel_id=1, source_target_pairs={{0,16},{16,0},{1,17},{17,1},{2,18},{18,2},{3,19},{19,3},{4,20},{20... | collective-permute-start | bytes 36872 | tf_op jit(solution)/shard_map/ppermute | solution.py:23
  5.4 0.7 collective-permute-done.other_ref
  6.1 1.2 %shard_map.68 = f32[8,24,128]{2,1,0:T(8,128)} custom-call(s32[5]{0:T(128)S(1)} %stack.23.index, f32[24,128]{1,0:T(8,128)S(1)} %shard_map.67.own_ref, f32[24,128]{1,0:T(8,128)S(1)} %collective-permute-done.other_ref), custom_call_target="tpu_custom_call" | custom-call | tf_op jit(solution)/shard_map/pallas_call | solution.py:28
  7.3 6.4 %all-to-all-start = ((f32[8,24,128]{2,1,0:T(8,128)}), f32[8,24,128]{2,1,0:T(8,128)S(1)}, u32[]{:S(2)}, u32[]{:S(2)}) async-start(f32[8,24,128]{2,1,0:T(8,128)} %shard_map.68), calls=%async_computation | async-start | bytes 196608 | tf_op jit(solution)/shard_map/all_to_all | solution.py:18
  13.8 7.0 %all-to-all-done.got_ref = f32[8,24,128]{2,1,0:T(8,128)S(1)} async-done(((f32[8,24,128]{2,1,0:T(8,128)}), f32[8,24,128]{2,1,0:T(8,128)S(1)}, u32[]{:S(2)}, u32[]{:S(2)}) %all-to-all-start) | async-done | bytes 98336 | tf_op jit(solution)/shard_map/all_to_all | solution.py:18
  20.8 1.4 %shard_map.69 = (f32[32,256]{1,0:T(8,128)S(1)}, f32[16,24,256]{2,1,0:T(8,128)}, f32[8,128]{1,0:T(8,128)S(1)}) custom-call(s32[5]{0:T(128)S(1)} %stack.23.index, f32[8,24,128]{2,1,0:T(8,128)S(1)} %all-to-all-done.got_ref), custom_call_target="tpu_custom_call" | custom-call | tf_op jit(solution)/shard_map/pallas_call | solution.py:28
  22.7 6.8 %all-to-all-start.1 = ((f32[16,24,256]{2,1,0:T(8,128)}), f32[16,24,256]{2,1,0:T(8,128)S(1)}, u32[]{:S(2)}, u32[]{:S(2)}) async-start(f32[16,24,256]{2,1,0:T(8,128)} %get-tuple-element.21), calls=%async_computation.1 | async-start | bytes 786432 | tf_op jit(solution)/shard_map/all_to_all | solution.py:18
  30.1 0.6 convolution_bitcast_fusion.1.kept_ref
  31.3 6.2 %all-to-all-done.1.got_ref = f32[16,24,256]{2,1,0:T(8,128)S(1)} async-done(((f32[16,24,256]{2,1,0:T(8,128)}), f32[16,24,256]{2,1,0:T(8,128)S(1)}, u32[]{:S(2)}, u32[]{:S(2)}) %all-to-all-start.1) | async-done | bytes 393248 | tf_op jit(solution)/shard_map/all_to_all | solution.py:18
  37.5 2.4 %shard_map.70 = (f32[16,24,256]{2,1,0:T(8,128)S(1)}, f32[16,256]{1,0:T(8,128)S(1)}) custom-call(s32[5]{0:T(128)S(1)} %stack.23.index, f32[16,24,256]{2,1,0:T(8,128)S(1)} %all-to-all-done.1.got_ref, f32[32,256]{1,0:T(8,128)S(1)} %get-tuple-element.20.block_ref, f32[384,256]{1,0:T(8,128)S(1)} %convolution_bitcast_fusion.1.kept_ref, ...), custom_call_target="tpu_custom_call" | custom-call | tf_op jit(solution)/shard_map/pallas_call | solution.py:28
  39.9 11.4 %all_to_all.42.got_ref = f32[16,24,256]{2,1,0:T(8,128)S(1)} all-to-all(f32[16,24,256]{2,1,0:T(8,128)S(1)} %get-tuple-element.23), channel_id=1, replica_groups=mesh['zl'=2,'x'=4,'core'=2,'zh'=4,'y'=4] {'x','y'}, dimensions={0} | all-to-all | bytes 786432 | tf_op jit(solution)/shard_map/all_to_all | solution.py:18
  51.8 9.7 %all_to_all.43.got_ref = f32[8,24,256]{2,1,0:T(8,128)S(1)} all-to-all(f32[8,24,256]{2,1,0:T(8,128)S(1)} %get-tuple-element.25), channel_id=1, replica_groups=mesh['zl'=2,'x'=4,'core'=2,'zh'=4,'y'=4] {'zl','zh'}, dimensions={0} | all-to-all | bytes 393216 | tf_op jit(solution)/shard_map/all_to_all | solution.py:18
  62.1 5.3 %collective-permute-start.2 = (f32[16,256]{1,0:T(8,128)S(1)}, f32[16,256]{1,0:T(8,128)S(1)}, u32[]{:S(2)}, u32[]{:S(2)}) collective-permute-start(f32[16,256]{1,0:T(8,128)S(1)} %get-tuple-element.28.ab_ref), channel_id=1, source_target_pairs={{0,16},{16,0},{1,17},{17,1},{2,18},{18,2},{3,19},{19,3},{4,20},{20... | collective-permute-start | bytes 49160 | tf_op jit(solution)/shard_map/ppermute | solution.py:23
  67.4 0.8 collective-permute-done.2.other_ref
  68.2 0.6 shard_map.73
  68.8 12.5 %all_to_all.44.got_ref = f32[16,24,256]{2,1,0:T(8,128)S(1)} all-to-all(f32[16,24,256]{2,1,0:T(8,128)S(1)} %get-tuple-element.30), channel_id=1, replica_groups=mesh['zl'=2,'x'=4,'core'=2,'zh'=4,'y'=4] {'x','y'}, dimensions={0} | all-to-all | bytes 786432 | tf_op jit(solution)/shard_map/all_to_all | solution.py:18
  81.3 2.4 %shard_map.74 = (f32[16,24,256]{2,1,0:T(8,128)S(1)}, f32[16,256]{1,0:T(8,128)S(1)}) custom-call(s32[5]{0:T(128)S(1)} %stack.23.index, f32[16,24,256]{2,1,0:T(8,128)S(1)} %all_to_all.44.got_ref, f32[32,256]{1,0:T(8,128)S(1)} %get-tuple-element.31.block_ref, f32[384,256]{1,0:T(8,128)S(1)} %convolution_bitcast_fusion.1.kept_ref, ...), custom_call_target="tpu_custom_call" | custom-call | tf_op jit(solution)/shard_map/pallas_call | solution.py:28
  83.7 11.3 %all_to_all.45.got_ref = f32[16,24,256]{2,1,0:T(8,128)S(1)} all-to-all(f32[16,24,256]{2,1,0:T(8,128)S(1)} %get-tuple-element.32), channel_id=1, replica_groups=mesh['zl'=2,'x'=4,'core'=2,'zh'=4,'y'=4] {'x','y'}, dimensions={0} | all-to-all | bytes 786432 | tf_op jit(solution)/shard_map/all_to_all | solution.py:18
  95.0 0.6 shard_map.75
  95.6 9.7 %all_to_all.46.got_ref = f32[8,24,128]{2,1,0:T(8,128)S(1)} all-to-all(f32[8,24,128]{2,1,0:T(8,128)S(1)} %shard_map.75), channel_id=1, replica_groups=mesh['zl'=2,'x'=4,'core'=2,'zh'=4,'y'=4] {'zl','zh'}, dimensions={0} | all-to-all | bytes 196608 | tf_op jit(solution)/shard_map/all_to_all | solution.py:18
  105.9 4.3 %collective-permute-start.3 = (f32[24,128]{1,0:T(8,128)S(1)}, f32[24,128]{1,0:T(8,128)S(1)}, u32[]{:S(2)}, u32[]{:S(2)}) collective-permute-start(f32[24,128]{1,0:T(8,128)S(1)} %shard_map.76.grad_ref), channel_id=1, source_target_pairs={{0,16},{16,0},{1,17},{17,1},{2,18},{18,2},{3,19},{19,3},{4,20},{20... | collective-permute-start | bytes 36872 | tf_op jit(solution)/shard_map/ppermute | solution.py:23
  110.2 0.8 collective-permute-done.3.other_ref
  111.1 1.3 %shard_map.77 = (f32[12,16]{1,0:T(8,128)}, f32[16,32]{1,0:T(8,128)}, f32[2,256]{1,0:T(2,128)}) custom-call(s32[5]{0:T(128)S(1)} %stack.23.index, f32[24,128]{1,0:T(8,128)S(1)} %get-tuple-element.29.old_ref, f32[24,128]{1,0:T(8,128)S(1)} %shard_map.76.grad_ref, f32[24,128]{1,0:T(8,128)S(1)} %collective-permute-done.3.other_ref), custom_call_target="tpu_custom_call" | custom-call | tf_op jit(solution)/shard_map/pallas_call | solution.py:28
  (24 shorter events, 3.6 us)
Async XLA Ops:
  0.6 0.7 copy-start.2
  0.6 0.7 copy-start
  0.7 0.7 copy-start.1
  0.7 29.4 %copy-start.3 = (f32[12,32,512]{2,1,0:T(8,128)S(1)}, f32[12,32,512]{2,1,0:T(8,128)}, u32[]{:S(2)}) copy-start(f32[12,32,512]{2,1,0:T(8,128)} %param.4) | copy-start | bytes 2359300
  2.0 4.1 %collective-permute-start = (f32[24,128]{1,0:T(8,128)S(1)}, f32[24,128]{1,0:T(8,128)S(1)}, u32[]{:S(2)}, u32[]{:S(2)}) collective-permute-start(f32[24,128]{1,0:T(8,128)S(1)} %shard_map.67.own_ref), channel_id=1, source_target_pairs={{0,16},{16,0},{1,17},{17,1},{2,18},{18,2},{3,19},{19,3},{4,20},{20... | collective-permute-start | bytes 36872 | tf_op jit(solution)/shard_map/ppermute | solution.py:23
  5.3 25.4 %collective-permute-start.1 = (f32[384,512]{1,0:T(8,128)}, f32[384,512]{1,0:T(8,128)S(1)}, u32[]{:S(2)}, u32[]{:S(2)}) collective-permute-start(f32[384,512]{1,0:T(8,128)} %bitcast.16), channel_id=1, source_target_pairs={{0,16},{16,0},{1,17},{17,1},{2,18},{18,2},{3,19},{19,3},{4,20},{20... | collective-permute-start | bytes 2359304 | tf_op jit(solution)/shard_map/ppermute | solution.py:23
  7.3 13.5 %all-to-all-start = ((f32[8,24,128]{2,1,0:T(8,128)}), f32[8,24,128]{2,1,0:T(8,128)S(1)}, u32[]{:S(2)}, u32[]{:S(2)}) async-start(f32[8,24,128]{2,1,0:T(8,128)} %shard_map.68), calls=%async_computation | async-start | bytes 196608 | tf_op jit(solution)/shard_map/all_to_all | solution.py:18
  22.7 14.8 %all-to-all-start.1 = ((f32[16,24,256]{2,1,0:T(8,128)}), f32[16,24,256]{2,1,0:T(8,128)S(1)}, u32[]{:S(2)}, u32[]{:S(2)}) async-start(f32[16,24,256]{2,1,0:T(8,128)} %get-tuple-element.21), calls=%async_computation.1 | async-start | bytes 786432 | tf_op jit(solution)/shard_map/all_to_all | solution.py:18
  62.1 6.1 %collective-permute-start.2 = (f32[16,256]{1,0:T(8,128)S(1)}, f32[16,256]{1,0:T(8,128)S(1)}, u32[]{:S(2)}, u32[]{:S(2)}) collective-permute-start(f32[16,256]{1,0:T(8,128)S(1)} %get-tuple-element.28.ab_ref), channel_id=1, source_target_pairs={{0,16},{16,0},{1,17},{17,1},{2,18},{18,2},{3,19},{19,3},{4,20},{20... | collective-permute-start | bytes 49160 | tf_op jit(solution)/shard_map/ppermute | solution.py:23
  105.9 5.2 %collective-permute-start.3 = (f32[24,128]{1,0:T(8,128)S(1)}, f32[24,128]{1,0:T(8,128)S(1)}, u32[]{:S(2)}, u32[]{:S(2)}) collective-permute-start(f32[24,128]{1,0:T(8,128)S(1)} %shard_map.76.grad_ref), channel_id=1, source_target_pairs={{0,16},{16,0},{1,17},{17,1},{2,18},{18,2},{3,19},{19,3},{4,20},{20... | collective-permute-start | bytes 36872 | tf_op jit(solution)/shard_map/ppermute | solution.py:23

commit v5 on v4

--- a/solution.py
+++ b/solution.py
@@ -82,19 +82,22 @@
     return c, ab
 
 
+def placed(a, bt, core, pad):
+    pad[...] = jnp.zeros((128, 128), F32)
+    pad[0:12, 0:16] = a
+    at = pad[...].T[0:16, :]
+    pad[32:48, 0:32] = bt
+    b = pad[32:48, :]
+    even = core == 0
+    at = jnp.where(even, at, pltpu.roll(at, 16, 1))
+    return at + jnp.where(even, pltpu.roll(b, 32, 1), pltpu.roll(b, 96, 1))
+
+
 def first_slip(index, a_ref, bt_ref, c_ref, out_ref, pad):
-    core = index[2]
-    pad[...] = jnp.zeros((128, 128), F32)
-    pad[0:12, 0:16] = a_ref[...]
-    at = pad[...].T[0:16, :]
-    pad[32:48, 0:32] = bt_ref[...]
-    b = pad[32:48, :]
-    a = jnp.where(core == 0, at, pltpu.roll(at, 12, 1))
-    b = jnp.where(core == 0, pltpu.roll(b, 32, 1), pltpu.roll(b, 96, 1))
     out_ref[0:8, :] = jnp.zeros((8, 128), F32)
     out_ref[0:2, :] = c_ref[:, 0:128]
     out_ref[2:4, :] = c_ref[:, 128:256]
-    out_ref[8:24, :] = a + b
+    out_ref[8:24, :] = placed(a_ref[...], bt_ref[...], index[2], pad)
 
 
 def first_pack(index, own_ref, other_ref, out_ref):
@@ -105,9 +108,8 @@
         out_ref[p, 8:24, :] = ab
 
 
-def block_from_slips(index, got_ref, block_ref, out_ref, core_ref):
+def block_from_slips(index, got_ref, block_ref, out_ref):
     zl, zh = index[0], index[3]
-    core_ref[...] = jnp.full((8, 128), index[2], jnp.int32).astype(F32)
     for p in range(8):
         block_ref[2 * p : 2 * p + 2, 0:128] = got_ref[p, 0:2, :]
         block_ref[2 * p : 2 * p + 2, 128:256] = got_ref[p, 2:4, :]
@@ -128,14 +130,14 @@
     index, got_ref, block_ref, kept_ref, came_ref, out_ref, own_ref, turn, khatri, terms, first
 ):
     x, core, y = index[1], index[2], index[4]
-    order = [i + 12 * core if i < 12 else i - 12 * core for i in range(24)]
+    order = [i + 16 * core if i < 12 else i + 4 - 16 * core for i in range(24)]
     for q in range(4):
         v = jnp.where(y == q, block_ref[16:32, 0:128], slot(got_ref, x * 4 + q))
         turn[16 * q : 16 * q + 16, :] = v
         turn[64 + 16 * q : 80 + 16 * q, :] = pltpu.roll(v, 96, 1)
     turned = turn[...].T
-    first[:, 0:128] = turned[0:24]
-    first[:, 128:256] = turned[64:88]
+    first[:, 0:128] = turned[0:32]
+    first[:, 128:256] = turned[64:96]
     a = [first[pl.ds(i, 1), :] for i in order]
     for q in range(4):
         v = jnp.where(x == q, block_ref[16:32, 128:256], slot(got_ref, q * 4 + y))
@@ -273,21 +275,27 @@
     b = jnp.where(core == 0, pltpu.roll(ab, 96, 1), pltpu.roll(ab, 32, 1))
     bt_ref[...] = b[:, 0:32]
     pad[...] = jnp.zeros((128, 128), F32)
-    pad[0:16, :] = jnp.where(core == 0, ab, pltpu.roll(ab, 116, 1))
+    pad[0:16, :] = jnp.where(core == 0, ab, pltpu.roll(ab, 112, 1))
     turned = pad[...].T
     a_ref[...] = turned[0:12, 0:16]
 
 
-def arrange(flats, core):
-    depth = flats[0].shape[1]
-    spot = lax.broadcasted_iota(jnp.int32, (depth, depth // 2), 1)
-    half = jnp.where(core == 0.0, 0, 32)
+def arrange(index, after_ref, own_ref, other_ref, kept_ref, came_ref):
+    del after_ref
+    spot = lax.broadcasted_iota(jnp.int32, (512, 256), 1)
     xs, ys = spot // 64, (spot // 16) % 4
     zls, zhs, us = (spot // 8) % 2, (spot // 2) % 4, spot % 2
-    source = zls * 256 + xs * 64 + half + zhs * 8 + ys * 2 + us
-    here = lax.broadcasted_iota(jnp.int32, (depth, depth // 2), 0)
-    pick = (here == source).astype(F32)
-    return [jnp.dot(flat, pick, precision=HIGH) for flat in flats]
+    source = zls * 256 + xs * 64 + index[2] * 32 + zhs * 8 + ys * 2 + us
+    here = lax.broadcasted_iota(jnp.int32, (512, 256), 0)
+    pick = jnp.where(here == source, 1.0, 0.0).astype(jnp.bfloat16)
+    for from_ref, to_ref in ((own_ref, kept_ref), (other_ref, came_ref)):
+        rest = from_ref[...]
+        total = jnp.zeros((384, 256), F32)
+        for _ in range(3):
+            part = rest.astype(jnp.bfloat16)
+            rest = rest - part.astype(F32)
+            total = total + jnp.dot(part, pick, preferred_element_type=F32)
+        to_ref[...] = total
 
 
 def per_device(tensor, first_factor, second_factor, third_factor):
@@ -299,15 +307,14 @@
     square, pair = (128, 128), (16, 256)
 
     flat = tensor.reshape(-1, depth)
+    b_t = second_factor.T
     flat_other = swap(flat)
-    (slip,) = call(first_slip, [(24, 128)], [square], index, first_factor, second_factor.T, third_factor)
+    (slip,) = call(first_slip, [(24, 128)], [square], index, first_factor, b_t, third_factor)
     (send,) = call(first_pack, [(8, 24, 128)], [], index, slip, swap(slip))
-    block, send, core = call(
-        block_from_slips, [(32, 256), wide, (8, 128)], [], index, exchange(send, Z)
-    )
-    targets = arrange((flat, flat_other), core[0, 0])
+    block, send = call(block_from_slips, [(32, 256), wide], [], index, exchange(send, Z))
+    targets = call(arrange, [(384, 256), (384, 256)], [], index, block, flat, flat_other)
     step = functools.partial(
-        call, gradients, [wide, pair], [square, (768, 256), (768, 256), (24, 256)], index
+        call, gradients, [wide, pair], [square, (768, 256), (768, 256), (32, 256)], index
     )
 
     send, own = step(exchange(send, XY), block, *targets)

time: 113 us -> 114 us (level)
  blocking collectives: 54.6 us -> 68.5 us
  starting transfers between devices: 26.2 us -> 19.4 us
  waiting for transfers between devices: 15.6 us -> 9.55 us
  matrix products: 1.15 us -> 0 us
    all_to_all x5 -> x6, blocking collectives: 54.6 us -> 68.5 us  [exchange(): got = lax.all_to_all(parts.reshape(-1, shape[2]), axis, 0, 0, tiled=True)]
    all_to_all x2 -> x1, waiting for transfers between devices: 13.2 us -> 6.75 us  [exchange(): got = lax.all_to_all(parts.reshape(-1, shape[2]), axis, 0, 0, tiled=True)]
    all_to_all x2 -> x1, starting transfers between devices: 13.2 us -> 6.75 us  [exchange(): got = lax.all_to_all(parts.reshape(-1, shape[2]), axis, 0, 0, tiled=True)]
    unnamed x8, local copies, waits for them, and re-layouts: 0.61 us -> 2.08 us
    dot_general x2 -> x0, matrix products: 1.15 us -> none  [arrange(): return [jnp.dot(flat, pick, precision=HIGH) for flat in flats]]
    pallas_call x11 -> x12, Pallas kernels: 12.2 us -> 12.9 us  [call(): pl.pallas_call(body, out_shape=[jax.ShapeDtypeStruct(s, F32) for s in out...]
  transfers between devices with their start and end apart: 6 -> 5, of which waited for: 5 -> 4; matrix products, arithmetic and copies ran while one was open for 2% -> 0% of each run, Pallas kernels for 2% -> 3%
where the time goes in v5:
time: 114 us; the launch traced here: 113 us
  blocking collectives  68.5 us (60%)
  starting transfers between devices  19.4 us (17%)
  Pallas kernels  12.9 us (11%)
  waiting for transfers between devices  9.55 us (8%)
  local copies, waits for them, and re-layouts  2.16 us (2%)
    all_to_all x6, blocking collectives, exchange(): got = lax.all_to_all(parts.reshape(-1, shape[2]), axis, 0, 0, tiled=True)  68.5 us
    pallas_call x12, Pallas kernels, call(): pl.pallas_call(body, out_shape=[jax.ShapeDtypeStruct(s, F32) for s in out...  12.9 us
    ppermute x4, starting transfers between devices, swap(): return lax.ppermute(value, 'core', [(0, 1), (1, 0)])  12.7 us
    all_to_all x1, starting transfers between devices, exchange(): got = lax.all_to_all(parts.reshape(-1, shape[2]), axis, 0, 0, tiled=True)  6.75 us
    all_to_all x1, waiting for transfers between devices, exchange(): got = lax.all_to_all(parts.reshape(-1, shape[2]), axis, 0, 0, tiled=True)  6.75 us
    ppermute x4, waiting for transfers between devices, swap(): return lax.ppermute(value, 'core', [(0, 1), (1, 0)])  2.8 us
  transfers between devices with their start and end apart: 5, of which 4 were waited for; matrix products, arithmetic and copies ran while one was open for 0% of the time, Pallas kernels for 3%

profile of v5, /device:TPU:1, one launch (start us, length us, event | category | flops | bytes accessed | tf_op | source)
XLA Modules:
  0.0 113.3 jit_solution(5486063796947484733)
XLA Ops:
  0.6 3.3 %collective-permute-start.1 = (f32[384,512]{1,0:T(8,128)}, f32[384,512]{1,0:T(8,128)S(1)}, u32[]{:S(2)}, u32[]{:S(2)}) collective-permute-start(f32[384,512]{1,0:T(8,128)} %bitcast.8), channel_id=1, source_target_pairs={{0,16},{16,0},{1,17},{17,1},{2,18},{18,2},{3,19},{19,3},{4,20},{20... | collective-permute-start | bytes 2359304 | tf_op jit(solution)/shard_map/ppermute | solution.py:23
  4.1 0.7 copy-done.1
  4.8 0.7 copy-done.2
  5.4 0.7 copy-done.3
  6.1 0.7 shard_map.67.own_ref
  6.9 1.1 collective-permute-done.other_ref
  8.6 13.2 %all_to_all.42.got_ref = f32[8,24,128]{2,1,0:T(8,128)S(1)} all-to-all(f32[8,24,128]{2,1,0:T(8,128)S(1)} %shard_map.68), channel_id=1, replica_groups=mesh['zl'=2,'x'=4,'core'=2,'zh'=4,'y'=4] {'zl','zh'}, dimensions={0} | all-to-all | bytes 196608 | tf_op jit(solution)/shard_map/all_to_all | solution.py:18
  21.7 1.4 %shard_map.69 = (f32[32,256]{1,0:T(8,128)S(1)}, f32[16,24,256]{2,1,0:T(8,128)}) custom-call(s32[5]{0:T(128)S(1)} %stack.23.index, f32[8,24,128]{2,1,0:T(8,128)S(1)} %all_to_all.42.got_ref), custom_call_target="tpu_custom_call" | custom-call | tf_op jit(solution)/shard_map/pallas_call | solution.py:28
  23.1 6.8 %all-to-all-start.1 = ((f32[16,24,256]{2,1,0:T(8,128)}), f32[16,24,256]{2,1,0:T(8,128)S(1)}, u32[]{:S(2)}, u32[]{:S(2)}) async-start(f32[16,24,256]{2,1,0:T(8,128)} %get-tuple-element.22), calls=%async_computation.1 | async-start | bytes 786432 | tf_op jit(solution)/shard_map/all_to_all | solution.py:18
  29.9 1.3 %shard_map.70 = (f32[384,256]{1,0:T(8,128)S(1)}, f32[384,256]{1,0:T(8,128)S(1)}) custom-call(s32[5]{0:T(128)S(1)} %stack.23.index, f32[32,256]{1,0:T(8,128)S(1)} %get-tuple-element.21.after_ref.block_ref, f32[384,512]{1,0:T(8,128)S(1)} %bitcast.9, f32[384,512]{1,0:T(8,128)S(1)} %collective-permute-done.1.other_ref), custom_call_target="tpu_custom_call" | custom-call | tf_op jit(solution)/shard_map/pallas_call | solution.py:28
  31.2 6.8 %all-to-all-done.1.got_ref = f32[16,24,256]{2,1,0:T(8,128)S(1)} async-done(((f32[16,24,256]{2,1,0:T(8,128)}), f32[16,24,256]{2,1,0:T(8,128)S(1)}, u32[]{:S(2)}, u32[]{:S(2)}) %all-to-all-start.1) | async-done | bytes 393248 | tf_op jit(solution)/shard_map/all_to_all | solution.py:18
  38.0 2.4 %shard_map.71 = (f32[16,24,256]{2,1,0:T(8,128)S(1)}, f32[16,256]{1,0:T(8,128)S(1)}) custom-call(s32[5]{0:T(128)S(1)} %stack.23.index, f32[16,24,256]{2,1,0:T(8,128)S(1)} %all-to-all-done.1.got_ref, f32[32,256]{1,0:T(8,128)S(1)} %get-tuple-element.21.after_ref.block_ref, f32[384,256]{1,0:T(8,128)S(1)} %get-tuple-element.23.kept_ref, ...), custom_call_target="tpu_custom_call" | custom-call | tf_op jit(solution)/shard_map/pallas_call | solution.py:28
  40.4 11.4 %all_to_all.43.got_ref = f32[16,24,256]{2,1,0:T(8,128)S(1)} all-to-all(f32[16,24,256]{2,1,0:T(8,128)S(1)} %get-tuple-element.25), channel_id=1, replica_groups=mesh['zl'=2,'x'=4,'core'=2,'zh'=4,'y'=4] {'x','y'}, dimensions={0} | all-to-all | bytes 786432 | tf_op jit(solution)/shard_map/all_to_all | solution.py:18
  52.3 10.7 %all_to_all.44.got_ref = f32[8,24,256]{2,1,0:T(8,128)S(1)} all-to-all(f32[8,24,256]{2,1,0:T(8,128)S(1)} %get-tuple-element.27), channel_id=1, replica_groups=mesh['zl'=2,'x'=4,'core'=2,'zh'=4,'y'=4] {'zl','zh'}, dimensions={0} | all-to-all | bytes 393216 | tf_op jit(solution)/shard_map/all_to_all | solution.py:18
  63.5 4.9 %collective-permute-start.2 = (f32[16,256]{1,0:T(8,128)S(1)}, f32[16,256]{1,0:T(8,128)S(1)}, u32[]{:S(2)}, u32[]{:S(2)}) collective-permute-start(f32[16,256]{1,0:T(8,128)S(1)} %get-tuple-element.30.ab_ref), channel_id=1, source_target_pairs={{0,16},{16,0},{1,17},{17,1},{2,18},{18,2},{3,19},{19,3},{4,20},{20... | collective-permute-start | bytes 49160 | tf_op jit(solution)/shard_map/ppermute | solution.py:23
  68.5 0.8 collective-permute-done.2.other_ref
  69.9 12.4 %all_to_all.45.got_ref = f32[16,24,256]{2,1,0:T(8,128)S(1)} all-to-all(f32[16,24,256]{2,1,0:T(8,128)S(1)} %get-tuple-element.32), channel_id=1, replica_groups=mesh['zl'=2,'x'=4,'core'=2,'zh'=4,'y'=4] {'x','y'}, dimensions={0} | all-to-all | bytes 786432 | tf_op jit(solution)/shard_map/all_to_all | solution.py:18
  82.4 2.4 %shard_map.75 = (f32[16,24,256]{2,1,0:T(8,128)S(1)}, f32[16,256]{1,0:T(8,128)S(1)}) custom-call(s32[5]{0:T(128)S(1)} %stack.23.index, f32[16,24,256]{2,1,0:T(8,128)S(1)} %all_to_all.45.got_ref, f32[32,256]{1,0:T(8,128)S(1)} %get-tuple-element.33.block_ref, f32[384,256]{1,0:T(8,128)S(1)} %get-tuple-element.23.kept_ref, f32[384,256]{1,0:T(8,128)S(1)} %get-tuple-element.24.came_ref), custom_call_target="tpu_custom_call" | custom-call | tf_op jit(solution)/shard_map/pallas_call | solution.py:28
  84.7 11.3 %all_to_all.46.got_ref = f32[16,24,256]{2,1,0:T(8,128)S(1)} all-to-all(f32[16,24,256]{2,1,0:T(8,128)S(1)} %get-tuple-element.34), channel_id=1, replica_groups=mesh['zl'=2,'x'=4,'core'=2,'zh'=4,'y'=4] {'x','y'}, dimensions={0} | all-to-all | bytes 786432 | tf_op jit(solution)/shard_map/all_to_all | solution.py:18
  96.0 0.6 shard_map.76
  96.6 9.6 %all_to_all.47.got_ref = f32[8,24,128]{2,1,0:T(8,128)S(1)} all-to-all(f32[8,24,128]{2,1,0:T(8,128)S(1)} %shard_map.76), channel_id=1, replica_groups=mesh['zl'=2,'x'=4,'core'=2,'zh'=4,'y'=4] {'zl','zh'}, dimensions={0} | all-to-all | bytes 196608 | tf_op jit(solution)/shard_map/all_to_all | solution.py:18
  106.8 4.3 %collective-permute-start.3 = (f32[24,128]{1,0:T(8,128)S(1)}, f32[24,128]{1,0:T(8,128)S(1)}, u32[]{:S(2)}, u32[]{:S(2)}) collective-permute-start(f32[24,128]{1,0:T(8,128)S(1)} %shard_map.77.grad_ref), channel_id=1, source_target_pairs={{0,16},{16,0},{1,17},{17,1},{2,18},{18,2},{3,19},{19,3},{4,20},{20... | collective-permute-start | bytes 36872 | tf_op jit(solution)/shard_map/ppermute | solution.py:23
  111.2 0.8 collective-permute-done.3.other_ref
  112.0 1.3 %shard_map.78 = (f32[12,16]{1,0:T(8,128)}, f32[16,32]{1,0:T(8,128)}, f32[2,256]{1,0:T(2,128)}) custom-call(s32[5]{0:T(128)S(1)} %stack.23.index, f32[24,128]{1,0:T(8,128)S(1)} %get-tuple-element.31.old_ref, f32[24,128]{1,0:T(8,128)S(1)} %shard_map.77.grad_ref, f32[24,128]{1,0:T(8,128)S(1)} %collective-permute-done.3.other_ref), custom_call_target="tpu_custom_call" | custom-call | tf_op jit(solution)/shard_map/pallas_call | solution.py:28
  (13 shorter events, 3.0 us)
Async XLA Ops:
  0.6 29.3 %copy-start = (f32[12,32,512]{2,1,0:T(8,128)S(1)}, f32[12,32,512]{2,1,0:T(8,128)}, u32[]{:S(2)}) copy-start(f32[12,32,512]{2,1,0:T(8,128)} %param.4) | copy-start | bytes 2359300
  0.6 29.2 %collective-permute-start.1 = (f32[384,512]{1,0:T(8,128)}, f32[384,512]{1,0:T(8,128)S(1)}, u32[]{:S(2)}, u32[]{:S(2)}) collective-permute-start(f32[384,512]{1,0:T(8,128)} %bitcast.8), channel_id=1, source_target_pairs={{0,16},{16,0},{1,17},{17,1},{2,18},{18,2},{3,19},{19,3},{4,20},{20... | collective-permute-start | bytes 2359304 | tf_op jit(solution)/shard_map/ppermute | solution.py:23
  4.1 0.7 copy-start.1
  4.7 0.7 copy-start.2
  5.4 0.7 copy-start.3
  6.8 1.2 %collective-permute-start = (f32[24,128]{1,0:T(8,128)S(1)}, f32[24,128]{1,0:T(8,128)S(1)}, u32[]{:S(2)}, u32[]{:S(2)}) collective-permute-start(f32[24,128]{1,0:T(8,128)S(1)} %shard_map.67.own_ref), channel_id=1, source_target_pairs={{0,16},{16,0},{1,17},{17,1},{2,18},{18,2},{3,19},{19,3},{4,20},{20... | collective-permute-start | bytes 36872 | tf_op jit(solution)/shard_map/ppermute | solution.py:23
  23.1 14.9 %all-to-all-start.1 = ((f32[16,24,256]{2,1,0:T(8,128)}), f32[16,24,256]{2,1,0:T(8,128)S(1)}, u32[]{:S(2)}, u32[]{:S(2)}) async-start(f32[16,24,256]{2,1,0:T(8,128)} %get-tuple-element.22), calls=%async_computation.1 | async-start | bytes 786432 | tf_op jit(solution)/shard_map/all_to_all | solution.py:18
  63.5 5.8 %collective-permute-start.2 = (f32[16,256]{1,0:T(8,128)S(1)}, f32[16,256]{1,0:T(8,128)S(1)}, u32[]{:S(2)}, u32[]{:S(2)}) collective-permute-start(f32[16,256]{1,0:T(8,128)S(1)} %get-tuple-element.30.ab_ref), channel_id=1, source_target_pairs={{0,16},{16,0},{1,17},{17,1},{2,18},{18,2},{3,19},{19,3},{4,20},{20... | collective-permute-start | bytes 49160 | tf_op jit(solution)/shard_map/ppermute | solution.py:23
  106.8 5.2 %collective-permute-start.3 = (f32[24,128]{1,0:T(8,128)S(1)}, f32[24,128]{1,0:T(8,128)S(1)}, u32[]{:S(2)}, u32[]{:S(2)}) collective-permute-start(f32[24,128]{1,0:T(8,128)S(1)} %shard_map.77.grad_ref), channel_id=1, source_target_pairs={{0,16},{16,0},{1,17},{17,1},{2,18},{18,2},{3,19},{19,3},{4,20},{20... | collective-permute-start | bytes 36872 | tf_op jit(solution)/shard_map/ppermute | solution.py:23

commit v6 on v5

--- a/solution.py
+++ b/solution.py
@@ -82,29 +82,18 @@
     return c, ab
 
 
-def placed(a, bt, core, pad):
+def first_pack(index, own_ref, other_ref, out_ref, pad):
+    even = index[2] == 0
+    own, other = own_ref[0:32, 0:128], other_ref[0:32, 0:128]
+    low, high = jnp.where(even, own, other), jnp.where(even, other, own)
     pad[...] = jnp.zeros((128, 128), F32)
-    pad[0:12, 0:16] = a
-    at = pad[...].T[0:16, :]
-    pad[32:48, 0:32] = bt
-    b = pad[32:48, :]
-    even = core == 0
-    at = jnp.where(even, at, pltpu.roll(at, 16, 1))
-    return at + jnp.where(even, pltpu.roll(b, 32, 1), pltpu.roll(b, 96, 1))
-
-
-def first_slip(index, a_ref, bt_ref, c_ref, out_ref, pad):
-    out_ref[0:8, :] = jnp.zeros((8, 128), F32)
-    out_ref[0:2, :] = c_ref[:, 0:128]
-    out_ref[2:4, :] = c_ref[:, 128:256]
-    out_ref[8:24, :] = placed(a_ref[...], bt_ref[...], index[2], pad)
-
-
-def first_pack(index, own_ref, other_ref, out_ref):
-    ab = own_ref[8:24, :] + other_ref[8:24, :]
-    c = own_ref[0:8, :]
-    for p in range(8):
-        out_ref[p, 0:8, :] = c
+    pad[0:16, :] = low[0:16]
+    pad[16:32, :] = high[0:16]
+    ab = pad[...].T[0:16, :] + pltpu.roll(low[16:32], 32, 1) + pltpu.roll(high[16:32], 96, 1)
+    for p in range(8):
+        out_ref[p, 0:8, :] = jnp.zeros((8, 128), F32)
+        out_ref[p, 0:2, :] = own_ref[32:34, 0:128]
+        out_ref[p, 2:4, :] = own_ref[32:34, 128:256]
         out_ref[p, 8:24, :] = ab
 
 
@@ -307,10 +296,14 @@
     square, pair = (128, 128), (16, 256)
 
     flat = tensor.reshape(-1, depth)
-    b_t = second_factor.T
+    arguments = (first_factor, 16), (second_factor.T, 16), (third_factor, 8)
+    shards = jnp.concatenate(
+        [jnp.pad(v, ((0, n - v.shape[0]), (0, 256 - v.shape[1]))) for v, n in arguments]
+    )
+    shards_other = swap(shards)
+    flat, shards_other = lax.optimization_barrier((flat, shards_other))
     flat_other = swap(flat)
-    (slip,) = call(first_slip, [(24, 128)], [square], index, first_factor, b_t, third_factor)
-    (send,) = call(first_pack, [(8, 24, 128)], [], index, slip, swap(slip))
+    (send,) = call(first_pack, [(8, 24, 128)], [square], index, shards, shards_other)
     block, send = call(block_from_slips, [(32, 256), wide], [], index, exchange(send, Z))
     targets = call(arrange, [(384, 256), (384, 256)], [], index, block, flat, flat_other)
     step = functools.partial(

time: 114 us -> 112 us (0.982)
  local copies, waits for them, and re-layouts: 2.16 us -> 0.09 us
    unnamed x8 -> x2, local copies, waits for them, and re-layouts: 2.08 us -> 0.01 us
    pallas_call x12 -> x11, Pallas kernels: 12.9 us -> 12.3 us  [call(): pl.pallas_call(body, out_shape=[jax.ShapeDtypeStruct(s, F32) for s in out...]
where the time goes in v6:
time: 112 us; the launch traced here: 111 us
  blocking collectives  68.7 us (61%)
  starting transfers between devices  19.5 us (17%)
  Pallas kernels  12.3 us (11%)
  waiting for transfers between devices  9.29 us (8%)
    all_to_all x6, blocking collectives, exchange(): got = lax.all_to_all(parts.reshape(-1, shape[2]), axis, 0, 0, tiled=True)  68.7 us
    ppermute x4, starting transfers between devices, swap(): return lax.ppermute(value, 'core', [(0, 1), (1, 0)])  12.8 us
    pallas_call x11, Pallas kernels, call(): pl.pallas_call(body, out_shape=[jax.ShapeDtypeStruct(s, F32) for s in out...  12.3 us
    all_to_all x1, starting transfers between devices, exchange(): got = lax.all_to_all(parts.reshape(-1, shape[2]), axis, 0, 0, tiled=True)  6.75 us
    all_to_all x1, waiting for transfers between devices, exchange(): got = lax.all_to_all(parts.reshape(-1, shape[2]), axis, 0, 0, tiled=True)  6.74 us
    ppermute x4, waiting for transfers between devices, swap(): return lax.ppermute(value, 'core', [(0, 1), (1, 0)])  2.55 us
  transfers between devices with their start and end apart: 5, of which 4 were waited for; matrix products, arithmetic and copies ran while one was open for 0% of the time, Pallas kernels for 3%

profile of v6, /device:TPU:1, one launch (start us, length us, event | category | flops | bytes accessed | tf_op | source)
XLA Modules:
  0.0 111.4 jit_solution(782621589614903627)
XLA Ops:
  0.6 0.8 select_maximum_fusion.own_ref
  1.5 3.2 %collective-permute-start = (f32[40,256]{1,0:T(8,128)S(1)}, f32[40,256]{1,0:T(8,128)S(1)}, u32[]{:S(2)}, u32[]{:S(2)}) collective-permute-start(f32[40,256]{1,0:T(8,128)S(1)} %select_maximum_fusion.own_ref), channel_id=1, source_target_pairs={{0,16},{16,0},{1,17},{17,1},{2,18},{18,2},{3,19},{19,3},{4,20},{20... | collective-permute-start | bytes 122888 | tf_op jit(solution)/shard_map/ppermute | solution.py:23
  4.7 0.9 collective-permute-done.other_ref
  6.0 0.6 shard_map.67
  6.6 13.2 %all_to_all.42.got_ref = f32[8,24,128]{2,1,0:T(8,128)S(1)} all-to-all(f32[8,24,128]{2,1,0:T(8,128)S(1)} %shard_map.67), channel_id=1, replica_groups=mesh['zl'=2,'x'=4,'core'=2,'zh'=4,'y'=4] {'zl','zh'}, dimensions={0} | all-to-all | bytes 196608 | tf_op jit(solution)/shard_map/all_to_all | solution.py:18
  19.8 1.4 %shard_map.68 = (f32[32,256]{1,0:T(8,128)S(1)}, f32[16,24,256]{2,1,0:T(8,128)}) custom-call(s32[5]{0:T(128)S(1)} %stack.23.index, f32[8,24,128]{2,1,0:T(8,128)S(1)} %all_to_all.42.got_ref), custom_call_target="tpu_custom_call" | custom-call | tf_op jit(solution)/shard_map/pallas_call | solution.py:28
  21.2 6.8 %all-to-all-start.1 = ((f32[16,24,256]{2,1,0:T(8,128)}), f32[16,24,256]{2,1,0:T(8,128)S(1)}, u32[]{:S(2)}, u32[]{:S(2)}) async-start(f32[16,24,256]{2,1,0:T(8,128)} %get-tuple-element.25), calls=%async_computation.1 | async-start | bytes 786432 | tf_op jit(solution)/shard_map/all_to_all | solution.py:18
  27.9 1.3 %shard_map.69 = (f32[384,256]{1,0:T(8,128)S(1)}, f32[384,256]{1,0:T(8,128)S(1)}) custom-call(s32[5]{0:T(128)S(1)} %stack.23.index, f32[32,256]{1,0:T(8,128)S(1)} %get-tuple-element.24.after_ref.block_ref, f32[384,512]{1,0:T(8,128)S(1)} %bitcast.9, f32[384,512]{1,0:T(8,128)S(1)} %collective-permute-done.1.other_ref), custom_call_target="tpu_custom_call" | custom-call | tf_op jit(solution)/shard_map/pallas_call | solution.py:28
  29.3 6.7 %all-to-all-done.1.got_ref = f32[16,24,256]{2,1,0:T(8,128)S(1)} async-done(((f32[16,24,256]{2,1,0:T(8,128)}), f32[16,24,256]{2,1,0:T(8,128)S(1)}, u32[]{:S(2)}, u32[]{:S(2)}) %all-to-all-start.1) | async-done | bytes 393248 | tf_op jit(solution)/shard_map/all_to_all | solution.py:18
  36.0 2.4 %shard_map.70 = (f32[16,24,256]{2,1,0:T(8,128)S(1)}, f32[16,256]{1,0:T(8,128)S(1)}) custom-call(s32[5]{0:T(128)S(1)} %stack.23.index, f32[16,24,256]{2,1,0:T(8,128)S(1)} %all-to-all-done.1.got_ref, f32[32,256]{1,0:T(8,128)S(1)} %get-tuple-element.24.after_ref.block_ref, f32[384,256]{1,0:T(8,128)S(1)} %get-tuple-element.27.kept_ref, ...), custom_call_target="tpu_custom_call" | custom-call | tf_op jit(solution)/shard_map/pallas_call | solution.py:28
  38.4 11.4 %all_to_all.43.got_ref = f32[16,24,256]{2,1,0:T(8,128)S(1)} all-to-all(f32[16,24,256]{2,1,0:T(8,128)S(1)} %get-tuple-element.29), channel_id=1, replica_groups=mesh['zl'=2,'x'=4,'core'=2,'zh'=4,'y'=4] {'x','y'}, dimensions={0} | all-to-all | bytes 786432 | tf_op jit(solution)/shard_map/all_to_all | solution.py:18
  49.8 0.6 shard_map.71
  50.4 10.7 %all_to_all.44.got_ref = f32[8,24,256]{2,1,0:T(8,128)S(1)} all-to-all(f32[8,24,256]{2,1,0:T(8,128)S(1)} %get-tuple-element.31), channel_id=1, replica_groups=mesh['zl'=2,'x'=4,'core'=2,'zh'=4,'y'=4] {'zl','zh'}, dimensions={0} | all-to-all | bytes 393216 | tf_op jit(solution)/shard_map/all_to_all | solution.py:18
  61.6 4.9 %collective-permute-start.2 = (f32[16,256]{1,0:T(8,128)S(1)}, f32[16,256]{1,0:T(8,128)S(1)}, u32[]{:S(2)}, u32[]{:S(2)}) collective-permute-start(f32[16,256]{1,0:T(8,128)S(1)} %get-tuple-element.34.ab_ref), channel_id=1, source_target_pairs={{0,16},{16,0},{1,17},{17,1},{2,18},{18,2},{3,19},{19,3},{4,20},{20... | collective-permute-start | bytes 49160 | tf_op jit(solution)/shard_map/ppermute | solution.py:23
  66.4 0.8 collective-permute-done.2.other_ref
  67.3 0.6 shard_map.73
  67.9 12.5 %all_to_all.45.got_ref = f32[16,24,256]{2,1,0:T(8,128)S(1)} all-to-all(f32[16,24,256]{2,1,0:T(8,128)S(1)} %get-tuple-element.36), channel_id=1, replica_groups=mesh['zl'=2,'x'=4,'core'=2,'zh'=4,'y'=4] {'x','y'}, dimensions={0} | all-to-all | bytes 786432 | tf_op jit(solution)/shard_map/all_to_all | solution.py:18
  80.4 2.4 %shard_map.74 = (f32[16,24,256]{2,1,0:T(8,128)S(1)}, f32[16,256]{1,0:T(8,128)S(1)}) custom-call(s32[5]{0:T(128)S(1)} %stack.23.index, f32[16,24,256]{2,1,0:T(8,128)S(1)} %all_to_all.45.got_ref, f32[32,256]{1,0:T(8,128)S(1)} %get-tuple-element.37.block_ref, f32[384,256]{1,0:T(8,128)S(1)} %get-tuple-element.27.kept_ref, f32[384,256]{1,0:T(8,128)S(1)} %get-tuple-element.28.came_ref), custom_call_target="tpu_custom_call" | custom-call | tf_op jit(solution)/shard_map/pallas_call | solution.py:28
  82.8 11.3 %all_to_all.46.got_ref = f32[16,24,256]{2,1,0:T(8,128)S(1)} all-to-all(f32[16,24,256]{2,1,0:T(8,128)S(1)} %get-tuple-element.38), channel_id=1, replica_groups=mesh['zl'=2,'x'=4,'core'=2,'zh'=4,'y'=4] {'x','y'}, dimensions={0} | all-to-all | bytes 786432 | tf_op jit(solution)/shard_map/all_to_all | solution.py:18
  94.1 0.6 shard_map.75
  94.7 9.6 %all_to_all.47.got_ref = f32[8,24,128]{2,1,0:T(8,128)S(1)} all-to-all(f32[8,24,128]{2,1,0:T(8,128)S(1)} %shard_map.75), channel_id=1, replica_groups=mesh['zl'=2,'x'=4,'core'=2,'zh'=4,'y'=4] {'zl','zh'}, dimensions={0} | all-to-all | bytes 196608 | tf_op jit(solution)/shard_map/all_to_all | solution.py:18
  104.9 4.3 %collective-permute-start.3 = (f32[24,128]{1,0:T(8,128)S(1)}, f32[24,128]{1,0:T(8,128)S(1)}, u32[]{:S(2)}, u32[]{:S(2)}) collective-permute-start(f32[24,128]{1,0:T(8,128)S(1)} %shard_map.76.grad_ref), channel_id=1, source_target_pairs={{0,16},{16,0},{1,17},{17,1},{2,18},{18,2},{3,19},{19,3},{4,20},{20... | collective-permute-start | bytes 36872 | tf_op jit(solution)/shard_map/ppermute | solution.py:23
  109.2 0.8 collective-permute-done.3.other_ref
  110.1 1.3 %shard_map.77 = (f32[12,16]{1,0:T(8,128)}, f32[16,32]{1,0:T(8,128)}, f32[2,256]{1,0:T(2,128)}) custom-call(s32[5]{0:T(128)S(1)} %stack.23.index, f32[24,128]{1,0:T(8,128)S(1)} %get-tuple-element.35.old_ref, f32[24,128]{1,0:T(8,128)S(1)} %shard_map.76.grad_ref, f32[24,128]{1,0:T(8,128)S(1)} %collective-permute-done.3.other_ref), custom_call_target="tpu_custom_call" | custom-call | tf_op jit(solution)/shard_map/pallas_call | solution.py:28
  (7 shorter events, 1.5 us)
Async XLA Ops:
  0.6 27.3 %copy-start = (f32[12,32,512]{2,1,0:T(8,128)S(1)}, f32[12,32,512]{2,1,0:T(8,128)}, u32[]{:S(2)}) copy-start(f32[12,32,512]{2,1,0:T(8,128)} %param.4) | copy-start | bytes 2359300
  1.5 4.1 %collective-permute-start = (f32[40,256]{1,0:T(8,128)S(1)}, f32[40,256]{1,0:T(8,128)S(1)}, u32[]{:S(2)}, u32[]{:S(2)}) collective-permute-start(f32[40,256]{1,0:T(8,128)S(1)} %select_maximum_fusion.own_ref), channel_id=1, source_target_pairs={{0,16},{16,0},{1,17},{17,1},{2,18},{18,2},{3,19},{19,3},{4,20},{20... | collective-permute-start | bytes 122888 | tf_op jit(solution)/shard_map/ppermute | solution.py:23
  5.6 22.4 %collective-permute-start.1 = (f32[384,512]{1,0:T(8,128)}, f32[384,512]{1,0:T(8,128)S(1)}, u32[]{:S(2)}, u32[]{:S(2)}) collective-permute-start(f32[384,512]{1,0:T(8,128)} %bitcast.8), channel_id=1, source_target_pairs={{0,16},{16,0},{1,17},{17,1},{2,18},{18,2},{3,19},{19,3},{4,20},{20... | collective-permute-start | bytes 2359304 | tf_op jit(solution)/shard_map/ppermute | solution.py:23
  21.2 14.9 %all-to-all-start.1 = ((f32[16,24,256]{2,1,0:T(8,128)}), f32[16,24,256]{2,1,0:T(8,128)S(1)}, u32[]{:S(2)}, u32[]{:S(2)}) async-start(f32[16,24,256]{2,1,0:T(8,128)} %get-tuple-element.25), calls=%async_computation.1 | async-start | bytes 786432 | tf_op jit(solution)/shard_map/all_to_all | solution.py:18
  61.6 5.7 %collective-permute-start.2 = (f32[16,256]{1,0:T(8,128)S(1)}, f32[16,256]{1,0:T(8,128)S(1)}, u32[]{:S(2)}, u32[]{:S(2)}) collective-permute-start(f32[16,256]{1,0:T(8,128)S(1)} %get-tuple-element.34.ab_ref), channel_id=1, source_target_pairs={{0,16},{16,0},{1,17},{17,1},{2,18},{18,2},{3,19},{19,3},{4,20},{20... | collective-permute-start | bytes 49160 | tf_op jit(solution)/shard_map/ppermute | solution.py:23
  104.9 5.2 %collective-permute-start.3 = (f32[24,128]{1,0:T(8,128)S(1)}, f32[24,128]{1,0:T(8,128)S(1)}, u32[]{:S(2)}, u32[]{:S(2)}) collective-permute-start(f32[24,128]{1,0:T(8,128)S(1)} %shard_map.76.grad_ref), channel_id=1, source_target_pairs={{0,16},{16,0},{1,17},{17,1},{2,18},{18,2},{3,19},{19,3},{4,20},{20... | collective-permute-start | bytes 36872 | tf_op jit(solution)/shard_map/ppermute | solution.py:23

commit v7 on v6

--- a/solution.py
+++ b/solution.py
@@ -136,9 +136,10 @@
     b = jnp.concatenate([turned[0:32], turned[32:64]], axis=1)
     for i in range(24):
         khatri[32 * i : 32 * i + 32, :] = a[i] * b
-    c = split(got_ref[:, 0:16, :].reshape(256, 256))
+    c = got_ref[:, 0:16, :].reshape(256, 256)
+    c, turned_c = split(c), split(c.T)
     parts = split(khatri[...])
-    model = product(parts, c, ((1,), (1,)))
+    model = product(parts, turned_c, ((1,), (0,)))
     target = jnp.concatenate([kept_ref[...], came_ref[...]], axis=0)
     deriv = split(jax.nn.sigmoid(model) - target)
     terms[...] = product(deriv, c, ((1,), (0,)))
@@ -269,22 +270,23 @@
     a_ref[...] = turned[0:12, 0:16]
 
 
-def arrange(index, after_ref, own_ref, other_ref, kept_ref, came_ref):
-    del after_ref
+def arrange(index, flat_ref, kept_ref, sent_ref):
     spot = lax.broadcasted_iota(jnp.int32, (512, 256), 1)
     xs, ys = spot // 64, (spot // 16) % 4
     zls, zhs, us = (spot // 8) % 2, (spot // 2) % 4, spot % 2
-    source = zls * 256 + xs * 64 + index[2] * 32 + zhs * 8 + ys * 2 + us
-    here = lax.broadcasted_iota(jnp.int32, (512, 256), 0)
-    pick = jnp.where(here == source, 1.0, 0.0).astype(jnp.bfloat16)
-    for from_ref, to_ref in ((own_ref, kept_ref), (other_ref, came_ref)):
-        rest = from_ref[...]
-        total = jnp.zeros((384, 256), F32)
-        for _ in range(3):
-            part = rest.astype(jnp.bfloat16)
-            rest = rest - part.astype(F32)
-            total = total + jnp.dot(part, pick, preferred_element_type=F32)
-        to_ref[...] = total
+    source = zls * 256 + xs * 64 + zhs * 8 + ys * 2 + us
+    gap = lax.broadcasted_iota(jnp.int32, (512, 256), 0) - source
+    own, other = index[2] * 32, 32 - index[2] * 32
+    picks = [jnp.where(gap == n, 1.0, 0.0).astype(jnp.bfloat16) for n in (own, other)]
+    totals = [jnp.zeros((384, 256), F32)] * 2
+    rest = flat_ref[...]
+    for _ in range(3):
+        part = rest.astype(jnp.bfloat16)
+        rest = rest - part.astype(F32)
+        totals = [
+            t + jnp.dot(part, pick, preferred_element_type=F32) for t, pick in zip(totals, picks)
+        ]
+    kept_ref[...], sent_ref[...] = totals
 
 
 def per_device(tensor, first_factor, second_factor, third_factor):
@@ -300,12 +302,13 @@
     shards = jnp.concatenate(
         [jnp.pad(v, ((0, n - v.shape[0]), (0, 256 - v.shape[1]))) for v, n in arguments]
     )
-    shards_other = swap(shards)
-    flat, shards_other = lax.optimization_barrier((flat, shards_other))
-    flat_other = swap(flat)
+    kept, sent = call(arrange, [(384, 256), (384, 256)], [], index, flat)
+    sent, shards_other = lax.optimization_barrier((sent, swap(shards)))
+    came = swap(sent)
     (send,) = call(first_pack, [(8, 24, 128)], [square], index, shards, shards_other)
-    block, send = call(block_from_slips, [(32, 256), wide], [], index, exchange(send, Z))
-    targets = call(arrange, [(384, 256), (384, 256)], [], index, block, flat, flat_other)
+    got, came = lax.optimization_barrier((exchange(send, Z), came))
+    block, send = call(block_from_slips, [(32, 256), wide], [], index, got)
+    targets = kept, came
     step = functools.partial(
         call, gradients, [wide, pair], [square, (768, 256), (768, 256), (32, 256)], index
     )

time: 112 us -> 111 us (level)
  blocking collectives: 68.7 us -> 82.5 us
  waiting for transfers between devices: 9.29 us -> 1.68 us
  starting transfers between devices: 19.5 us -> 13.1 us
  Pallas kernels: 12.3 us -> 10.8 us
  local copies, waits for them, and re-layouts: 0.09 us -> 1.22 us
    all_to_all x6 -> x7, blocking collectives: 68.7 us -> 82.5 us  [exchange(): got = lax.all_to_all(parts.reshape(-1, shape[2]), axis, 0, 0, tiled=True)]
    all_to_all x1 -> x0, starting transfers between devices: 6.75 us -> none  [exchange(): got = lax.all_to_all(parts.reshape(-1, shape[2]), axis, 0, 0, tiled=True)]
    all_to_all x1 -> x0, waiting for transfers between devices: 6.74 us -> none  [exchange(): got = lax.all_to_all(parts.reshape(-1, shape[2]), axis, 0, 0, tiled=True)]
    pallas_call x11, Pallas kernels: 12.3 us -> 10.8 us  [call(): pl.pallas_call(body, out_shape=[jax.ShapeDtypeStruct(s, F32) for s in out...]
    unnamed x2, local copies, waits for them, and re-layouts: 0.01 us -> 1.13 us
  transfers between devices with their start and end apart: 5 -> 4, of which waited for: 4 -> 2; matrix products, arithmetic and copies ran while one was open for 0% -> 0% of each run, Pallas kernels for 3% -> 2%
where the time goes in v7:
time: 111 us
  blocking collectives  82.5 us (74%)
  starting transfers between devices  13.1 us (12%)
  Pallas kernels  10.8 us (10%)
  waiting for transfers between devices  1.68 us (2%)
  local copies, waits for them, and re-layouts  1.22 us (1%)
    all_to_all x7, blocking collectives, exchange(): got = lax.all_to_all(parts.reshape(-1, shape[2]), axis, 0, 0, tiled=True)  82.5 us
    ppermute x4, starting transfers between devices, swap(): return lax.ppermute(value, 'core', [(0, 1), (1, 0)])  13.1 us
    pallas_call x11, Pallas kernels, call(): pl.pallas_call(body, out_shape=[jax.ShapeDtypeStruct(s, F32) for s in out...  10.8 us
  transfers between devices with their start and end apart: 4, of which 2 were waited for; matrix products, arithmetic and copies ran while one was open for 0% of the time, Pallas kernels for 2%

profile of v7, /device:TPU:1, one launch (start us, length us, event | category | flops | bytes accessed | tf_op | source)
XLA Modules:
  0.0 110.8 jit_solution(6262954625908934024)
XLA Ops:
  0.6 0.7 select_maximum_fusion.own_ref
  1.4 3.2 %collective-permute-start = (f32[40,256]{1,0:T(8,128)S(1)}, f32[40,256]{1,0:T(8,128)S(1)}, u32[]{:S(2)}, u32[]{:S(2)}) collective-permute-start(f32[40,256]{1,0:T(8,128)S(1)} %select_maximum_fusion.own_ref), channel_id=1, source_target_pairs={{0,16},{16,0},{1,17},{17,1},{2,18},{18,2},{3,19},{19,3},{4,20},{20... | collective-permute-start | bytes 122888 | tf_op jit(solution)/shard_map/ppermute | solution.py:23
  4.7 1.1 %copy-done = f32[12,32,512]{2,1,0:T(8,128)S(1)} copy-done((f32[12,32,512]{2,1,0:T(8,128)S(1)}, f32[12,32,512]{2,1,0:T(8,128)}, u32[]{:S(2)}) %copy-start) | copy-done | bytes 786456
  5.8 1.4 %shard_map.67 = (f32[384,256]{1,0:T(8,128)S(1)}, f32[384,256]{1,0:T(8,128)S(1)}) custom-call(s32[5]{0:T(128)S(1)} %stack.23.index, f32[384,512]{1,0:T(8,128)S(1)} %bitcast.8), custom_call_target="tpu_custom_call" | custom-call | tf_op jit(solution)/shard_map/pallas_call | solution.py:28
  7.3 0.6 shard_map.68
  7.9 13.2 %all_to_all.42.got_ref = f32[8,24,128]{2,1,0:T(8,128)S(1)} all-to-all(f32[8,24,128]{2,1,0:T(8,128)S(1)} %shard_map.68), channel_id=1, replica_groups=mesh['zl'=2,'x'=4,'core'=2,'zh'=4,'y'=4] {'zl','zh'}, dimensions={0} | all-to-all | bytes 196608 | tf_op jit(solution)/shard_map/all_to_all | solution.py:18
  21.1 0.6 shard_map.69
  21.7 14.5 %all_to_all.43.got_ref = f32[16,24,256]{2,1,0:T(8,128)S(1)} all-to-all(f32[16,24,256]{2,1,0:T(8,128)S(1)} %get-tuple-element.30), channel_id=1, replica_groups=mesh['zl'=2,'x'=4,'core'=2,'zh'=4,'y'=4] {'x','y'}, dimensions={0} | all-to-all | bytes 786432 | tf_op jit(solution)/shard_map/all_to_all | solution.py:18
  36.3 2.0 %shard_map.70 = (f32[16,24,256]{2,1,0:T(8,128)S(1)}, f32[16,256]{1,0:T(8,128)S(1)}) custom-call(s32[5]{0:T(128)S(1)} %stack.23.index, f32[16,24,256]{2,1,0:T(8,128)S(1)} %all_to_all.43.got_ref, f32[32,256]{1,0:T(8,128)S(1)} %get-tuple-element.29.block_ref, f32[384,256]{1,0:T(8,128)S(1)} %get-tuple-element.31.kept_ref, ...), custom_call_target="tpu_custom_call" | custom-call | tf_op jit(solution)/shard_map/pallas_call | solution.py:28
  38.3 11.6 %all_to_all.44.got_ref = f32[16,24,256]{2,1,0:T(8,128)S(1)} all-to-all(f32[16,24,256]{2,1,0:T(8,128)S(1)} %get-tuple-element.33), channel_id=1, replica_groups=mesh['zl'=2,'x'=4,'core'=2,'zh'=4,'y'=4] {'x','y'}, dimensions={0} | all-to-all | bytes 786432 | tf_op jit(solution)/shard_map/all_to_all | solution.py:18
  49.9 0.6 shard_map.71
  50.5 9.7 %all_to_all.45.got_ref = f32[8,24,256]{2,1,0:T(8,128)S(1)} all-to-all(f32[8,24,256]{2,1,0:T(8,128)S(1)} %get-tuple-element.35), channel_id=1, replica_groups=mesh['zl'=2,'x'=4,'core'=2,'zh'=4,'y'=4] {'zl','zh'}, dimensions={0} | all-to-all | bytes 393216 | tf_op jit(solution)/shard_map/all_to_all | solution.py:18
  60.2 0.6 shard_map.72
  60.8 5.4 %collective-permute-start.2 = (f32[16,256]{1,0:T(8,128)S(1)}, f32[16,256]{1,0:T(8,128)S(1)}, u32[]{:S(2)}, u32[]{:S(2)}) collective-permute-start(f32[16,256]{1,0:T(8,128)S(1)} %get-tuple-element.38.ab_ref), channel_id=1, source_target_pairs={{0,16},{16,0},{1,17},{17,1},{2,18},{18,2},{3,19},{19,3},{4,20},{20... | collective-permute-start | bytes 49160 | tf_op jit(solution)/shard_map/ppermute | solution.py:23
  66.2 0.8 collective-permute-done.2.other_ref
  67.0 0.6 shard_map.73
  67.6 12.5 %all_to_all.46.got_ref = f32[16,24,256]{2,1,0:T(8,128)S(1)} all-to-all(f32[16,24,256]{2,1,0:T(8,128)S(1)} %get-tuple-element.40), channel_id=1, replica_groups=mesh['zl'=2,'x'=4,'core'=2,'zh'=4,'y'=4] {'x','y'}, dimensions={0} | all-to-all | bytes 786432 | tf_op jit(solution)/shard_map/all_to_all | solution.py:18
  80.1 2.0 %shard_map.74 = (f32[16,24,256]{2,1,0:T(8,128)S(1)}, f32[16,256]{1,0:T(8,128)S(1)}) custom-call(s32[5]{0:T(128)S(1)} %stack.23.index, f32[16,24,256]{2,1,0:T(8,128)S(1)} %all_to_all.46.got_ref, f32[32,256]{1,0:T(8,128)S(1)} %get-tuple-element.41.block_ref, f32[384,256]{1,0:T(8,128)S(1)} %get-tuple-element.31.kept_ref, ...), custom_call_target="tpu_custom_call" | custom-call | tf_op jit(solution)/shard_map/pallas_call | solution.py:28
  82.1 11.3 %all_to_all.47.got_ref = f32[16,24,256]{2,1,0:T(8,128)S(1)} all-to-all(f32[16,24,256]{2,1,0:T(8,128)S(1)} %get-tuple-element.42), channel_id=1, replica_groups=mesh['zl'=2,'x'=4,'core'=2,'zh'=4,'y'=4] {'x','y'}, dimensions={0} | all-to-all | bytes 786432 | tf_op jit(solution)/shard_map/all_to_all | solution.py:18
  93.4 0.6 shard_map.75
  94.0 9.7 %all_to_all.48.got_ref = f32[8,24,128]{2,1,0:T(8,128)S(1)} all-to-all(f32[8,24,128]{2,1,0:T(8,128)S(1)} %shard_map.75), channel_id=1, replica_groups=mesh['zl'=2,'x'=4,'core'=2,'zh'=4,'y'=4] {'zl','zh'}, dimensions={0} | all-to-all | bytes 196608 | tf_op jit(solution)/shard_map/all_to_all | solution.py:18
  104.3 4.3 %collective-permute-start.3 = (f32[24,128]{1,0:T(8,128)S(1)}, f32[24,128]{1,0:T(8,128)S(1)}, u32[]{:S(2)}, u32[]{:S(2)}) collective-permute-start(f32[24,128]{1,0:T(8,128)S(1)} %shard_map.76.grad_ref), channel_id=1, source_target_pairs={{0,16},{16,0},{1,17},{17,1},{2,18},{18,2},{3,19},{19,3},{4,20},{20... | collective-permute-start | bytes 36872 | tf_op jit(solution)/shard_map/ppermute | solution.py:23
  108.6 0.8 collective-permute-done.3.other_ref
  109.5 1.3 %shard_map.77 = (f32[12,16]{1,0:T(8,128)}, f32[16,32]{1,0:T(8,128)}, f32[2,256]{1,0:T(2,128)}) custom-call(s32[5]{0:T(128)S(1)} %stack.23.index, f32[24,128]{1,0:T(8,128)S(1)} %get-tuple-element.39.old_ref, f32[24,128]{1,0:T(8,128)S(1)} %shard_map.76.grad_ref, f32[24,128]{1,0:T(8,128)S(1)} %collective-permute-done.3.other_ref), custom_call_target="tpu_custom_call" | custom-call | tf_op jit(solution)/shard_map/pallas_call | solution.py:28
  (6 shorter events, 0.7 us)
Async XLA Ops:
  1.4 5.8 %collective-permute-start = (f32[40,256]{1,0:T(8,128)S(1)}, f32[40,256]{1,0:T(8,128)S(1)}, u32[]{:S(2)}, u32[]{:S(2)}) collective-permute-start(f32[40,256]{1,0:T(8,128)S(1)} %select_maximum_fusion.own_ref), channel_id=1, source_target_pairs={{0,16},{16,0},{1,17},{17,1},{2,18},{18,2},{3,19},{19,3},{4,20},{20... | collective-permute-start | bytes 122888 | tf_op jit(solution)/shard_map/ppermute | solution.py:23
  4.7 1.1 %copy-start = (f32[12,32,512]{2,1,0:T(8,128)S(1)}, f32[12,32,512]{2,1,0:T(8,128)}, u32[]{:S(2)}) copy-start(f32[12,32,512]{2,1,0:T(8,128)} %param.4) | copy-start | bytes 2359300
  7.2 13.9 %collective-permute-start.1 = (f32[384,256]{1,0:T(8,128)S(1)}, f32[384,256]{1,0:T(8,128)S(1)}, u32[]{:S(2)}, u32[]{:S(2)}) collective-permute-start(f32[384,256]{1,0:T(8,128)S(1)} %get-tuple-element.27), channel_id=1, source_target_pairs={{0,16},{16,0},{1,17},{17,1},{2,18},{18,2},{3,19},{19,3},{4,20},{20... | collective-permute-start | bytes 1179656 | tf_op jit(solution)/shard_map/ppermute | solution.py:23
  60.8 6.2 %collective-permute-start.2 = (f32[16,256]{1,0:T(8,128)S(1)}, f32[16,256]{1,0:T(8,128)S(1)}, u32[]{:S(2)}, u32[]{:S(2)}) collective-permute-start(f32[16,256]{1,0:T(8,128)S(1)} %get-tuple-element.38.ab_ref), channel_id=1, source_target_pairs={{0,16},{16,0},{1,17},{17,1},{2,18},{18,2},{3,19},{19,3},{4,20},{20... | collective-permute-start | bytes 49160 | tf_op jit(solution)/shard_map/ppermute | solution.py:23
  104.3 5.2 %collective-permute-start.3 = (f32[24,128]{1,0:T(8,128)S(1)}, f32[24,128]{1,0:T(8,128)S(1)}, u32[]{:S(2)}, u32[]{:S(2)}) collective-permute-start(f32[24,128]{1,0:T(8,128)S(1)} %shard_map.76.grad_ref), channel_id=1, source_target_pairs={{0,16},{16,0},{1,17},{17,1},{2,18},{18,2},{3,19},{19,3},{4,20},{20... | collective-permute-start | bytes 36872 | tf_op jit(solution)/shard_map/ppermute | solution.py:23

commit v8 on v6

--- a/solution.py
+++ b/solution.py
@@ -82,7 +82,7 @@
     return c, ab
 
 
-def first_pack(index, own_ref, other_ref, out_ref, pad):
+def first_pack(index, own_ref, other_ref, out_ref, done_ref, pad):
     even = index[2] == 0
     own, other = own_ref[0:32, 0:128], other_ref[0:32, 0:128]
     low, high = jnp.where(even, own, other), jnp.where(even, other, own)
@@ -95,6 +95,7 @@
         out_ref[p, 0:2, :] = own_ref[32:34, 0:128]
         out_ref[p, 2:4, :] = own_ref[32:34, 128:256]
         out_ref[p, 8:24, :] = ab
+    done_ref[...] = ab
 
 
 def block_from_slips(index, got_ref, block_ref, out_ref):
@@ -136,9 +137,10 @@
     b = jnp.concatenate([turned[0:32], turned[32:64]], axis=1)
     for i in range(24):
         khatri[32 * i : 32 * i + 32, :] = a[i] * b
-    c = split(got_ref[:, 0:16, :].reshape(256, 256))
+    c = got_ref[:, 0:16, :].reshape(256, 256)
+    c, turned_c = split(c), split(c.T)
     parts = split(khatri[...])
-    model = product(parts, c, ((1,), (1,)))
+    model = product(parts, turned_c, ((1,), (0,)))
     target = jnp.concatenate([kept_ref[...], came_ref[...]], axis=0)
     deriv = split(jax.nn.sigmoid(model) - target)
     terms[...] = product(deriv, c, ((1,), (0,)))
@@ -303,9 +305,12 @@
     shards_other = swap(shards)
     flat, shards_other = lax.optimization_barrier((flat, shards_other))
     flat_other = swap(flat)
-    (send,) = call(first_pack, [(8, 24, 128)], [square], index, shards, shards_other)
-    block, send = call(block_from_slips, [(32, 256), wide], [], index, exchange(send, Z))
-    targets = call(arrange, [(384, 256), (384, 256)], [], index, block, flat, flat_other)
+    send, done = call(
+        first_pack, [(8, 24, 128), (16, 128)], [square], index, shards, shards_other
+    )
+    targets = call(arrange, [(384, 256), (384, 256)], [], index, done, flat, flat_other)
+    got, targets = lax.optimization_barrier((exchange(send, Z), targets))
+    block, send = call(block_from_slips, [(32, 256), wide], [], index, got)
     step = functools.partial(
         call, gradients, [wide, pair], [square, (768, 256), (768, 256), (32, 256)], index
     )

time: 112 us -> 111 us (level)
  waiting for transfers between devices: 9.29 us -> 6.96 us
  blocking collectives: 68.7 us -> 70 us
    all_to_all x1, waiting for transfers between devices: 6.74 us -> 4.41 us  [exchange(): got = lax.all_to_all(parts.reshape(-1, shape[2]), axis, 0, 0, tiled=True)]
    all_to_all x6, blocking collectives: 68.7 us -> 70 us  [exchange(): got = lax.all_to_all(parts.reshape(-1, shape[2]), axis, 0, 0, tiled=True)]
    unnamed x2, local copies, waits for them, and re-layouts: 0.01 us -> 1.13 us
  transfers between devices with their start and end apart: 5 -> 5, of which waited for: 4 -> 4; matrix products, arithmetic and copies ran while one was open for 0% -> 0% of each run, Pallas kernels for 3% -> 2%
where the time goes in v8:
time: 111 us; the launch traced here: 110 us
  blocking collectives  70 us (63%)
  starting transfers between devices  19.3 us (17%)
  Pallas kernels  11.5 us (10%)
  waiting for transfers between devices  6.96 us (6%)
  local copies, waits for them, and re-layouts  1.21 us (1%)
    all_to_all x6, blocking collectives, exchange(): got = lax.all_to_all(parts.reshape(-1, shape[2]), axis, 0, 0, tiled=True)  70 us
    ppermute x4, starting transfers between devices, swap(): return lax.ppermute(value, 'core', [(0, 1), (1, 0)])  12.8 us
    pallas_call x11, Pallas kernels, call(): pl.pallas_call(body, out_shape=[jax.ShapeDtypeStruct(s, F32) for s in out...  11.5 us
    all_to_all x1, starting transfers between devices, exchange(): got = lax.all_to_all(parts.reshape(-1, shape[2]), axis, 0, 0, tiled=True)  6.45 us
    all_to_all x1, waiting for transfers between devices, exchange(): got = lax.all_to_all(parts.reshape(-1, shape[2]), axis, 0, 0, tiled=True)  4.41 us
    ppermute x4, waiting for transfers between devices, swap(): return lax.ppermute(value, 'core', [(0, 1), (1, 0)])  2.55 us
  transfers between devices with their start and end apart: 5, of which 4 were waited for; matrix products, arithmetic and copies ran while one was open for 0% of the time, Pallas kernels for 2%

profile of v8, /device:TPU:1, one launch (start us, length us, event | category | flops | bytes accessed | tf_op | source)
XLA Modules:
  0.0 110.5 jit_solution(11340355514180565924)
XLA Ops:
  0.6 0.7 select_maximum_fusion.own_ref
  1.4 3.2 %collective-permute-start = (f32[40,256]{1,0:T(8,128)S(1)}, f32[40,256]{1,0:T(8,128)S(1)}, u32[]{:S(2)}, u32[]{:S(2)}) collective-permute-start(f32[40,256]{1,0:T(8,128)S(1)} %select_maximum_fusion.own_ref), channel_id=1, source_target_pairs={{0,16},{16,0},{1,17},{17,1},{2,18},{18,2},{3,19},{19,3},{4,20},{20... | collective-permute-start | bytes 122888 | tf_op jit(solution)/shard_map/ppermute | solution.py:23
  4.6 0.9 collective-permute-done.other_ref
  5.9 1.3 %shard_map.67 = (f32[8,24,128]{2,1,0:T(8,128)}, f32[16,128]{1,0:T(8,128)S(1)}) custom-call(s32[5]{0:T(128)S(1)} %stack.23.index, f32[40,256]{1,0:T(8,128)S(1)} %select_maximum_fusion.own_ref, f32[40,256]{1,0:T(8,128)S(1)} %collective-permute-done.other_ref), custom_call_target="tpu_custom_call" | custom-call | tf_op jit(solution)/shard_map/pallas_call | solution.py:28
  7.2 6.4 %all-to-all-start = ((f32[8,24,128]{2,1,0:T(8,128)}), f32[8,24,128]{2,1,0:T(8,128)S(1)}, u32[]{:S(2)}, u32[]{:S(2)}) async-start(f32[8,24,128]{2,1,0:T(8,128)} %get-tuple-element.29), calls=%async_computation | async-start | bytes 196608 | tf_op jit(solution)/shard_map/all_to_all | solution.py:18
  13.7 1.1 %copy-done = f32[12,32,512]{2,1,0:T(8,128)S(1)} copy-done((f32[12,32,512]{2,1,0:T(8,128)S(1)}, f32[12,32,512]{2,1,0:T(8,128)}, u32[]{:S(2)}) %copy-start) | copy-done | bytes 786456
  14.8 1.4 %shard_map.68 = (f32[384,256]{1,0:T(8,128)S(1)}, f32[384,256]{1,0:T(8,128)S(1)}) custom-call(s32[5]{0:T(128)S(1)} %stack.23.index, f32[16,128]{1,0:T(8,128)S(1)} %get-tuple-element.30.after_ref, f32[384,512]{1,0:T(8,128)S(1)} %bitcast.9, f32[384,512]{1,0:T(8,128)S(1)} %collective-permute-done.1.other_ref), custom_call_target="tpu_custom_call" | custom-call | tf_op jit(solution)/shard_map/pallas_call | solution.py:28
  16.2 4.4 %all-to-all-done.got_ref = f32[8,24,128]{2,1,0:T(8,128)S(1)} async-done(((f32[8,24,128]{2,1,0:T(8,128)}), f32[8,24,128]{2,1,0:T(8,128)S(1)}, u32[]{:S(2)}, u32[]{:S(2)}) %all-to-all-start) | async-done | bytes 98336 | tf_op jit(solution)/shard_map/all_to_all | solution.py:18
  20.6 0.6 shard_map.69
  21.2 14.7 %all_to_all.42.got_ref = f32[16,24,256]{2,1,0:T(8,128)S(1)} all-to-all(f32[16,24,256]{2,1,0:T(8,128)S(1)} %get-tuple-element.36), channel_id=1, replica_groups=mesh['zl'=2,'x'=4,'core'=2,'zh'=4,'y'=4] {'x','y'}, dimensions={0} | all-to-all | bytes 786432 | tf_op jit(solution)/shard_map/all_to_all | solution.py:18
  35.9 2.0 %shard_map.70 = (f32[16,24,256]{2,1,0:T(8,128)S(1)}, f32[16,256]{1,0:T(8,128)S(1)}) custom-call(s32[5]{0:T(128)S(1)} %stack.23.index, f32[16,24,256]{2,1,0:T(8,128)S(1)} %all_to_all.42.got_ref, f32[32,256]{1,0:T(8,128)S(1)} %get-tuple-element.35.block_ref, f32[384,256]{1,0:T(8,128)S(1)} %get-tuple-element.37.kept_ref, f32[384,256]{1,0:T(8,128)S(1)} %get-tuple-element.38.came_ref), custom_call_target="tpu_custom_call" | custom-call | tf_op jit(solution)/shard_map/pallas_call | solution.py:28
  37.9 11.4 %all_to_all.43.got_ref = f32[16,24,256]{2,1,0:T(8,128)S(1)} all-to-all(f32[16,24,256]{2,1,0:T(8,128)S(1)} %get-tuple-element.39), channel_id=1, replica_groups=mesh['zl'=2,'x'=4,'core'=2,'zh'=4,'y'=4] {'x','y'}, dimensions={0} | all-to-all | bytes 786432 | tf_op jit(solution)/shard_map/all_to_all | solution.py:18
  49.8 10.7 %all_to_all.44.got_ref = f32[8,24,256]{2,1,0:T(8,128)S(1)} all-to-all(f32[8,24,256]{2,1,0:T(8,128)S(1)} %get-tuple-element.41), channel_id=1, replica_groups=mesh['zl'=2,'x'=4,'core'=2,'zh'=4,'y'=4] {'zl','zh'}, dimensions={0} | all-to-all | bytes 393216 | tf_op jit(solution)/shard_map/all_to_all | solution.py:18
  61.1 4.9 %collective-permute-start.2 = (f32[16,256]{1,0:T(8,128)S(1)}, f32[16,256]{1,0:T(8,128)S(1)}, u32[]{:S(2)}, u32[]{:S(2)}) collective-permute-start(f32[16,256]{1,0:T(8,128)S(1)} %get-tuple-element.44.ab_ref), channel_id=1, source_target_pairs={{0,16},{16,0},{1,17},{17,1},{2,18},{18,2},{3,19},{19,3},{4,20},{20... | collective-permute-start | bytes 49160 | tf_op jit(solution)/shard_map/ppermute | solution.py:23
  66.0 0.8 collective-permute-done.2.other_ref
  66.8 0.6 shard_map.73
  67.5 12.5 %all_to_all.45.got_ref = f32[16,24,256]{2,1,0:T(8,128)S(1)} all-to-all(f32[16,24,256]{2,1,0:T(8,128)S(1)} %get-tuple-element.46), channel_id=1, replica_groups=mesh['zl'=2,'x'=4,'core'=2,'zh'=4,'y'=4] {'x','y'}, dimensions={0} | all-to-all | bytes 786432 | tf_op jit(solution)/shard_map/all_to_all | solution.py:18
  79.9 2.0 %shard_map.74 = (f32[16,24,256]{2,1,0:T(8,128)S(1)}, f32[16,256]{1,0:T(8,128)S(1)}) custom-call(s32[5]{0:T(128)S(1)} %stack.23.index, f32[16,24,256]{2,1,0:T(8,128)S(1)} %all_to_all.45.got_ref, f32[32,256]{1,0:T(8,128)S(1)} %get-tuple-element.47.block_ref, f32[384,256]{1,0:T(8,128)S(1)} %get-tuple-element.37.kept_ref, f32[384,256]{1,0:T(8,128)S(1)} %get-tuple-element.38.came_ref), custom_call_target="tpu_custom_call" | custom-call | tf_op jit(solution)/shard_map/pallas_call | solution.py:28
  81.9 11.3 %all_to_all.46.got_ref = f32[16,24,256]{2,1,0:T(8,128)S(1)} all-to-all(f32[16,24,256]{2,1,0:T(8,128)S(1)} %get-tuple-element.48), channel_id=1, replica_groups=mesh['zl'=2,'x'=4,'core'=2,'zh'=4,'y'=4] {'x','y'}, dimensions={0} | all-to-all | bytes 786432 | tf_op jit(solution)/shard_map/all_to_all | solution.py:18
  93.2 0.6 shard_map.75
  93.8 9.6 %all_to_all.47.got_ref = f32[8,24,128]{2,1,0:T(8,128)S(1)} all-to-all(f32[8,24,128]{2,1,0:T(8,128)S(1)} %shard_map.75), channel_id=1, replica_groups=mesh['zl'=2,'x'=4,'core'=2,'zh'=4,'y'=4] {'zl','zh'}, dimensions={0} | all-to-all | bytes 196608 | tf_op jit(solution)/shard_map/all_to_all | solution.py:18
  104.0 4.3 %collective-permute-start.3 = (f32[24,128]{1,0:T(8,128)S(1)}, f32[24,128]{1,0:T(8,128)S(1)}, u32[]{:S(2)}, u32[]{:S(2)}) collective-permute-start(f32[24,128]{1,0:T(8,128)S(1)} %shard_map.76.grad_ref), channel_id=1, source_target_pairs={{0,16},{16,0},{1,17},{17,1},{2,18},{18,2},{3,19},{19,3},{4,20},{20... | collective-permute-start | bytes 36872 | tf_op jit(solution)/shard_map/ppermute | solution.py:23
  108.3 0.8 collective-permute-done.3.other_ref
  109.2 1.3 %shard_map.77 = (f32[12,16]{1,0:T(8,128)}, f32[16,32]{1,0:T(8,128)}, f32[2,256]{1,0:T(2,128)}) custom-call(s32[5]{0:T(128)S(1)} %stack.23.index, f32[24,128]{1,0:T(8,128)S(1)} %get-tuple-element.45.old_ref, f32[24,128]{1,0:T(8,128)S(1)} %shard_map.76.grad_ref, f32[24,128]{1,0:T(8,128)S(1)} %collective-permute-done.3.other_ref), custom_call_target="tpu_custom_call" | custom-call | tf_op jit(solution)/shard_map/pallas_call | solution.py:28
  (7 shorter events, 2.1 us)
Async XLA Ops:
  1.4 4.1 %collective-permute-start = (f32[40,256]{1,0:T(8,128)S(1)}, f32[40,256]{1,0:T(8,128)S(1)}, u32[]{:S(2)}, u32[]{:S(2)}) collective-permute-start(f32[40,256]{1,0:T(8,128)S(1)} %select_maximum_fusion.own_ref), channel_id=1, source_target_pairs={{0,16},{16,0},{1,17},{17,1},{2,18},{18,2},{3,19},{19,3},{4,20},{20... | collective-permute-start | bytes 122888 | tf_op jit(solution)/shard_map/ppermute | solution.py:23
  5.5 8.2 %collective-permute-start.1 = (f32[384,512]{1,0:T(8,128)}, f32[384,512]{1,0:T(8,128)S(1)}, u32[]{:S(2)}, u32[]{:S(2)}) collective-permute-start(f32[384,512]{1,0:T(8,128)} %bitcast.8), channel_id=1, source_target_pairs={{0,16},{16,0},{1,17},{17,1},{2,18},{18,2},{3,19},{19,3},{4,20},{20... | collective-permute-start | bytes 2359304 | tf_op jit(solution)/shard_map/ppermute | solution.py:23
  7.2 13.4 %all-to-all-start = ((f32[8,24,128]{2,1,0:T(8,128)}), f32[8,24,128]{2,1,0:T(8,128)S(1)}, u32[]{:S(2)}, u32[]{:S(2)}) async-start(f32[8,24,128]{2,1,0:T(8,128)} %get-tuple-element.29), calls=%async_computation | async-start | bytes 196608 | tf_op jit(solution)/shard_map/all_to_all | solution.py:18
  13.6 1.1 %copy-start = (f32[12,32,512]{2,1,0:T(8,128)S(1)}, f32[12,32,512]{2,1,0:T(8,128)}, u32[]{:S(2)}) copy-start(f32[12,32,512]{2,1,0:T(8,128)} %param.4) | copy-start | bytes 2359300
  61.1 5.8 %collective-permute-start.2 = (f32[16,256]{1,0:T(8,128)S(1)}, f32[16,256]{1,0:T(8,128)S(1)}, u32[]{:S(2)}, u32[]{:S(2)}) collective-permute-start(f32[16,256]{1,0:T(8,128)S(1)} %get-tuple-element.44.ab_ref), channel_id=1, source_target_pairs={{0,16},{16,0},{1,17},{17,1},{2,18},{18,2},{3,19},{19,3},{4,20},{20... | collective-permute-start | bytes 49160 | tf_op jit(solution)/shard_map/ppermute | solution.py:23
  104.0 5.2 %collective-permute-start.3 = (f32[24,128]{1,0:T(8,128)S(1)}, f32[24,128]{1,0:T(8,128)S(1)}, u32[]{:S(2)}, u32[]{:S(2)}) collective-permute-start(f32[24,128]{1,0:T(8,128)S(1)} %shard_map.76.grad_ref), channel_id=1, source_target_pairs={{0,16},{16,0},{1,17},{17,1},{2,18},{18,2},{3,19},{19,3},{4,20},{20... | collective-permute-start | bytes 36872 | tf_op jit(solution)/shard_map/ppermute | solution.py:23

commit v9 on v8

--- a/solution.py
+++ b/solution.py
@@ -23,16 +23,19 @@
     return lax.ppermute(value, "core", [(0, 1), (1, 0)])
 
 
-def call(body, outs, scratch, index, *operands):
+def call(body, outs, scratch, *operands):
+    def kernel(*refs):
+        body([lax.axis_index(n) for n in ("zl", "x", "core", "zh", "y")], *refs)
+
     vmem = pl.BlockSpec(memory_space=pltpu.VMEM)
     return pl.pallas_call(
-        body,
+        kernel,
         out_shape=[jax.ShapeDtypeStruct(s, F32) for s in outs],
-        in_specs=[pl.BlockSpec(memory_space=pltpu.SMEM)] + [vmem] * len(operands),
+        in_specs=[vmem] * len(operands),
         out_specs=[vmem] * len(outs),
         scratch_shapes=[pltpu.VMEM(s, F32) for s in scratch],
         compiler_params=pltpu.CompilerParams(vmem_limit_bytes=40 * 1024 * 1024),
-    )(index, *operands)
+    )(*operands)
 
 
 def lanes(rows=16):
@@ -290,7 +293,6 @@
 
 
 def per_device(tensor, first_factor, second_factor, third_factor):
-    index = jnp.stack([lax.axis_index(n) for n in ("zl", "x", "core", "zh", "y")])
     n_i, n_j, depth = tensor.shape
     size_i, size_j = n_i * 16, n_j * 16
     rates = tuple(4.0 / float(n) ** 0.5 for n in (size_j * depth, size_i * depth, size_i * size_j))
@@ -306,36 +308,34 @@
     flat, shards_other = lax.optimization_barrier((flat, shards_other))
     flat_other = swap(flat)
     send, done = call(
-        first_pack, [(8, 24, 128), (16, 128)], [square], index, shards, shards_other
-    )
-    targets = call(arrange, [(384, 256), (384, 256)], [], index, done, flat, flat_other)
+        first_pack, [(8, 24, 128), (16, 128)], [square], shards, shards_other
+    )
+    targets = call(arrange, [(384, 256), (384, 256)], [], done, flat, flat_other)
     got, targets = lax.optimization_barrier((exchange(send, Z), targets))
-    block, send = call(block_from_slips, [(32, 256), wide], [], index, got)
+    block, send = call(block_from_slips, [(32, 256), wide], [], got)
     step = functools.partial(
-        call, gradients, [wide, pair], [square, (768, 256), (768, 256), (32, 256)], index
+        call, gradients, [wide, pair], [square, (768, 256), (768, 256), (32, 256)]
     )
 
     send, own = step(exchange(send, XY), block, *targets)
-    send, own = call(middle_pack, [(8, 24, 256), pair], [], index, exchange(send, XY), own)
-    grad_c, grad_ab = call(middle_sum, [pair, pair], [], index, exchange(send, Z), own)
+    send, own = call(middle_pack, [(8, 24, 256), pair], [], exchange(send, XY), own)
+    grad_c, grad_ab = call(middle_sum, [pair, pair], [], exchange(send, Z), own)
     slip, block, send = call(
         functools.partial(middle_update, rates),
         [(24, 128), (32, 256), wide],
         [(32, 256)],
-        index,
         block,
         grad_c,
         grad_ab,
         swap(grad_ab),
     )
     send, own = step(exchange(send, XY), block, *targets)
-    (send,) = call(last_pack, [(8, 24, 128)], [(32, 256)], index, exchange(send, XY), own)
-    (grad,) = call(last_sum, [(24, 128)], [], index, exchange(send, Z))
+    (send,) = call(last_pack, [(8, 24, 128)], [(32, 256)], exchange(send, XY), own)
+    (grad,) = call(last_sum, [(24, 128)], [], exchange(send, Z))
     new_a, new_bt, new_c = call(
         functools.partial(last_update, rates),
         [(n_i, 16), (16, n_j), third_factor.shape],
         [square],
-        index,
         slip,
         grad,
         swap(grad),

time: 111 us -> 105 us (0.946)
  Pallas kernels: 11.5 us -> 5.53 us
    pallas_call x11, Pallas kernels: 11.5 us -> 5.53 us  [call(): pl.pallas_call(kernel, out_shape=[jax.ShapeDtypeStruct(s, F32) for s in o...]
  transfers between devices with their start and end apart: 5 -> 5, of which waited for: 4 -> 4; matrix products, arithmetic and copies ran while one was open for 0% -> 0% of each run, Pallas kernels for 2% -> 1%
where the time goes in v9:
time: 105 us
  blocking collectives  70 us (67%)
  starting transfers between devices  19.3 us (18%)
  waiting for transfers between devices  7.52 us (7%)
  Pallas kernels  5.53 us (5%)
  local copies, waits for them, and re-layouts  1.13 us (1%)
    all_to_all x6, blocking collectives, exchange(): got = lax.all_to_all(parts.reshape(-1, shape[2]), axis, 0, 0, tiled=True)  70 us
    ppermute x4, starting transfers between devices, swap(): return lax.ppermute(value, 'core', [(0, 1), (1, 0)])  12.8 us
    all_to_all x1, starting transfers between devices, exchange(): got = lax.all_to_all(parts.reshape(-1, shape[2]), axis, 0, 0, tiled=True)  6.45 us
    pallas_call x11, Pallas kernels, call(): pl.pallas_call(kernel, out_shape=[jax.ShapeDtypeStruct(s, F32) for s in o...  5.53 us
    all_to_all x1, waiting for transfers between devices, exchange(): got = lax.all_to_all(parts.reshape(-1, shape[2]), axis, 0, 0, tiled=True)  4.97 us
    ppermute x4, waiting for transfers between devices, swap(): return lax.ppermute(value, 'core', [(0, 1), (1, 0)])  2.55 us
  transfers between devices with their start and end apart: 5, of which 4 were waited for; matrix products, arithmetic and copies ran while one was open for 0% of the time, Pallas kernels for 1%

profile of v9, /device:TPU:1, one launch (start us, length us, event | category | flops | bytes accessed | tf_op | source)
XLA Modules:
  0.0 104.9 jit_solution(11669760788415957499)
XLA Ops:
  0.6 0.7 select_maximum_fusion.refs_0_
  1.4 3.2 %collective-permute-start = (f32[40,256]{1,0:T(8,128)S(1)}, f32[40,256]{1,0:T(8,128)S(1)}, u32[]{:S(2)}, u32[]{:S(2)}) collective-permute-start(f32[40,256]{1,0:T(8,128)S(1)} %select_maximum_fusion.refs_0_), channel_id=1, source_target_pairs={{0,16},{16,0},{1,17},{17,1},{2,18},{18,2},{3,19},{19,3},{4,20},{20... | collective-permute-start | bytes 122888 | tf_op jit(solution)/shard_map/ppermute | solution.py:23
  4.6 0.9 collective-permute-done.refs_1_
  5.5 0.3 collective-permute-start.1
  5.8 0.7 shard_map.67
  6.6 6.4 %all-to-all-start = ((f32[8,24,128]{2,1,0:T(8,128)}), f32[8,24,128]{2,1,0:T(8,128)S(1)}, u32[]{:S(2)}, u32[]{:S(2)}) async-start(f32[8,24,128]{2,1,0:T(8,128)} %get-tuple-element.29), calls=%async_computation | async-start | bytes 196608 | tf_op jit(solution)/shard_map/all_to_all | solution.py:18
  13.0 1.1 %copy-done = f32[12,32,512]{2,1,0:T(8,128)S(1)} copy-done((f32[12,32,512]{2,1,0:T(8,128)S(1)}, f32[12,32,512]{2,1,0:T(8,128)}, u32[]{:S(2)}) %copy-start) | copy-done | bytes 786456
  14.2 0.8 shard_map.68
  15.0 5.0 %all-to-all-done.refs_0_ = f32[8,24,128]{2,1,0:T(8,128)S(1)} async-done(((f32[8,24,128]{2,1,0:T(8,128)}), f32[8,24,128]{2,1,0:T(8,128)S(1)}, u32[]{:S(2)}, u32[]{:S(2)}) %all-to-all-start) | async-done | bytes 98336 | tf_op jit(solution)/shard_map/all_to_all | solution.py:18
  19.9 0.1 shard_map.69
  20.0 14.7 %all_to_all.42.refs_0_ = f32[16,24,256]{2,1,0:T(8,128)S(1)} all-to-all(f32[16,24,256]{2,1,0:T(8,128)S(1)} %get-tuple-element.36), channel_id=1, replica_groups=mesh['zl'=2,'x'=4,'core'=2,'zh'=4,'y'=4] {'x','y'}, dimensions={0} | all-to-all | bytes 786432 | tf_op jit(solution)/shard_map/all_to_all | solution.py:18
  34.7 1.5 %shard_map.70 = (f32[16,24,256]{2,1,0:T(8,128)S(1)}, f32[16,256]{1,0:T(8,128)S(1)}) custom-call(f32[16,24,256]{2,1,0:T(8,128)S(1)} %all_to_all.42.refs_0_, f32[32,256]{1,0:T(8,128)S(1)} %get-tuple-element.35.refs_1_.refs_0_, f32[384,256]{1,0:T(8,128)S(1)} %get-tuple-element.37.refs_2_, f32[384,256]{1,0:T(8,128)S(1)} %get-tuple-element.38.refs_3_), custom_call_target="tpu_custom_call" | custom-call | tf_op jit(solution)/shard_map/pallas_call | solution.py:31
  36.2 11.4 %all_to_all.43.refs_0_ = f32[16,24,256]{2,1,0:T(8,128)S(1)} all-to-all(f32[16,24,256]{2,1,0:T(8,128)S(1)} %get-tuple-element.39), channel_id=1, replica_groups=mesh['zl'=2,'x'=4,'core'=2,'zh'=4,'y'=4] {'x','y'}, dimensions={0} | all-to-all | bytes 786432 | tf_op jit(solution)/shard_map/all_to_all | solution.py:18
  47.6 10.7 %all_to_all.44.refs_0_ = f32[8,24,256]{2,1,0:T(8,128)S(1)} all-to-all(f32[8,24,256]{2,1,0:T(8,128)S(1)} %get-tuple-element.41), channel_id=1, replica_groups=mesh['zl'=2,'x'=4,'core'=2,'zh'=4,'y'=4] {'zl','zh'}, dimensions={0} | all-to-all | bytes 393216 | tf_op jit(solution)/shard_map/all_to_all | solution.py:18
  58.3 4.9 %collective-permute-start.2 = (f32[16,256]{1,0:T(8,128)S(1)}, f32[16,256]{1,0:T(8,128)S(1)}, u32[]{:S(2)}, u32[]{:S(2)}) collective-permute-start(f32[16,256]{1,0:T(8,128)S(1)} %get-tuple-element.44.refs_2_), channel_id=1, source_target_pairs={{0,16},{16,0},{1,17},{17,1},{2,18},{18,2},{3,19},{19,3},{4,20},{20... | collective-permute-start | bytes 49160 | tf_op jit(solution)/shard_map/ppermute | solution.py:23
  63.2 0.8 collective-permute-done.2.refs_3_
  64.1 12.4 %all_to_all.45.refs_0_ = f32[16,24,256]{2,1,0:T(8,128)S(1)} all-to-all(f32[16,24,256]{2,1,0:T(8,128)S(1)} %get-tuple-element.46), channel_id=1, replica_groups=mesh['zl'=2,'x'=4,'core'=2,'zh'=4,'y'=4] {'x','y'}, dimensions={0} | all-to-all | bytes 786432 | tf_op jit(solution)/shard_map/all_to_all | solution.py:18
  76.6 1.5 %shard_map.74 = (f32[16,24,256]{2,1,0:T(8,128)S(1)}, f32[16,256]{1,0:T(8,128)S(1)}) custom-call(f32[16,24,256]{2,1,0:T(8,128)S(1)} %all_to_all.45.refs_0_, f32[32,256]{1,0:T(8,128)S(1)} %get-tuple-element.47.refs_1_, f32[384,256]{1,0:T(8,128)S(1)} %get-tuple-element.37.refs_2_, f32[384,256]{1,0:T(8,128)S(1)} %get-tuple-element.38.refs_3_), custom_call_target="tpu_custom_call" | custom-call | tf_op jit(solution)/shard_map/pallas_call | solution.py:31
  78.0 11.3 %all_to_all.46.refs_0_ = f32[16,24,256]{2,1,0:T(8,128)S(1)} all-to-all(f32[16,24,256]{2,1,0:T(8,128)S(1)} %get-tuple-element.48), channel_id=1, replica_groups=mesh['zl'=2,'x'=4,'core'=2,'zh'=4,'y'=4] {'x','y'}, dimensions={0} | all-to-all | bytes 786432 | tf_op jit(solution)/shard_map/all_to_all | solution.py:18
  89.3 0.1 shard_map.75
  89.4 9.6 %all_to_all.47.refs_0_ = f32[8,24,128]{2,1,0:T(8,128)S(1)} all-to-all(f32[8,24,128]{2,1,0:T(8,128)S(1)} %shard_map.75), channel_id=1, replica_groups=mesh['zl'=2,'x'=4,'core'=2,'zh'=4,'y'=4] {'zl','zh'}, dimensions={0} | all-to-all | bytes 196608 | tf_op jit(solution)/shard_map/all_to_all | solution.py:18
  99.0 4.3 %collective-permute-start.3 = (f32[24,128]{1,0:T(8,128)S(1)}, f32[24,128]{1,0:T(8,128)S(1)}, u32[]{:S(2)}, u32[]{:S(2)}) collective-permute-start(f32[24,128]{1,0:T(8,128)S(1)} %shard_map.76.refs_1_), channel_id=1, source_target_pairs={{0,16},{16,0},{1,17},{17,1},{2,18},{18,2},{3,19},{19,3},{4,20},{20... | collective-permute-start | bytes 36872 | tf_op jit(solution)/shard_map/ppermute | solution.py:23
  103.4 0.8 collective-permute-done.3.refs_2_
  104.2 0.7 shard_map.77
  (6 shorter events, 0.2 us)
Async XLA Ops:
  1.4 4.1 %collective-permute-start = (f32[40,256]{1,0:T(8,128)S(1)}, f32[40,256]{1,0:T(8,128)S(1)}, u32[]{:S(2)}, u32[]{:S(2)}) collective-permute-start(f32[40,256]{1,0:T(8,128)S(1)} %select_maximum_fusion.refs_0_), channel_id=1, source_target_pairs={{0,16},{16,0},{1,17},{17,1},{2,18},{18,2},{3,19},{19,3},{4,20},{20... | collective-permute-start | bytes 122888 | tf_op jit(solution)/shard_map/ppermute | solution.py:23
  5.5 7.5 %collective-permute-start.1 = (f32[384,512]{1,0:T(8,128)}, f32[384,512]{1,0:T(8,128)S(1)}, u32[]{:S(2)}, u32[]{:S(2)}) collective-permute-start(f32[384,512]{1,0:T(8,128)} %bitcast.3), channel_id=1, source_target_pairs={{0,16},{16,0},{1,17},{17,1},{2,18},{18,2},{3,19},{19,3},{4,20},{20... | collective-permute-start | bytes 2359304 | tf_op jit(solution)/shard_map/ppermute | solution.py:23
  6.6 13.4 %all-to-all-start = ((f32[8,24,128]{2,1,0:T(8,128)}), f32[8,24,128]{2,1,0:T(8,128)S(1)}, u32[]{:S(2)}, u32[]{:S(2)}) async-start(f32[8,24,128]{2,1,0:T(8,128)} %get-tuple-element.29), calls=%async_computation | async-start | bytes 196608 | tf_op jit(solution)/shard_map/all_to_all | solution.py:18
  13.0 1.1 %copy-start = (f32[12,32,512]{2,1,0:T(8,128)S(1)}, f32[12,32,512]{2,1,0:T(8,128)}, u32[]{:S(2)}) copy-start(f32[12,32,512]{2,1,0:T(8,128)} %param.4) | copy-start | bytes 2359300
  58.3 5.8 %collective-permute-start.2 = (f32[16,256]{1,0:T(8,128)S(1)}, f32[16,256]{1,0:T(8,128)S(1)}, u32[]{:S(2)}, u32[]{:S(2)}) collective-permute-start(f32[16,256]{1,0:T(8,128)S(1)} %get-tuple-element.44.refs_2_), channel_id=1, source_target_pairs={{0,16},{16,0},{1,17},{17,1},{2,18},{18,2},{3,19},{19,3},{4,20},{20... | collective-permute-start | bytes 49160 | tf_op jit(solution)/shard_map/ppermute | solution.py:23
  99.0 5.2 %collective-permute-start.3 = (f32[24,128]{1,0:T(8,128)S(1)}, f32[24,128]{1,0:T(8,128)S(1)}, u32[]{:S(2)}, u32[]{:S(2)}) collective-permute-start(f32[24,128]{1,0:T(8,128)S(1)} %shard_map.76.refs_1_), channel_id=1, source_target_pairs={{0,16},{16,0},{1,17},{17,1},{2,18},{18,2},{3,19},{19,3},{4,20},{20... | collective-permute-start | bytes 36872 | tf_op jit(solution)/shard_map/ppermute | solution.py:23

commit v10 on v9

--- a/solution.py
+++ b/solution.py
@@ -120,7 +120,7 @@
 
 
 def gradients(
-    index, got_ref, block_ref, kept_ref, came_ref, out_ref, own_ref, turn, khatri, terms, first
+    index, got_ref, block_ref, kept_ref, came_ref, pieces_ref, deriv_ref, khatri, turn, terms, first
 ):
     x, core, y = index[1], index[2], index[4]
     order = [i + 16 * core if i < 12 else i + 4 - 16 * core for i in range(24)]
@@ -145,9 +145,10 @@
     parts = split(khatri[...])
     model = product(parts, turned_c, ((1,), (0,)))
     target = jnp.concatenate([kept_ref[...], came_ref[...]], axis=0)
-    deriv = split(jax.nn.sigmoid(model) - target)
+    deriv = jax.nn.sigmoid(model) - target
+    deriv_ref[...] = deriv
+    deriv = split(deriv)
     terms[...] = product(deriv, c, ((1,), (0,)))
-    grad_c = product(deriv, parts, ((0,), (0,)))
     grad_b = jnp.zeros((32, 256), F32)
     turn[...] = jnp.zeros((128, 128), F32)
     for i in range(24):
@@ -157,25 +158,39 @@
         turn[pl.ds(order[i], 1), :] = row[:, 0:128]
         turn[pl.ds(order[i] + 64, 1), :] = row[:, 128:256]
     turned = turn[...].T
-    pieces_a = [
-        turned[16 * q : 16 * q + 16] + pltpu.roll(turned[64 + 16 * q : 80 + 16 * q], 32, 1)
-        for q in range(4)
-    ]
+    for q in range(4):
+        pieces_ref[16 * q : 16 * q + 16, 0:128] = turned[16 * q : 16 * q + 16] + pltpu.roll(
+            turned[64 + 16 * q : 80 + 16 * q], 32, 1
+        )
     turn[...] = jnp.zeros((128, 128), F32)
     turn[0:32, :] = grad_b[:, 0:128]
     turn[32:64, :] = grad_b[:, 128:256]
     turned = turn[...].T
-    pieces_b = [
-        turned[32 * q : 32 * q + 16] + pltpu.roll(turned[32 * q + 16 : 32 * q + 32], 64, 1)
-        for q in range(4)
+    for q in range(4):
+        pieces_ref[16 * q : 16 * q + 16, 128:256] = turned[32 * q : 32 * q + 16] + pltpu.roll(
+            turned[32 * q + 16 : 32 * q + 32], 64, 1
+        )
+
+
+def third_gradient(index, deriv_ref, khatri_ref, out_ref):
+    del index
+    out_ref[...] = product(split(deriv_ref[...]), split(khatri_ref[...]), ((0,), (0,)))
+
+
+def gradients_pack(index, pieces_ref, other_ref, c_ref, out_ref, own_ref):
+    x, y = index[1], index[4]
+    pieces = [
+        pieces_ref[16 * q : 16 * q + 16, :] + other_ref[16 * q : 16 * q + 16, :] for q in range(4)
     ]
-    out_ref[:, 0:16, :] = grad_c.reshape(16, 16, 256)
+    out_ref[:, 0:16, :] = c_ref[...].reshape(16, 16, 256)
     for p in range(16):
-        fill_slot(out_ref, p, jnp.where(x == p // 4, pieces_a[p % 4], pieces_b[p // 4]))
-    own_a, own_b = pieces_a[0], pieces_b[0]
+        fill_slot(
+            out_ref, p, jnp.where(x == p // 4, pieces[p % 4][:, 0:128], pieces[p // 4][:, 128:256])
+        )
+    own_a, own_b = pieces[0][:, 0:128], pieces[0][:, 128:256]
     for q in range(1, 4):
-        own_a = jnp.where(y == q, pieces_a[q], own_a)
-        own_b = jnp.where(x == q, pieces_b[q], own_b)
+        own_a = jnp.where(y == q, pieces[q][:, 0:128], own_a)
+        own_b = jnp.where(x == q, pieces[q][:, 128:256], own_b)
     own_ref[:, 0:128] = own_a
     own_ref[:, 128:256] = own_b
 
@@ -199,22 +214,17 @@
     sum_ref[:, 128:256] = b
 
 
-def middle_sum(index, got_ref, own_ref, c_ref, ab_ref):
+def middle_update(rates, index, got_ref, own_ref, block_ref, slip_ref, block_out, out_ref, new):
     zl, zh = index[0], index[3]
-    c_ref[...] = jnp.sum(got_ref[:, 0:16, :], axis=0)
+    rate_a, rate_b, rate_c = rates
+    c = jnp.sum(got_ref[:, 0:16, :], axis=0)
     a = own_ref[:, 0:128]
     for q in range(4):
         a = a + jnp.where(zh == q, 0.0, slot(got_ref, zl * 4 + q))
-    ab_ref[:, 0:128] = a
-    ab_ref[:, 128:256] = own_ref[:, 128:256] + slot(got_ref, (1 - zl) * 4 + zh)
-
-
-def middle_update(rates, index, block_ref, c_ref, ab_ref, other_ref, slip_ref, block_out, out_ref, new):
-    rate_a, rate_b, rate_c = rates
-    ab = ab_ref[...] + other_ref[...]
-    new[0:16, :] = block_ref[0:16, :] - rate_c * c_ref[...]
-    new[16:32, 0:128] = block_ref[16:32, 0:128] - rate_a * ab[:, 0:128]
-    new[16:32, 128:256] = block_ref[16:32, 128:256] - rate_b * ab[:, 128:256]
+    b = own_ref[:, 128:256] + slot(got_ref, (1 - zl) * 4 + zh)
+    new[0:16, :] = block_ref[0:16, :] - rate_c * c
+    new[16:32, 0:128] = block_ref[16:32, 0:128] - rate_a * a
+    new[16:32, 128:256] = block_ref[16:32, 128:256] - rate_b * b
     block = new[...]
     block_out[...] = block
     send_block(block, out_ref, index[1])
@@ -245,27 +255,20 @@
         out_ref[p, 8:24, :] = ab_p
 
 
-def last_sum(index, got_ref, slip_ref):
-    zl, zh = index[0], index[3]
+def last_update(rates, index, old_ref, got_ref, a_ref, bt_ref, c_ref, pad):
+    zl, core, zh = index[0], index[2], index[3]
+    rate_a, rate_b, rate_c = rates
     c = got_ref[0, 0:8, :]
     for p in range(1, 8):
         c = c + got_ref[p, 0:8, :]
+    c = old_ref[0:8, :] - rate_c * c
+    c_ref[:, 0:128] = c[0:2, :]
+    c_ref[:, 128:256] = c[2:4, :]
     a = got_ref[zl * 4, 8:24, :]
     for q in range(1, 4):
         a = a + got_ref[zl * 4 + q, 8:24, :]
     b = got_ref[zh, 8:24, :] + got_ref[4 + zh, 8:24, :]
-    slip_ref[0:8, :] = c
-    slip_ref[8:24, :] = jnp.where(lanes() < 32, a, b)
-
-
-def last_update(rates, index, old_ref, grad_ref, other_ref, a_ref, bt_ref, c_ref, pad):
-    rate_a, rate_b, rate_c = rates
-    core = index[2]
-    c = old_ref[0:8, :] - rate_c * grad_ref[0:8, :]
-    c_ref[:, 0:128] = c[0:2, :]
-    c_ref[:, 128:256] = c[2:4, :]
-    rate = jnp.where(lanes() < 32, rate_a, rate_b)
-    ab = old_ref[8:24, :] - rate * (grad_ref[8:24, :] + other_ref[8:24, :])
+    ab = old_ref[8:24, :] - jnp.where(lanes() < 32, rate_a * a, rate_b * b)
     b = jnp.where(core == 0, pltpu.roll(ab, 96, 1), pltpu.roll(ab, 32, 1))
     bt_ref[...] = b[:, 0:32]
     pad[...] = jnp.zeros((128, 128), F32)
@@ -313,32 +316,33 @@
     targets = call(arrange, [(384, 256), (384, 256)], [], done, flat, flat_other)
     got, targets = lax.optimization_barrier((exchange(send, Z), targets))
     block, send = call(block_from_slips, [(32, 256), wide], [], got)
-    step = functools.partial(
-        call, gradients, [wide, pair], [square, (768, 256), (768, 256), (32, 256)]
-    )
-
-    send, own = step(exchange(send, XY), block, *targets)
+    tall = (768, 256)
+
+    def step(got, block):
+        pieces, deriv, khatri = call(
+            gradients, [(64, 256), tall, tall], [square, tall, (32, 256)], got, block, *targets
+        )
+        (grad_c,) = call(third_gradient, [(256, 256)], [], deriv, khatri)
+        return call(gradients_pack, [wide, pair], [], pieces, swap(pieces), grad_c)
+
+    send, own = step(exchange(send, XY), block)
     send, own = call(middle_pack, [(8, 24, 256), pair], [], exchange(send, XY), own)
-    grad_c, grad_ab = call(middle_sum, [pair, pair], [], exchange(send, Z), own)
     slip, block, send = call(
         functools.partial(middle_update, rates),
         [(24, 128), (32, 256), wide],
         [(32, 256)],
+        exchange(send, Z),
+        own,
         block,
-        grad_c,
-        grad_ab,
-        swap(grad_ab),
-    )
-    send, own = step(exchange(send, XY), block, *targets)
+    )
+    send, own = step(exchange(send, XY), block)
     (send,) = call(last_pack, [(8, 24, 128)], [(32, 256)], exchange(send, XY), own)
-    (grad,) = call(last_sum, [(24, 128)], [], exchange(send, Z))
     new_a, new_bt, new_c = call(
         functools.partial(last_update, rates),
         [(n_i, 16), (16, n_j), third_factor.shape],
         [square],
         slip,
-        grad,
-        swap(grad),
+        exchange(send, Z),
     )
     return (new_a, new_bt.T, new_c)
 

time: 105 us -> 105 us (level)
  starting transfers between devices: 19.3 us -> 16.9 us
  Pallas kernels: 5.53 us -> 7.06 us
    ppermute x4, starting transfers between devices: 12.8 us -> 10.5 us  [swap(): return lax.ppermute(value, 'core', [(0, 1), (1, 0)])]
    pallas_call x11 -> x13, Pallas kernels: 5.53 us -> 7.06 us  [call(): pl.pallas_call(kernel, out_shape=[jax.ShapeDtypeStruct(s, F32) for s in o...]
  transfers between devices with their start and end apart: 5 -> 5, of which waited for: 4 -> 4; matrix products, arithmetic and copies ran while one was open for 0% -> 0% of each run, Pallas kernels for 1% -> 2%
where the time goes in v10:
time: 105 us; the launch traced here: 104 us
  blocking collectives  70.9 us (68%)
  starting transfers between devices  16.9 us (16%)
  Pallas kernels  7.06 us (7%)
  waiting for transfers between devices  6.59 us (6%)
  local copies, waits for them, and re-layouts  1.13 us (1%)
    all_to_all x6, blocking collectives, exchange(): got = lax.all_to_all(parts.reshape(-1, shape[2]), axis, 0, 0, tiled=True)  70.9 us
    ppermute x4, starting transfers between devices, swap(): return lax.ppermute(value, 'core', [(0, 1), (1, 0)])  10.5 us
    pallas_call x13, Pallas kernels, call(): pl.pallas_call(kernel, out_shape=[jax.ShapeDtypeStruct(s, F32) for s in o...  7.06 us
    all_to_all x1, starting transfers between devices, exchange(): got = lax.all_to_all(parts.reshape(-1, shape[2]), axis, 0, 0, tiled=True)  6.45 us
    all_to_all x1, waiting for transfers between devices, exchange(): got = lax.all_to_all(parts.reshape(-1, shape[2]), axis, 0, 0, tiled=True)  4.97 us
  transfers between devices with their start and end apart: 5, of which 4 were waited for; matrix products, arithmetic and copies ran while one was open for 0% of the time, Pallas kernels for 2%

profile of v10, /device:TPU:1, one launch (start us, length us, event | category | flops | bytes accessed | tf_op | source)
XLA Modules:
  0.0 104.1 jit_solution(4959540954884586897)
XLA Ops:
  0.6 0.7 select_maximum_fusion.refs_0_
  1.4 3.2 %collective-permute-start = (f32[40,256]{1,0:T(8,128)S(1)}, f32[40,256]{1,0:T(8,128)S(1)}, u32[]{:S(2)}, u32[]{:S(2)}) collective-permute-start(f32[40,256]{1,0:T(8,128)S(1)} %select_maximum_fusion.refs_0_), channel_id=1, source_target_pairs={{0,16},{16,0},{1,17},{17,1},{2,18},{18,2},{3,19},{19,3},{4,20},{20... | collective-permute-start | bytes 122888 | tf_op jit(solution)/shard_map/ppermute | solution.py:23
  4.6 0.9 collective-permute-done.refs_1_
  5.5 0.3 collective-permute-start.1
  5.8 0.7 shard_map.67
  6.6 6.4 %all-to-all-start = ((f32[8,24,128]{2,1,0:T(8,128)}), f32[8,24,128]{2,1,0:T(8,128)S(1)}, u32[]{:S(2)}, u32[]{:S(2)}) async-start(f32[8,24,128]{2,1,0:T(8,128)} %get-tuple-element.33), calls=%async_computation | async-start | bytes 196608 | tf_op jit(solution)/shard_map/all_to_all | solution.py:18
  13.0 1.1 %copy-done = f32[12,32,512]{2,1,0:T(8,128)S(1)} copy-done((f32[12,32,512]{2,1,0:T(8,128)S(1)}, f32[12,32,512]{2,1,0:T(8,128)}, u32[]{:S(2)}) %copy-start) | copy-done | bytes 786456
  14.2 0.8 shard_map.68
  15.0 5.0 %all-to-all-done.refs_0_ = f32[8,24,128]{2,1,0:T(8,128)S(1)} async-done(((f32[8,24,128]{2,1,0:T(8,128)}), f32[8,24,128]{2,1,0:T(8,128)S(1)}, u32[]{:S(2)}, u32[]{:S(2)}) %all-to-all-start) | async-done | bytes 98336 | tf_op jit(solution)/shard_map/all_to_all | solution.py:18
  20.0 14.7 %all_to_all.42.refs_0_ = f32[16,24,256]{2,1,0:T(8,128)S(1)} all-to-all(f32[16,24,256]{2,1,0:T(8,128)S(1)} %get-tuple-element.39), channel_id=1, replica_groups=mesh['zl'=2,'x'=4,'core'=2,'zh'=4,'y'=4] {'x','y'}, dimensions={0} | all-to-all | bytes 786432 | tf_op jit(solution)/shard_map/all_to_all | solution.py:18
  34.7 1.7 %shard_map.70 = (f32[64,256]{1,0:T(8,128)S(1)}, f32[768,256]{1,0:T(8,128)S(1)}, f32[768,256]{1,0:T(8,128)S(1)}) custom-call(f32[16,24,256]{2,1,0:T(8,128)S(1)} %all_to_all.42.refs_0_, f32[32,256]{1,0:T(8,128)S(1)} %get-tuple-element.40.refs_1_.refs_2_, f32[384,256]{1,0:T(8,128)S(1)} %get-tuple-element.41.refs_2_, f32[384,256]{1,0:T(8,128)S(1)} %get-tuple-element.42.refs_3_), custom_call_target="tpu_custom_call" | custom-call | tf_op jit(solution)/shard_map/pallas_call | solution.py:31
  36.4 2.8 %collective-permute-start.2 = (f32[64,256]{1,0:T(8,128)S(1)}, f32[64,256]{1,0:T(8,128)S(1)}, u32[]{:S(2)}, u32[]{:S(2)}) collective-permute-start(f32[64,256]{1,0:T(8,128)S(1)} %get-tuple-element.43.refs_0_), channel_id=1, source_target_pairs={{0,16},{16,0},{1,17},{17,1},{2,18},{18,2},{3,19},{19,3},{4,20},{20... | collective-permute-start | bytes 196616 | tf_op jit(solution)/shard_map/ppermute | solution.py:23
  39.2 0.5 shard_map.71.refs_2_
  39.7 0.4 collective-permute-done.2.refs_1_
  40.1 12.5 %all_to_all.43.refs_0_ = f32[16,24,256]{2,1,0:T(8,128)S(1)} all-to-all(f32[16,24,256]{2,1,0:T(8,128)S(1)} %get-tuple-element.46), channel_id=1, replica_groups=mesh['zl'=2,'x'=4,'core'=2,'zh'=4,'y'=4] {'x','y'}, dimensions={0} | all-to-all | bytes 786432 | tf_op jit(solution)/shard_map/all_to_all | solution.py:18
  52.6 10.2 %all_to_all.44.refs_0_ = f32[8,24,256]{2,1,0:T(8,128)S(1)} all-to-all(f32[8,24,256]{2,1,0:T(8,128)S(1)} %get-tuple-element.48), channel_id=1, replica_groups=mesh['zl'=2,'x'=4,'core'=2,'zh'=4,'y'=4] {'zl','zh'}, dimensions={0} | all-to-all | bytes 393216 | tf_op jit(solution)/shard_map/all_to_all | solution.py:18
  62.9 11.3 %all_to_all.45.refs_0_ = f32[16,24,256]{2,1,0:T(8,128)S(1)} all-to-all(f32[16,24,256]{2,1,0:T(8,128)S(1)} %get-tuple-element.51), channel_id=1, replica_groups=mesh['zl'=2,'x'=4,'core'=2,'zh'=4,'y'=4] {'x','y'}, dimensions={0} | all-to-all | bytes 786432 | tf_op jit(solution)/shard_map/all_to_all | solution.py:18
  74.2 1.7 %shard_map.75 = (f32[64,256]{1,0:T(8,128)S(1)}, f32[768,256]{1,0:T(8,128)S(1)}, f32[768,256]{1,0:T(8,128)S(1)}) custom-call(f32[16,24,256]{2,1,0:T(8,128)S(1)} %all_to_all.45.refs_0_, f32[32,256]{1,0:T(8,128)S(1)} %get-tuple-element.52.refs_1_, f32[384,256]{1,0:T(8,128)S(1)} %get-tuple-element.41.refs_2_, f32[384,256]{1,0:T(8,128)S(1)} %get-tuple-element.42.refs_3_), custom_call_target="tpu_custom_call" | custom-call | tf_op jit(solution)/shard_map/pallas_call | solution.py:31
  75.9 4.1 %collective-permute-start.3 = (f32[64,256]{1,0:T(8,128)S(1)}, f32[64,256]{1,0:T(8,128)S(1)}, u32[]{:S(2)}, u32[]{:S(2)}) collective-permute-start(f32[64,256]{1,0:T(8,128)S(1)} %get-tuple-element.53.refs_0_), channel_id=1, source_target_pairs={{0,16},{16,0},{1,17},{17,1},{2,18},{18,2},{3,19},{19,3},{4,20},{20... | collective-permute-start | bytes 196616 | tf_op jit(solution)/shard_map/ppermute | solution.py:23
  80.0 0.5 shard_map.76.refs_2_
  80.6 0.4 collective-permute-done.3.refs_1_
  81.0 12.5 %all_to_all.46.refs_0_ = f32[16,24,256]{2,1,0:T(8,128)S(1)} all-to-all(f32[16,24,256]{2,1,0:T(8,128)S(1)} %get-tuple-element.56), channel_id=1, replica_groups=mesh['zl'=2,'x'=4,'core'=2,'zh'=4,'y'=4] {'x','y'}, dimensions={0} | all-to-all | bytes 786432 | tf_op jit(solution)/shard_map/all_to_all | solution.py:18
  93.5 9.8 %all_to_all.47.refs_1_ = f32[8,24,128]{2,1,0:T(8,128)S(1)} all-to-all(f32[8,24,128]{2,1,0:T(8,128)S(1)} %shard_map.78), channel_id=1, replica_groups=mesh['zl'=2,'x'=4,'core'=2,'zh'=4,'y'=4] {'zl','zh'}, dimensions={0} | all-to-all | bytes 196608 | tf_op jit(solution)/shard_map/all_to_all | solution.py:18
  103.3 0.8 shard_map.79
  (8 shorter events, 0.4 us)
Async XLA Ops:
  1.4 4.1 %collective-permute-start = (f32[40,256]{1,0:T(8,128)S(1)}, f32[40,256]{1,0:T(8,128)S(1)}, u32[]{:S(2)}, u32[]{:S(2)}) collective-permute-start(f32[40,256]{1,0:T(8,128)S(1)} %select_maximum_fusion.refs_0_), channel_id=1, source_target_pairs={{0,16},{16,0},{1,17},{17,1},{2,18},{18,2},{3,19},{19,3},{4,20},{20... | collective-permute-start | bytes 122888 | tf_op jit(solution)/shard_map/ppermute | solution.py:23
  5.5 7.5 %collective-permute-start.1 = (f32[384,512]{1,0:T(8,128)}, f32[384,512]{1,0:T(8,128)S(1)}, u32[]{:S(2)}, u32[]{:S(2)}) collective-permute-start(f32[384,512]{1,0:T(8,128)} %bitcast.3), channel_id=1, source_target_pairs={{0,16},{16,0},{1,17},{17,1},{2,18},{18,2},{3,19},{19,3},{4,20},{20... | collective-permute-start | bytes 2359304 | tf_op jit(solution)/shard_map/ppermute | solution.py:23
  6.6 13.4 %all-to-all-start = ((f32[8,24,128]{2,1,0:T(8,128)}), f32[8,24,128]{2,1,0:T(8,128)S(1)}, u32[]{:S(2)}, u32[]{:S(2)}) async-start(f32[8,24,128]{2,1,0:T(8,128)} %get-tuple-element.33), calls=%async_computation | async-start | bytes 196608 | tf_op jit(solution)/shard_map/all_to_all | solution.py:18
  13.0 1.1 %copy-start = (f32[12,32,512]{2,1,0:T(8,128)S(1)}, f32[12,32,512]{2,1,0:T(8,128)}, u32[]{:S(2)}) copy-start(f32[12,32,512]{2,1,0:T(8,128)} %param.4) | copy-start | bytes 2359300
  36.4 3.7 %collective-permute-start.2 = (f32[64,256]{1,0:T(8,128)S(1)}, f32[64,256]{1,0:T(8,128)S(1)}, u32[]{:S(2)}, u32[]{:S(2)}) collective-permute-start(f32[64,256]{1,0:T(8,128)S(1)} %get-tuple-element.43.refs_0_), channel_id=1, source_target_pairs={{0,16},{16,0},{1,17},{17,1},{2,18},{18,2},{3,19},{19,3},{4,20},{20... | collective-permute-start | bytes 196616 | tf_op jit(solution)/shard_map/ppermute | solution.py:23
  75.9 5.0 %collective-permute-start.3 = (f32[64,256]{1,0:T(8,128)S(1)}, f32[64,256]{1,0:T(8,128)S(1)}, u32[]{:S(2)}, u32[]{:S(2)}) collective-permute-start(f32[64,256]{1,0:T(8,128)S(1)} %get-tuple-element.53.refs_0_), channel_id=1, source_target_pairs={{0,16},{16,0},{1,17},{17,1},{2,18},{18,2},{3,19},{19,3},{4,20},{20... | collective-permute-start | bytes 196616 | tf_op jit(solution)/shard_map/ppermute | solution.py:23

commit v11 on v9

--- a/solution.py
+++ b/solution.py
@@ -8,7 +8,7 @@
 from jax.sharding import Mesh, PartitionSpec as P
 
 XY = ("x", "y")
-Z = ("zl", "zh")
+Z = ("zh", "zl")
 HIGH = lax.Precision.HIGHEST
 F32 = jnp.float32
 
@@ -109,11 +109,11 @@
     at = lanes()
     a = jnp.zeros((16, 128), F32)
     for q in range(4):
-        v = jnp.where(at < 32, got_ref[zl * 4 + q, 8:24, :], 0.0)
+        v = jnp.where(at < 32, got_ref[2 * q + zl, 8:24, :], 0.0)
         a = a + (pltpu.roll(v, 32 * q, 1) if q else v)
     second = (at // 32) % 2 == 1
-    low = jnp.where(second, got_ref[zh, 8:24, :], 0.0)
-    high = jnp.where(second, got_ref[4 + zh, 8:24, :], 0.0)
+    low = jnp.where(second, got_ref[2 * zh, 8:24, :], 0.0)
+    high = jnp.where(second, got_ref[2 * zh + 1, 8:24, :], 0.0)
     block_ref[16:32, 0:128] = a
     block_ref[16:32, 128:256] = pltpu.roll(low, 96, 1) + high
     send_block(block_ref[...], out_ref, index[1])
@@ -194,7 +194,7 @@
     c, a, b = sum_xy(index, got_ref, own_ref)
     for p in range(8):
         out_ref[p, 0:16, :] = c
-        fill_slot(out_ref, p, jnp.where(index[0] == p // 4, a, b))
+        fill_slot(out_ref, p, jnp.where(index[0] == p % 2, a, b))
     sum_ref[:, 0:128] = a
     sum_ref[:, 128:256] = b
 
@@ -204,9 +204,9 @@
     c_ref[...] = jnp.sum(got_ref[:, 0:16, :], axis=0)
     a = own_ref[:, 0:128]
     for q in range(4):
-        a = a + jnp.where(zh == q, 0.0, slot(got_ref, zl * 4 + q))
+        a = a + jnp.where(zh == q, 0.0, slot(got_ref, 2 * q + zl))
     ab_ref[:, 0:128] = a
-    ab_ref[:, 128:256] = own_ref[:, 128:256] + slot(got_ref, (1 - zl) * 4 + zh)
+    ab_ref[:, 128:256] = own_ref[:, 128:256] + slot(got_ref, 2 * zh + 1 - zl)
 
 
 def middle_update(rates, index, block_ref, c_ref, ab_ref, other_ref, slip_ref, block_out, out_ref, new):
@@ -218,11 +218,11 @@
     block = new[...]
     block_out[...] = block
     send_block(block, out_ref, index[1])
-    own = index[0] * 4 + index[3]
+    own = index[3] * 2 + index[0]
     c = jnp.zeros((2, 256), F32)
     ab = jnp.zeros((16, 128), F32)
     for p in range(8):
-        c_p, ab_p = slip_of(block, p, p // 4, p % 4)
+        c_p, ab_p = slip_of(block, p, p % 2, p // 2)
         c = jnp.where(own == p, c_p, c)
         ab = jnp.where(own == p, ab_p, ab)
     slip_ref[0:8, :] = jnp.zeros((8, 128), F32)
@@ -238,7 +238,7 @@
     new[16:32, 128:256] = b
     block = new[...]
     for p in range(8):
-        c_p, ab_p = slip_of(block, p, p // 4, p % 4)
+        c_p, ab_p = slip_of(block, p, p % 2, p // 2)
         out_ref[p, 0:8, :] = jnp.zeros((8, 128), F32)
         out_ref[p, 0:2, :] = c_p[:, 0:128]
         out_ref[p, 2:4, :] = c_p[:, 128:256]
@@ -250,10 +250,10 @@
     c = got_ref[0, 0:8, :]
     for p in range(1, 8):
         c = c + got_ref[p, 0:8, :]
-    a = got_ref[zl * 4, 8:24, :]
+    a = got_ref[zl, 8:24, :]
     for q in range(1, 4):
-        a = a + got_ref[zl * 4 + q, 8:24, :]
-    b = got_ref[zh, 8:24, :] + got_ref[4 + zh, 8:24, :]
+        a = a + got_ref[2 * q + zl, 8:24, :]
+    b = got_ref[2 * zh, 8:24, :] + got_ref[2 * zh + 1, 8:24, :]
     slip_ref[0:8, :] = c
     slip_ref[8:24, :] = jnp.where(lanes() < 32, a, b)
 
@@ -278,7 +278,7 @@
     del after_ref
     spot = lax.broadcasted_iota(jnp.int32, (512, 256), 1)
     xs, ys = spot // 64, (spot // 16) % 4
-    zls, zhs, us = (spot // 8) % 2, (spot // 2) % 4, spot % 2
+    zhs, zls, us = (spot // 4) % 4, (spot // 2) % 2, spot % 2
     source = zls * 256 + xs * 64 + index[2] * 32 + zhs * 8 + ys * 2 + us
     here = lax.broadcasted_iota(jnp.int32, (512, 256), 0)
     pick = jnp.where(here == source, 1.0, 0.0).astype(jnp.bfloat16)

time: 105 us -> 107 us (1.019)
  no operation moved by 1% of the time
where the time goes in v11:
time: 107 us
  blocking collectives  71 us (66%)
  starting transfers between devices  19.6 us (18%)
  waiting for transfers between devices  8.07 us (8%)
  Pallas kernels  5.54 us (5%)
  local copies, waits for them, and re-layouts  1.13 us (1%)
    all_to_all x6, blocking collectives, exchange(): got = lax.all_to_all(parts.reshape(-1, shape[2]), axis, 0, 0, tiled=True)  71 us
    ppermute x4, starting transfers between devices, swap(): return lax.ppermute(value, 'core', [(0, 1), (1, 0)])  13.1 us
    all_to_all x1, starting transfers between devices, exchange(): got = lax.all_to_all(parts.reshape(-1, shape[2]), axis, 0, 0, tiled=True)  6.45 us
    pallas_call x11, Pallas kernels, call(): pl.pallas_call(kernel, out_shape=[jax.ShapeDtypeStruct(s, F32) for s in o...  5.54 us
    all_to_all x1, waiting for transfers between devices, exchange(): got = lax.all_to_all(parts.reshape(-1, shape[2]), axis, 0, 0, tiled=True)  5.53 us
    ppermute x4, waiting for transfers between devices, swap(): return lax.ppermute(value, 'core', [(0, 1), (1, 0)])  2.55 us
  transfers between devices with their start and end apart: 5, of which 4 were waited for; matrix products, arithmetic and copies ran while one was open for 0% of the time, Pallas kernels for 1%

profile of v11, /device:TPU:1, one launch (start us, length us, event | category | flops | bytes accessed | tf_op | source)
XLA Modules:
  0.0 106.7 jit_solution(5741747207683638991)
XLA Ops:
  0.6 0.7 select_maximum_fusion.refs_0_
  1.4 3.2 %collective-permute-start = (f32[40,256]{1,0:T(8,128)S(1)}, f32[40,256]{1,0:T(8,128)S(1)}, u32[]{:S(2)}, u32[]{:S(2)}) collective-permute-start(f32[40,256]{1,0:T(8,128)S(1)} %select_maximum_fusion.refs_0_), channel_id=1, source_target_pairs={{0,16},{16,0},{1,17},{17,1},{2,18},{18,2},{3,19},{19,3},{4,20},{20... | collective-permute-start | bytes 122888 | tf_op jit(solution)/shard_map/ppermute | solution.py:23
  4.6 0.9 collective-permute-done.refs_1_
  5.5 0.3 collective-permute-start.1
  5.8 0.7 shard_map.67
  6.6 6.4 %all-to-all-start = ((f32[8,24,128]{2,1,0:T(8,128)}), f32[8,24,128]{2,1,0:T(8,128)S(1)}, u32[]{:S(2)}, u32[]{:S(2)}) async-start(f32[8,24,128]{2,1,0:T(8,128)} %get-tuple-element.29), calls=%async_computation | async-start | bytes 196608 | tf_op jit(solution)/shard_map/all_to_all | solution.py:18
  13.0 1.1 %copy-done = f32[12,32,512]{2,1,0:T(8,128)S(1)} copy-done((f32[12,32,512]{2,1,0:T(8,128)S(1)}, f32[12,32,512]{2,1,0:T(8,128)}, u32[]{:S(2)}) %copy-start) | copy-done | bytes 786456
  14.2 0.8 shard_map.68
  15.0 5.5 %all-to-all-done.refs_0_ = f32[8,24,128]{2,1,0:T(8,128)S(1)} async-done(((f32[8,24,128]{2,1,0:T(8,128)}), f32[8,24,128]{2,1,0:T(8,128)S(1)}, u32[]{:S(2)}, u32[]{:S(2)}) %all-to-all-start) | async-done | bytes 98336 | tf_op jit(solution)/shard_map/all_to_all | solution.py:18
  20.5 0.1 shard_map.69
  20.6 14.5 %all_to_all.42.refs_0_ = f32[16,24,256]{2,1,0:T(8,128)S(1)} all-to-all(f32[16,24,256]{2,1,0:T(8,128)S(1)} %get-tuple-element.36), channel_id=1, replica_groups=mesh['zl'=2,'x'=4,'core'=2,'zh'=4,'y'=4] {'x','y'}, dimensions={0} | all-to-all | bytes 786432 | tf_op jit(solution)/shard_map/all_to_all | solution.py:18
  35.1 1.5 %shard_map.70 = (f32[16,24,256]{2,1,0:T(8,128)S(1)}, f32[16,256]{1,0:T(8,128)S(1)}) custom-call(f32[16,24,256]{2,1,0:T(8,128)S(1)} %all_to_all.42.refs_0_, f32[32,256]{1,0:T(8,128)S(1)} %get-tuple-element.35.refs_1_.refs_0_, f32[384,256]{1,0:T(8,128)S(1)} %get-tuple-element.37.refs_2_, f32[384,256]{1,0:T(8,128)S(1)} %get-tuple-element.38.refs_3_), custom_call_target="tpu_custom_call" | custom-call | tf_op jit(solution)/shard_map/pallas_call | solution.py:31
  36.6 11.6 %all_to_all.43.refs_0_ = f32[16,24,256]{2,1,0:T(8,128)S(1)} all-to-all(f32[16,24,256]{2,1,0:T(8,128)S(1)} %get-tuple-element.39), channel_id=1, replica_groups=mesh['zl'=2,'x'=4,'core'=2,'zh'=4,'y'=4] {'x','y'}, dimensions={0} | all-to-all | bytes 786432 | tf_op jit(solution)/shard_map/all_to_all | solution.py:18
  48.3 11.0 %all_to_all.44.refs_0_ = f32[8,24,256]{2,1,0:T(8,128)S(1)} all-to-all(f32[8,24,256]{2,1,0:T(8,128)S(1)} %get-tuple-element.41), channel_id=1, replica_groups=mesh['zl'=2,'x'=4,'core'=2,'zh'=4,'y'=4] {'zh','zl'}, dimensions={0} | all-to-all | bytes 393216 | tf_op jit(solution)/shard_map/all_to_all | solution.py:18
  59.3 5.5 %collective-permute-start.2 = (f32[16,256]{1,0:T(8,128)S(1)}, f32[16,256]{1,0:T(8,128)S(1)}, u32[]{:S(2)}, u32[]{:S(2)}) collective-permute-start(f32[16,256]{1,0:T(8,128)S(1)} %get-tuple-element.44.refs_2_), channel_id=1, source_target_pairs={{0,16},{16,0},{1,17},{17,1},{2,18},{18,2},{3,19},{19,3},{4,20},{20... | collective-permute-start | bytes 49160 | tf_op jit(solution)/shard_map/ppermute | solution.py:23
  64.8 0.8 collective-permute-done.2.refs_3_
  65.8 12.5 %all_to_all.45.refs_0_ = f32[16,24,256]{2,1,0:T(8,128)S(1)} all-to-all(f32[16,24,256]{2,1,0:T(8,128)S(1)} %get-tuple-element.46), channel_id=1, replica_groups=mesh['zl'=2,'x'=4,'core'=2,'zh'=4,'y'=4] {'x','y'}, dimensions={0} | all-to-all | bytes 786432 | tf_op jit(solution)/shard_map/all_to_all | solution.py:18
  78.2 1.5 %shard_map.74 = (f32[16,24,256]{2,1,0:T(8,128)S(1)}, f32[16,256]{1,0:T(8,128)S(1)}) custom-call(f32[16,24,256]{2,1,0:T(8,128)S(1)} %all_to_all.45.refs_0_, f32[32,256]{1,0:T(8,128)S(1)} %get-tuple-element.47.refs_1_, f32[384,256]{1,0:T(8,128)S(1)} %get-tuple-element.37.refs_2_, f32[384,256]{1,0:T(8,128)S(1)} %get-tuple-element.38.refs_3_), custom_call_target="tpu_custom_call" | custom-call | tf_op jit(solution)/shard_map/pallas_call | solution.py:31
  79.7 11.3 %all_to_all.46.refs_0_ = f32[16,24,256]{2,1,0:T(8,128)S(1)} all-to-all(f32[16,24,256]{2,1,0:T(8,128)S(1)} %get-tuple-element.48), channel_id=1, replica_groups=mesh['zl'=2,'x'=4,'core'=2,'zh'=4,'y'=4] {'x','y'}, dimensions={0} | all-to-all | bytes 786432 | tf_op jit(solution)/shard_map/all_to_all | solution.py:18
  91.0 0.1 shard_map.75
  91.1 10.0 %all_to_all.47.refs_0_ = f32[8,24,128]{2,1,0:T(8,128)S(1)} all-to-all(f32[8,24,128]{2,1,0:T(8,128)S(1)} %shard_map.75), channel_id=1, replica_groups=mesh['zl'=2,'x'=4,'core'=2,'zh'=4,'y'=4] {'zh','zl'}, dimensions={0} | all-to-all | bytes 196608 | tf_op jit(solution)/shard_map/all_to_all | solution.py:18
  101.1 4.0 %collective-permute-start.3 = (f32[24,128]{1,0:T(8,128)S(1)}, f32[24,128]{1,0:T(8,128)S(1)}, u32[]{:S(2)}, u32[]{:S(2)}) collective-permute-start(f32[24,128]{1,0:T(8,128)S(1)} %shard_map.76.refs_1_), channel_id=1, source_target_pairs={{0,16},{16,0},{1,17},{17,1},{2,18},{18,2},{3,19},{19,3},{4,20},{20... | collective-permute-start | bytes 36872 | tf_op jit(solution)/shard_map/ppermute | solution.py:23
  105.2 0.8 collective-permute-done.3.refs_2_
  106.0 0.7 shard_map.77
  (6 shorter events, 0.2 us)
Async XLA Ops:
  1.4 4.1 %collective-permute-start = (f32[40,256]{1,0:T(8,128)S(1)}, f32[40,256]{1,0:T(8,128)S(1)}, u32[]{:S(2)}, u32[]{:S(2)}) collective-permute-start(f32[40,256]{1,0:T(8,128)S(1)} %select_maximum_fusion.refs_0_), channel_id=1, source_target_pairs={{0,16},{16,0},{1,17},{17,1},{2,18},{18,2},{3,19},{19,3},{4,20},{20... | collective-permute-start | bytes 122888 | tf_op jit(solution)/shard_map/ppermute | solution.py:23
  5.5 7.5 %collective-permute-start.1 = (f32[384,512]{1,0:T(8,128)}, f32[384,512]{1,0:T(8,128)S(1)}, u32[]{:S(2)}, u32[]{:S(2)}) collective-permute-start(f32[384,512]{1,0:T(8,128)} %bitcast.3), channel_id=1, source_target_pairs={{0,16},{16,0},{1,17},{17,1},{2,18},{18,2},{3,19},{19,3},{4,20},{20... | collective-permute-start | bytes 2359304 | tf_op jit(solution)/shard_map/ppermute | solution.py:23
  6.6 13.9 %all-to-all-start = ((f32[8,24,128]{2,1,0:T(8,128)}), f32[8,24,128]{2,1,0:T(8,128)S(1)}, u32[]{:S(2)}, u32[]{:S(2)}) async-start(f32[8,24,128]{2,1,0:T(8,128)} %get-tuple-element.29), calls=%async_computation | async-start | bytes 196608 | tf_op jit(solution)/shard_map/all_to_all | solution.py:18
  13.0 1.1 %copy-start = (f32[12,32,512]{2,1,0:T(8,128)S(1)}, f32[12,32,512]{2,1,0:T(8,128)}, u32[]{:S(2)}) copy-start(f32[12,32,512]{2,1,0:T(8,128)} %param.4) | copy-start | bytes 2359300
  59.3 6.3 %collective-permute-start.2 = (f32[16,256]{1,0:T(8,128)S(1)}, f32[16,256]{1,0:T(8,128)S(1)}, u32[]{:S(2)}, u32[]{:S(2)}) collective-permute-start(f32[16,256]{1,0:T(8,128)S(1)} %get-tuple-element.44.refs_2_), channel_id=1, source_target_pairs={{0,16},{16,0},{1,17},{17,1},{2,18},{18,2},{3,19},{19,3},{4,20},{20... | collective-permute-start | bytes 49160 | tf_op jit(solution)/shard_map/ppermute | solution.py:23
  101.1 4.9 %collective-permute-start.3 = (f32[24,128]{1,0:T(8,128)S(1)}, f32[24,128]{1,0:T(8,128)S(1)}, u32[]{:S(2)}, u32[]{:S(2)}) collective-permute-start(f32[24,128]{1,0:T(8,128)S(1)} %shard_map.76.refs_1_), channel_id=1, source_target_pairs={{0,16},{16,0},{1,17},{17,1},{2,18},{18,2},{3,19},{19,3},{4,20},{20... | collective-permute-start | bytes 36872 | tf_op jit(solution)/shard_map/ppermute | solution.py:23

commit v12 on v9

--- a/solution.py
+++ b/solution.py
@@ -190,31 +190,29 @@
     return c, a, b
 
 
-def middle_pack(index, got_ref, own_ref, out_ref, sum_ref):
-    c, a, b = sum_xy(index, got_ref, own_ref)
-    for p in range(8):
-        out_ref[p, 0:16, :] = c
-        fill_slot(out_ref, p, jnp.where(index[0] == p // 4, a, b))
-    sum_ref[:, 0:128] = a
-    sum_ref[:, 128:256] = b
-
-
-def middle_sum(index, got_ref, own_ref, c_ref, ab_ref):
+def middle_total(index, got_ref, own_ref, c_ref, ab_ref):
+    c_ref[...], ab_ref[:, 0:128], ab_ref[:, 128:256] = sum_xy(index, got_ref, own_ref)
+
+
+def middle_pack(index, c_ref, ab_ref, other_ref, out_ref, sum_ref):
+    ab = ab_ref[...] + other_ref[...]
+    sum_ref[...] = ab
+    for p in range(8):
+        out_ref[p, 0:16, :] = c_ref[...]
+        fill_slot(out_ref, p, jnp.where(index[0] == p // 4, ab[:, 0:128], ab[:, 128:256]))
+
+
+def middle_update(rates, index, got_ref, own_ref, block_ref, slip_ref, block_out, out_ref, new):
     zl, zh = index[0], index[3]
-    c_ref[...] = jnp.sum(got_ref[:, 0:16, :], axis=0)
+    rate_a, rate_b, rate_c = rates
+    c = jnp.sum(got_ref[:, 0:16, :], axis=0)
     a = own_ref[:, 0:128]
     for q in range(4):
         a = a + jnp.where(zh == q, 0.0, slot(got_ref, zl * 4 + q))
-    ab_ref[:, 0:128] = a
-    ab_ref[:, 128:256] = own_ref[:, 128:256] + slot(got_ref, (1 - zl) * 4 + zh)
-
-
-def middle_update(rates, index, block_ref, c_ref, ab_ref, other_ref, slip_ref, block_out, out_ref, new):
-    rate_a, rate_b, rate_c = rates
-    ab = ab_ref[...] + other_ref[...]
-    new[0:16, :] = block_ref[0:16, :] - rate_c * c_ref[...]
-    new[16:32, 0:128] = block_ref[16:32, 0:128] - rate_a * ab[:, 0:128]
-    new[16:32, 128:256] = block_ref[16:32, 128:256] - rate_b * ab[:, 128:256]
+    b = own_ref[:, 128:256] + slot(got_ref, (1 - zl) * 4 + zh)
+    new[0:16, :] = block_ref[0:16, :] - rate_c * c
+    new[16:32, 0:128] = block_ref[16:32, 0:128] - rate_a * a
+    new[16:32, 128:256] = block_ref[16:32, 128:256] - rate_b * b
     block = new[...]
     block_out[...] = block
     send_block(block, out_ref, index[1])
@@ -318,16 +316,17 @@
     )
 
     send, own = step(exchange(send, XY), block, *targets)
-    send, own = call(middle_pack, [(8, 24, 256), pair], [], exchange(send, XY), own)
-    grad_c, grad_ab = call(middle_sum, [pair, pair], [], exchange(send, Z), own)
+    total_c, total_ab = call(middle_total, [pair, pair], [], exchange(send, XY), own)
+    send, own = call(
+        middle_pack, [(8, 24, 256), pair], [], total_c, total_ab, swap(total_ab)
+    )
     slip, block, send = call(
         functools.partial(middle_update, rates),
         [(24, 128), (32, 256), wide],
         [(32, 256)],
+        exchange(send, Z),
+        own,
         block,
-        grad_c,
-        grad_ab,
-        swap(grad_ab),
     )
     send, own = step(exchange(send, XY), block, *targets)
     (send,) = call(last_pack, [(8, 24, 128)], [(32, 256)], exchange(send, XY), own)

time: 105 us -> 106 us (level)
  no operation moved by 1% of the time
where the time goes in v12:
time: 106 us; the launch traced here: 105 us
  blocking collectives  70.1 us (66%)
  starting transfers between devices  19.3 us (18%)
  waiting for transfers between devices  7.52 us (7%)
  Pallas kernels  5.55 us (5%)
  local copies, waits for them, and re-layouts  1.13 us (1%)
    all_to_all x6, blocking collectives, exchange(): got = lax.all_to_all(parts.reshape(-1, shape[2]), axis, 0, 0, tiled=True)  70.1 us
    ppermute x4, starting transfers between devices, swap(): return lax.ppermute(value, 'core', [(0, 1), (1, 0)])  12.9 us
    all_to_all x1, starting transfers between devices, exchange(): got = lax.all_to_all(parts.reshape(-1, shape[2]), axis, 0, 0, tiled=True)  6.45 us
    pallas_call x11, Pallas kernels, call(): pl.pallas_call(kernel, out_shape=[jax.ShapeDtypeStruct(s, F32) for s in o...  5.55 us
    all_to_all x1, waiting for transfers between devices, exchange(): got = lax.all_to_all(parts.reshape(-1, shape[2]), axis, 0, 0, tiled=True)  4.97 us
    ppermute x4, waiting for transfers between devices, swap(): return lax.ppermute(value, 'core', [(0, 1), (1, 0)])  2.55 us
  transfers between devices with their start and end apart: 5, of which 4 were waited for; matrix products, arithmetic and copies ran while one was open for 0% of the time, Pallas kernels for 1%

profile of v12, /device:TPU:1, one launch (start us, length us, event | category | flops | bytes accessed | tf_op | source)
XLA Modules:
  0.0 105.0 jit_solution(6087919535086564101)
XLA Ops:
  0.6 0.7 select_maximum_fusion.refs_0_
  1.4 3.2 %collective-permute-start = (f32[40,256]{1,0:T(8,128)S(1)}, f32[40,256]{1,0:T(8,128)S(1)}, u32[]{:S(2)}, u32[]{:S(2)}) collective-permute-start(f32[40,256]{1,0:T(8,128)S(1)} %select_maximum_fusion.refs_0_), channel_id=1, source_target_pairs={{0,16},{16,0},{1,17},{17,1},{2,18},{18,2},{3,19},{19,3},{4,20},{20... | collective-permute-start | bytes 122888 | tf_op jit(solution)/shard_map/ppermute | solution.py:23
  4.6 0.9 collective-permute-done.refs_1_
  5.5 0.3 collective-permute-start.1
  5.8 0.7 shard_map.67
  6.6 6.4 %all-to-all-start = ((f32[8,24,128]{2,1,0:T(8,128)}), f32[8,24,128]{2,1,0:T(8,128)S(1)}, u32[]{:S(2)}, u32[]{:S(2)}) async-start(f32[8,24,128]{2,1,0:T(8,128)} %get-tuple-element.29), calls=%async_computation | async-start | bytes 196608 | tf_op jit(solution)/shard_map/all_to_all | solution.py:18
  13.0 1.1 %copy-done = f32[12,32,512]{2,1,0:T(8,128)S(1)} copy-done((f32[12,32,512]{2,1,0:T(8,128)S(1)}, f32[12,32,512]{2,1,0:T(8,128)}, u32[]{:S(2)}) %copy-start) | copy-done | bytes 786456
  14.2 0.8 shard_map.68
  15.0 5.0 %all-to-all-done.refs_0_ = f32[8,24,128]{2,1,0:T(8,128)S(1)} async-done(((f32[8,24,128]{2,1,0:T(8,128)}), f32[8,24,128]{2,1,0:T(8,128)S(1)}, u32[]{:S(2)}, u32[]{:S(2)}) %all-to-all-start) | async-done | bytes 98336 | tf_op jit(solution)/shard_map/all_to_all | solution.py:18
  19.9 0.1 shard_map.69
  20.0 14.7 %all_to_all.42.refs_0_ = f32[16,24,256]{2,1,0:T(8,128)S(1)} all-to-all(f32[16,24,256]{2,1,0:T(8,128)S(1)} %get-tuple-element.35), channel_id=1, replica_groups=mesh['zl'=2,'x'=4,'core'=2,'zh'=4,'y'=4] {'x','y'}, dimensions={0} | all-to-all | bytes 786432 | tf_op jit(solution)/shard_map/all_to_all | solution.py:18
  34.7 1.5 %shard_map.70 = (f32[16,24,256]{2,1,0:T(8,128)S(1)}, f32[16,256]{1,0:T(8,128)S(1)}) custom-call(f32[16,24,256]{2,1,0:T(8,128)S(1)} %all_to_all.42.refs_0_, f32[32,256]{1,0:T(8,128)S(1)} %get-tuple-element.36.refs_1_.refs_2_, f32[384,256]{1,0:T(8,128)S(1)} %get-tuple-element.37.refs_2_, f32[384,256]{1,0:T(8,128)S(1)} %get-tuple-element.38.refs_3_), custom_call_target="tpu_custom_call" | custom-call | tf_op jit(solution)/shard_map/pallas_call | solution.py:31
  36.2 11.4 %all_to_all.43.refs_0_ = f32[16,24,256]{2,1,0:T(8,128)S(1)} all-to-all(f32[16,24,256]{2,1,0:T(8,128)S(1)} %get-tuple-element.39), channel_id=1, replica_groups=mesh['zl'=2,'x'=4,'core'=2,'zh'=4,'y'=4] {'x','y'}, dimensions={0} | all-to-all | bytes 786432 | tf_op jit(solution)/shard_map/all_to_all | solution.py:18
  47.6 4.0 %collective-permute-start.2 = (f32[16,256]{1,0:T(8,128)S(1)}, f32[16,256]{1,0:T(8,128)S(1)}, u32[]{:S(2)}, u32[]{:S(2)}) collective-permute-start(f32[16,256]{1,0:T(8,128)S(1)} %get-tuple-element.42.refs_1_), channel_id=1, source_target_pairs={{0,16},{16,0},{1,17},{17,1},{2,18},{18,2},{3,19},{19,3},{4,20},{20... | collective-permute-start | bytes 49160 | tf_op jit(solution)/shard_map/ppermute | solution.py:23
  51.6 0.8 collective-permute-done.2.refs_2_
  52.5 10.2 %all_to_all.44.refs_0_ = f32[8,24,256]{2,1,0:T(8,128)S(1)} all-to-all(f32[8,24,256]{2,1,0:T(8,128)S(1)} %get-tuple-element.43), channel_id=1, replica_groups=mesh['zl'=2,'x'=4,'core'=2,'zh'=4,'y'=4] {'zl','zh'}, dimensions={0} | all-to-all | bytes 393216 | tf_op jit(solution)/shard_map/all_to_all | solution.py:18
  62.7 0.1 shard_map.73
  62.8 11.2 %all_to_all.45.refs_0_ = f32[16,24,256]{2,1,0:T(8,128)S(1)} all-to-all(f32[16,24,256]{2,1,0:T(8,128)S(1)} %get-tuple-element.46), channel_id=1, replica_groups=mesh['zl'=2,'x'=4,'core'=2,'zh'=4,'y'=4] {'x','y'}, dimensions={0} | all-to-all | bytes 786432 | tf_op jit(solution)/shard_map/all_to_all | solution.py:18
  74.1 1.5 %shard_map.74 = (f32[16,24,256]{2,1,0:T(8,128)S(1)}, f32[16,256]{1,0:T(8,128)S(1)}) custom-call(f32[16,24,256]{2,1,0:T(8,128)S(1)} %all_to_all.45.refs_0_, f32[32,256]{1,0:T(8,128)S(1)} %get-tuple-element.47.refs_1_, f32[384,256]{1,0:T(8,128)S(1)} %get-tuple-element.37.refs_2_, f32[384,256]{1,0:T(8,128)S(1)} %get-tuple-element.38.refs_3_), custom_call_target="tpu_custom_call" | custom-call | tf_op jit(solution)/shard_map/pallas_call | solution.py:31
  75.5 11.5 %all_to_all.46.refs_0_ = f32[16,24,256]{2,1,0:T(8,128)S(1)} all-to-all(f32[16,24,256]{2,1,0:T(8,128)S(1)} %get-tuple-element.48), channel_id=1, replica_groups=mesh['zl'=2,'x'=4,'core'=2,'zh'=4,'y'=4] {'x','y'}, dimensions={0} | all-to-all | bytes 786432 | tf_op jit(solution)/shard_map/all_to_all | solution.py:18
  87.1 11.1 %all_to_all.47.refs_0_ = f32[8,24,128]{2,1,0:T(8,128)S(1)} all-to-all(f32[8,24,128]{2,1,0:T(8,128)S(1)} %shard_map.75), channel_id=1, replica_groups=mesh['zl'=2,'x'=4,'core'=2,'zh'=4,'y'=4] {'zl','zh'}, dimensions={0} | all-to-all | bytes 196608 | tf_op jit(solution)/shard_map/all_to_all | solution.py:18
  98.2 5.2 %collective-permute-start.3 = (f32[24,128]{1,0:T(8,128)S(1)}, f32[24,128]{1,0:T(8,128)S(1)}, u32[]{:S(2)}, u32[]{:S(2)}) collective-permute-start(f32[24,128]{1,0:T(8,128)S(1)} %shard_map.76.refs_1_), channel_id=1, source_target_pairs={{0,16},{16,0},{1,17},{17,1},{2,18},{18,2},{3,19},{19,3},{4,20},{20... | collective-permute-start | bytes 36872 | tf_op jit(solution)/shard_map/ppermute | solution.py:23
  103.4 0.8 collective-permute-done.3.refs_2_
  104.3 0.7 shard_map.77
  (6 shorter events, 0.2 us)
Async XLA Ops:
  1.4 4.1 %collective-permute-start = (f32[40,256]{1,0:T(8,128)S(1)}, f32[40,256]{1,0:T(8,128)S(1)}, u32[]{:S(2)}, u32[]{:S(2)}) collective-permute-start(f32[40,256]{1,0:T(8,128)S(1)} %select_maximum_fusion.refs_0_), channel_id=1, source_target_pairs={{0,16},{16,0},{1,17},{17,1},{2,18},{18,2},{3,19},{19,3},{4,20},{20... | collective-permute-start | bytes 122888 | tf_op jit(solution)/shard_map/ppermute | solution.py:23
  5.5 7.5 %collective-permute-start.1 = (f32[384,512]{1,0:T(8,128)}, f32[384,512]{1,0:T(8,128)S(1)}, u32[]{:S(2)}, u32[]{:S(2)}) collective-permute-start(f32[384,512]{1,0:T(8,128)} %bitcast.3), channel_id=1, source_target_pairs={{0,16},{16,0},{1,17},{17,1},{2,18},{18,2},{3,19},{19,3},{4,20},{20... | collective-permute-start | bytes 2359304 | tf_op jit(solution)/shard_map/ppermute | solution.py:23
  6.6 13.4 %all-to-all-start = ((f32[8,24,128]{2,1,0:T(8,128)}), f32[8,24,128]{2,1,0:T(8,128)S(1)}, u32[]{:S(2)}, u32[]{:S(2)}) async-start(f32[8,24,128]{2,1,0:T(8,128)} %get-tuple-element.29), calls=%async_computation | async-start | bytes 196608 | tf_op jit(solution)/shard_map/all_to_all | solution.py:18
  13.0 1.1 %copy-start = (f32[12,32,512]{2,1,0:T(8,128)S(1)}, f32[12,32,512]{2,1,0:T(8,128)}, u32[]{:S(2)}) copy-start(f32[12,32,512]{2,1,0:T(8,128)} %param.4) | copy-start | bytes 2359300
  47.6 4.9 %collective-permute-start.2 = (f32[16,256]{1,0:T(8,128)S(1)}, f32[16,256]{1,0:T(8,128)S(1)}, u32[]{:S(2)}, u32[]{:S(2)}) collective-permute-start(f32[16,256]{1,0:T(8,128)S(1)} %get-tuple-element.42.refs_1_), channel_id=1, source_target_pairs={{0,16},{16,0},{1,17},{17,1},{2,18},{18,2},{3,19},{19,3},{4,20},{20... | collective-permute-start | bytes 49160 | tf_op jit(solution)/shard_map/ppermute | solution.py:23
  98.2 6.1 %collective-permute-start.3 = (f32[24,128]{1,0:T(8,128)S(1)}, f32[24,128]{1,0:T(8,128)S(1)}, u32[]{:S(2)}, u32[]{:S(2)}) collective-permute-start(f32[24,128]{1,0:T(8,128)S(1)} %shard_map.76.refs_1_), channel_id=1, source_target_pairs={{0,16},{16,0},{1,17},{17,1},{2,18},{18,2},{3,19},{19,3},{4,20},{20... | collective-permute-start | bytes 36872 | tf_op jit(solution)/shard_map/ppermute | solution.py:23

commit v13 on v7

--- a/solution.py
+++ b/solution.py
@@ -23,16 +23,19 @@
     return lax.ppermute(value, "core", [(0, 1), (1, 0)])
 
 
-def call(body, outs, scratch, index, *operands):
+def call(body, outs, scratch, *operands):
+    def kernel(*refs):
+        body([lax.axis_index(n) for n in ("zl", "x", "core", "zh", "y")], *refs)
+
     vmem = pl.BlockSpec(memory_space=pltpu.VMEM)
     return pl.pallas_call(
-        body,
+        kernel,
         out_shape=[jax.ShapeDtypeStruct(s, F32) for s in outs],
-        in_specs=[pl.BlockSpec(memory_space=pltpu.SMEM)] + [vmem] * len(operands),
+        in_specs=[vmem] * len(operands),
         out_specs=[vmem] * len(outs),
         scratch_shapes=[pltpu.VMEM(s, F32) for s in scratch],
         compiler_params=pltpu.CompilerParams(vmem_limit_bytes=40 * 1024 * 1024),
-    )(index, *operands)
+    )(*operands)
 
 
 def lanes(rows=16):
@@ -270,15 +273,16 @@
     a_ref[...] = turned[0:12, 0:16]
 
 
-def arrange(index, flat_ref, kept_ref, sent_ref):
+def arrange(flat_ref, kept_ref, sent_ref):
     spot = lax.broadcasted_iota(jnp.int32, (512, 256), 1)
     xs, ys = spot // 64, (spot // 16) % 4
     zls, zhs, us = (spot // 8) % 2, (spot // 2) % 4, spot % 2
     source = zls * 256 + xs * 64 + zhs * 8 + ys * 2 + us
     gap = lax.broadcasted_iota(jnp.int32, (512, 256), 0) - source
-    own, other = index[2] * 32, 32 - index[2] * 32
+    core = lax.axis_index("core")
+    own, other = core * 32, 32 - core * 32
     picks = [jnp.where(gap == n, 1.0, 0.0).astype(jnp.bfloat16) for n in (own, other)]
-    totals = [jnp.zeros((384, 256), F32)] * 2
+    totals = [jnp.zeros((128, 256), F32)] * 2
     rest = flat_ref[...]
     for _ in range(3):
         part = rest.astype(jnp.bfloat16)
@@ -290,7 +294,6 @@
 
 
 def per_device(tensor, first_factor, second_factor, third_factor):
-    index = jnp.stack([lax.axis_index(n) for n in ("zl", "x", "core", "zh", "y")])
     n_i, n_j, depth = tensor.shape
     size_i, size_j = n_i * 16, n_j * 16
     rates = tuple(4.0 / float(n) ** 0.5 for n in (size_j * depth, size_i * depth, size_i * size_j))
@@ -302,38 +305,43 @@
     shards = jnp.concatenate(
         [jnp.pad(v, ((0, n - v.shape[0]), (0, 256 - v.shape[1]))) for v, n in arguments]
     )
-    kept, sent = call(arrange, [(384, 256), (384, 256)], [], index, flat)
+    kept, sent = pl.pallas_call(
+        arrange,
+        grid=(3,),
+        in_specs=[pl.BlockSpec((128, depth), lambda i: (i, 0))],
+        out_specs=[pl.BlockSpec((128, depth // 2), lambda i: (i, 0))] * 2,
+        out_shape=[jax.ShapeDtypeStruct((384, depth // 2), F32)] * 2,
+        compiler_params=pltpu.CompilerParams(vmem_limit_bytes=62_800_000),
+    )(flat)
     sent, shards_other = lax.optimization_barrier((sent, swap(shards)))
     came = swap(sent)
-    (send,) = call(first_pack, [(8, 24, 128)], [square], index, shards, shards_other)
+    (send,) = call(first_pack, [(8, 24, 128)], [square], shards, shards_other)
     got, came = lax.optimization_barrier((exchange(send, Z), came))
-    block, send = call(block_from_slips, [(32, 256), wide], [], index, got)
     targets = kept, came
+    block, send = call(block_from_slips, [(32, 256), wide], [], got)
     step = functools.partial(
-        call, gradients, [wide, pair], [square, (768, 256), (768, 256), (32, 256)], index
+        call, gradients, [wide, pair], [square, (768, 256), (768, 256), (32, 256)]
     )
 
     send, own = step(exchange(send, XY), block, *targets)
-    send, own = call(middle_pack, [(8, 24, 256), pair], [], index, exchange(send, XY), own)
-    grad_c, grad_ab = call(middle_sum, [pair, pair], [], index, exchange(send, Z), own)
+    send, own = call(middle_pack, [(8, 24, 256), pair], [], exchange(send, XY), own)
+    grad_c, grad_ab = call(middle_sum, [pair, pair], [], exchange(send, Z), own)
     slip, block, send = call(
         functools.partial(middle_update, rates),
         [(24, 128), (32, 256), wide],
         [(32, 256)],
-        index,
         block,
         grad_c,
         grad_ab,
         swap(grad_ab),
     )
     send, own = step(exchange(send, XY), block, *targets)
-    (send,) = call(last_pack, [(8, 24, 128)], [(32, 256)], index, exchange(send, XY), own)
-    (grad,) = call(last_sum, [(24, 128)], [], index, exchange(send, Z))
+    (send,) = call(last_pack, [(8, 24, 128)], [(32, 256)], exchange(send, XY), own)
+    (grad,) = call(last_sum, [(24, 128)], [], exchange(send, Z))
     new_a, new_bt, new_c = call(
         functools.partial(last_update, rates),
         [(n_i, 16), (16, n_j), third_factor.shape],
         [square],
-        index,
         slip,
         grad,
         swap(grad),

time: 111 us -> 107 us (0.964)
  Pallas kernels: 10.8 us -> 7.62 us
  local copies, waits for them, and re-layouts: 1.22 us -> 0.01 us
    pallas_call x11, Pallas kernels: 10.8 us -> 7.62 us  [the longest x10 4.06 us: call(): pl.pallas_call(kernel, out_shape=[jax.ShapeDtypeStruct(s, F32) for s in o...]
    unnamed x2, local copies, waits for them, and re-layouts: 1.13 us -> 0.01 us
  transfers between devices with their start and end apart: 4 -> 4, of which waited for: 2 -> 2; matrix products, arithmetic and copies ran while one was open for 0% -> 0% of each run, Pallas kernels for 2% -> 3%
where the time goes in v13:
time: 107 us; the launch traced here: 106 us
  blocking collectives  82.6 us (77%)
  starting transfers between devices  13 us (12%)
  Pallas kernels  7.62 us (7%)
  waiting for transfers between devices  1.68 us (2%)
    all_to_all x7, blocking collectives, exchange(): got = lax.all_to_all(parts.reshape(-1, shape[2]), axis, 0, 0, tiled=True)  82.6 us
    ppermute x4, starting transfers between devices, swap(): return lax.ppermute(value, 'core', [(0, 1), (1, 0)])  13 us
    pallas_call x10, Pallas kernels, call(): pl.pallas_call(kernel, out_shape=[jax.ShapeDtypeStruct(s, F32) for s in o...  4.06 us
    pallas_call x1, Pallas kernels, per_device(): pl.pallas_call(arrange, grid=(3,), in_specs=[pl.BlockSpec((128, depth), l...  3.56 us
  transfers between devices with their start and end apart: 4, of which 2 were waited for; matrix products, arithmetic and copies ran while one was open for 0% of the time, Pallas kernels for 3%

profile of v13, /device:TPU:1, one launch (start us, length us, event | category | flops | bytes accessed | tf_op | source)
XLA Modules:
  0.0 106.3 jit_solution(7215269595464964347)
XLA Ops:
  0.6 0.7 select_maximum_fusion.refs_0_
  1.4 3.2 %collective-permute-start = (f32[40,256]{1,0:T(8,128)S(1)}, f32[40,256]{1,0:T(8,128)S(1)}, u32[]{:S(2)}, u32[]{:S(2)}) collective-permute-start(f32[40,256]{1,0:T(8,128)S(1)} %select_maximum_fusion.refs_0_), channel_id=1, source_target_pairs={{0,16},{16,0},{1,17},{17,1},{2,18},{18,2},{3,19},{19,3},{4,20},{20... | collective-permute-start | bytes 122888 | tf_op jit(solution)/shard_map/ppermute | solution.py:23
  4.6 3.6 %shard_map.67 = (f32[384,256]{1,0:T(8,128)}, f32[384,256]{1,0:T(8,128)}) custom-call(f32[384,512]{1,0:T(8,128)} %bitcast.3), custom_call_target="tpu_custom_call" | custom-call | tf_op jit(solution)/shard_map/pallas_call | solution.py:308
  8.2 0.0 collective-permute-done.refs_1_
  8.2 0.0 collective-permute-start.1
  8.2 0.1 shard_map.68
  8.3 13.2 %all_to_all.42.refs_0_ = f32[8,24,128]{2,1,0:T(8,128)S(1)} all-to-all(f32[8,24,128]{2,1,0:T(8,128)S(1)} %shard_map.68), channel_id=1, replica_groups=mesh['zl'=2,'x'=4,'core'=2,'zh'=4,'y'=4] {'zl','zh'}, dimensions={0} | all-to-all | bytes 196608 | tf_op jit(solution)/shard_map/all_to_all | solution.py:18
  21.4 0.0 collective-permute-done.1.refs_3_
  21.4 0.1 shard_map.69
  21.6 14.7 %all_to_all.43.refs_0_ = f32[16,24,256]{2,1,0:T(8,128)S(1)} all-to-all(f32[16,24,256]{2,1,0:T(8,128)S(1)} %get-tuple-element.30), channel_id=1, replica_groups=mesh['zl'=2,'x'=4,'core'=2,'zh'=4,'y'=4] {'x','y'}, dimensions={0} | all-to-all | bytes 786432 | tf_op jit(solution)/shard_map/all_to_all | solution.py:18
  36.2 1.5 %shard_map.70 = (f32[16,24,256]{2,1,0:T(8,128)S(1)}, f32[16,256]{1,0:T(8,128)S(1)}) custom-call(f32[16,24,256]{2,1,0:T(8,128)S(1)} %all_to_all.43.refs_0_, f32[32,256]{1,0:T(8,128)S(1)} %get-tuple-element.29.refs_1_.refs_0_, f32[384,256]{1,0:T(8,128)S(1)} %copy-done, f32[384,256]{1,0:T(8,128)S(1)} %collective-permute-done.1.refs_3_), custom_call_target="tpu_custom_call" | custom-call | tf_op jit(solution)/shard_map/pallas_call | solution.py:31
  37.7 11.6 %all_to_all.44.refs_0_ = f32[16,24,256]{2,1,0:T(8,128)S(1)} all-to-all(f32[16,24,256]{2,1,0:T(8,128)S(1)} %get-tuple-element.33), channel_id=1, replica_groups=mesh['zl'=2,'x'=4,'core'=2,'zh'=4,'y'=4] {'x','y'}, dimensions={0} | all-to-all | bytes 786432 | tf_op jit(solution)/shard_map/all_to_all | solution.py:18
  49.3 9.7 %all_to_all.45.refs_0_ = f32[8,24,256]{2,1,0:T(8,128)S(1)} all-to-all(f32[8,24,256]{2,1,0:T(8,128)S(1)} %get-tuple-element.35), channel_id=1, replica_groups=mesh['zl'=2,'x'=4,'core'=2,'zh'=4,'y'=4] {'zl','zh'}, dimensions={0} | all-to-all | bytes 393216 | tf_op jit(solution)/shard_map/all_to_all | solution.py:18
  59.1 5.4 %collective-permute-start.2 = (f32[16,256]{1,0:T(8,128)S(1)}, f32[16,256]{1,0:T(8,128)S(1)}, u32[]{:S(2)}, u32[]{:S(2)}) collective-permute-start(f32[16,256]{1,0:T(8,128)S(1)} %get-tuple-element.38.refs_2_), channel_id=1, source_target_pairs={{0,16},{16,0},{1,17},{17,1},{2,18},{18,2},{3,19},{19,3},{4,20},{20... | collective-permute-start | bytes 49160 | tf_op jit(solution)/shard_map/ppermute | solution.py:23
  64.5 0.8 collective-permute-done.2.refs_3_
  65.3 0.1 shard_map.73
  65.4 12.5 %all_to_all.46.refs_0_ = f32[16,24,256]{2,1,0:T(8,128)S(1)} all-to-all(f32[16,24,256]{2,1,0:T(8,128)S(1)} %get-tuple-element.40), channel_id=1, replica_groups=mesh['zl'=2,'x'=4,'core'=2,'zh'=4,'y'=4] {'x','y'}, dimensions={0} | all-to-all | bytes 786432 | tf_op jit(solution)/shard_map/all_to_all | solution.py:18
  77.9 1.5 %shard_map.74 = (f32[16,24,256]{2,1,0:T(8,128)S(1)}, f32[16,256]{1,0:T(8,128)S(1)}) custom-call(f32[16,24,256]{2,1,0:T(8,128)S(1)} %all_to_all.46.refs_0_, f32[32,256]{1,0:T(8,128)S(1)} %get-tuple-element.41.refs_1_, f32[384,256]{1,0:T(8,128)S(1)} %copy-done, f32[384,256]{1,0:T(8,128)S(1)} %collective-permute-done.1.refs_3_), custom_call_target="tpu_custom_call" | custom-call | tf_op jit(solution)/shard_map/pallas_call | solution.py:31
  79.4 11.3 %all_to_all.47.refs_0_ = f32[16,24,256]{2,1,0:T(8,128)S(1)} all-to-all(f32[16,24,256]{2,1,0:T(8,128)S(1)} %get-tuple-element.42), channel_id=1, replica_groups=mesh['zl'=2,'x'=4,'core'=2,'zh'=4,'y'=4] {'x','y'}, dimensions={0} | all-to-all | bytes 786432 | tf_op jit(solution)/shard_map/all_to_all | solution.py:18
  90.6 0.1 shard_map.75
  90.7 9.7 %all_to_all.48.refs_0_ = f32[8,24,128]{2,1,0:T(8,128)S(1)} all-to-all(f32[8,24,128]{2,1,0:T(8,128)S(1)} %shard_map.75), channel_id=1, replica_groups=mesh['zl'=2,'x'=4,'core'=2,'zh'=4,'y'=4] {'zl','zh'}, dimensions={0} | all-to-all | bytes 196608 | tf_op jit(solution)/shard_map/all_to_all | solution.py:18
  100.4 4.3 %collective-permute-start.3 = (f32[24,128]{1,0:T(8,128)S(1)}, f32[24,128]{1,0:T(8,128)S(1)}, u32[]{:S(2)}, u32[]{:S(2)}) collective-permute-start(f32[24,128]{1,0:T(8,128)S(1)} %shard_map.76.refs_1_), channel_id=1, source_target_pairs={{0,16},{16,0},{1,17},{17,1},{2,18},{18,2},{3,19},{19,3},{4,20},{20... | collective-permute-start | bytes 36872 | tf_op jit(solution)/shard_map/ppermute | solution.py:23
  104.8 0.8 collective-permute-done.3.refs_2_
  105.6 0.7 shard_map.77
  (5 shorter events, 0.1 us)
Async XLA Ops:
  1.4 6.8 %collective-permute-start = (f32[40,256]{1,0:T(8,128)S(1)}, f32[40,256]{1,0:T(8,128)S(1)}, u32[]{:S(2)}, u32[]{:S(2)}) collective-permute-start(f32[40,256]{1,0:T(8,128)S(1)} %select_maximum_fusion.refs_0_), channel_id=1, source_target_pairs={{0,16},{16,0},{1,17},{17,1},{2,18},{18,2},{3,19},{19,3},{4,20},{20... | collective-permute-start | bytes 122888 | tf_op jit(solution)/shard_map/ppermute | solution.py:23
  8.2 13.3 %collective-permute-start.1 = (f32[384,256]{1,0:T(8,128)}, f32[384,256]{1,0:T(8,128)S(1)}, u32[]{:S(2)}, u32[]{:S(2)}) collective-permute-start(f32[384,256]{1,0:T(8,128)} %get-tuple-element.27), channel_id=1, source_target_pairs={{0,16},{16,0},{1,17},{17,1},{2,18},{18,2},{3,19},{19,3},{4,20},{20... | collective-permute-start | bytes 1179656 | tf_op jit(solution)/shard_map/ppermute | solution.py:23
  21.5 14.7 %copy-start = (f32[384,256]{1,0:T(8,128)S(1)}, f32[384,256]{1,0:T(8,128)}, u32[]{:S(2)}) copy-start(f32[384,256]{1,0:T(8,128)} %get-tuple-element.31.refs_2_) | copy-start | bytes 1179652
  59.1 6.2 %collective-permute-start.2 = (f32[16,256]{1,0:T(8,128)S(1)}, f32[16,256]{1,0:T(8,128)S(1)}, u32[]{:S(2)}, u32[]{:S(2)}) collective-permute-start(f32[16,256]{1,0:T(8,128)S(1)} %get-tuple-element.38.refs_2_), channel_id=1, source_target_pairs={{0,16},{16,0},{1,17},{17,1},{2,18},{18,2},{3,19},{19,3},{4,20},{20... | collective-permute-start | bytes 49160 | tf_op jit(solution)/shard_map/ppermute | solution.py:23
  100.4 5.2 %collective-permute-start.3 = (f32[24,128]{1,0:T(8,128)S(1)}, f32[24,128]{1,0:T(8,128)S(1)}, u32[]{:S(2)}, u32[]{:S(2)}) collective-permute-start(f32[24,128]{1,0:T(8,128)S(1)} %shard_map.76.refs_1_), channel_id=1, source_target_pairs={{0,16},{16,0},{1,17},{17,1},{2,18},{18,2},{3,19},{19,3},{4,20},{20... | collective-permute-start | bytes 36872 | tf_op jit(solution)/shard_map/ppermute | solution.py:23

commit v14 on v9

--- a/solution.py
+++ b/solution.py
@@ -85,7 +85,7 @@
     return c, ab
 
 
-def first_pack(index, own_ref, other_ref, out_ref, done_ref, pad):
+def first_pack(index, own_ref, other_ref, out_ref, pad):
     even = index[2] == 0
     own, other = own_ref[0:32, 0:128], other_ref[0:32, 0:128]
     low, high = jnp.where(even, own, other), jnp.where(even, other, own)
@@ -98,7 +98,6 @@
         out_ref[p, 0:2, :] = own_ref[32:34, 0:128]
         out_ref[p, 2:4, :] = own_ref[32:34, 128:256]
         out_ref[p, 8:24, :] = ab
-    done_ref[...] = ab
 
 
 def block_from_slips(index, got_ref, block_ref, out_ref):
@@ -307,12 +306,9 @@
     shards_other = swap(shards)
     flat, shards_other = lax.optimization_barrier((flat, shards_other))
     flat_other = swap(flat)
-    send, done = call(
-        first_pack, [(8, 24, 128), (16, 128)], [square], shards, shards_other
-    )
-    targets = call(arrange, [(384, 256), (384, 256)], [], done, flat, flat_other)
-    got, targets = lax.optimization_barrier((exchange(send, Z), targets))
-    block, send = call(block_from_slips, [(32, 256), wide], [], got)
+    (send,) = call(first_pack, [(8, 24, 128)], [square], shards, shards_other)
+    block, send = call(block_from_slips, [(32, 256), wide], [], exchange(send, Z))
+    targets = call(arrange, [(384, 256), (384, 256)], [], block, flat, flat_other)
     step = functools.partial(
         call, gradients, [wide, pair], [square, (768, 256), (768, 256), (32, 256)]
     )

time: 105 us -> 106 us (level)
  waiting for transfers between devices: 7.52 us -> 9.83 us
  blocking collectives: 70 us -> 68.6 us
  local copies, waits for them, and re-layouts: 1.13 us -> 0.01 us
    all_to_all x1, waiting for transfers between devices: 4.97 us -> 7.29 us  [exchange(): got = lax.all_to_all(parts.reshape(-1, shape[2]), axis, 0, 0, tiled=True)]
    all_to_all x6, blocking collectives: 70 us -> 68.6 us  [exchange(): got = lax.all_to_all(parts.reshape(-1, shape[2]), axis, 0, 0, tiled=True)]
    unnamed x2, local copies, waits for them, and re-layouts: 1.13 us -> 0.01 us
  transfers between devices with their start and end apart: 5 -> 5, of which waited for: 4 -> 4; matrix products, arithmetic and copies ran while one was open for 0% -> 0% of each run, Pallas kernels for 1% -> 2%
where the time goes in v14:
time: 106 us; the launch traced here: 105 us
  blocking collectives  68.6 us (65%)
  starting transfers between devices  19.5 us (18%)
  waiting for transfers between devices  9.83 us (9%)
  Pallas kernels  5.59 us (5%)
    all_to_all x6, blocking collectives, exchange(): got = lax.all_to_all(parts.reshape(-1, shape[2]), axis, 0, 0, tiled=True)  68.6 us
    ppermute x4, starting transfers between devices, swap(): return lax.ppermute(value, 'core', [(0, 1), (1, 0)])  12.8 us
    all_to_all x1, waiting for transfers between devices, exchange(): got = lax.all_to_all(parts.reshape(-1, shape[2]), axis, 0, 0, tiled=True)  7.29 us
    all_to_all x1, starting transfers between devices, exchange(): got = lax.all_to_all(parts.reshape(-1, shape[2]), axis, 0, 0, tiled=True)  6.75 us
    pallas_call x11, Pallas kernels, call(): pl.pallas_call(kernel, out_shape=[jax.ShapeDtypeStruct(s, F32) for s in o...  5.59 us
    ppermute x4, waiting for transfers between devices, swap(): return lax.ppermute(value, 'core', [(0, 1), (1, 0)])  2.55 us
  transfers between devices with their start and end apart: 5, of which 4 were waited for; matrix products, arithmetic and copies ran while one was open for 0% of the time, Pallas kernels for 2%

profile of v14, /device:TPU:1, one launch (start us, length us, event | category | flops | bytes accessed | tf_op | source)
XLA Modules:
  0.0 105.1 jit_solution(10504278239900934844)
XLA Ops:
  0.6 0.8 select_maximum_fusion.refs_0_
  1.5 3.2 %collective-permute-start = (f32[40,256]{1,0:T(8,128)S(1)}, f32[40,256]{1,0:T(8,128)S(1)}, u32[]{:S(2)}, u32[]{:S(2)}) collective-permute-start(f32[40,256]{1,0:T(8,128)S(1)} %select_maximum_fusion.refs_0_), channel_id=1, source_target_pairs={{0,16},{16,0},{1,17},{17,1},{2,18},{18,2},{3,19},{19,3},{4,20},{20... | collective-permute-start | bytes 122888 | tf_op jit(solution)/shard_map/ppermute | solution.py:23
  4.7 0.9 collective-permute-done.refs_1_
  5.6 0.3 collective-permute-start.1
  5.9 0.1 shard_map.67
  6.0 13.2 %all_to_all.42.refs_0_ = f32[8,24,128]{2,1,0:T(8,128)S(1)} all-to-all(f32[8,24,128]{2,1,0:T(8,128)S(1)} %shard_map.67), channel_id=1, replica_groups=mesh['zl'=2,'x'=4,'core'=2,'zh'=4,'y'=4] {'zl','zh'}, dimensions={0} | all-to-all | bytes 196608 | tf_op jit(solution)/shard_map/all_to_all | solution.py:18
  19.2 0.8 shard_map.68
  20.0 6.8 %all-to-all-start.1 = ((f32[16,24,256]{2,1,0:T(8,128)}), f32[16,24,256]{2,1,0:T(8,128)S(1)}, u32[]{:S(2)}, u32[]{:S(2)}) async-start(f32[16,24,256]{2,1,0:T(8,128)} %get-tuple-element.25), calls=%async_computation.1 | async-start | bytes 786432 | tf_op jit(solution)/shard_map/all_to_all | solution.py:18
  26.8 0.8 shard_map.69
  27.6 7.3 %all-to-all-done.1.refs_0_ = f32[16,24,256]{2,1,0:T(8,128)S(1)} async-done(((f32[16,24,256]{2,1,0:T(8,128)}), f32[16,24,256]{2,1,0:T(8,128)S(1)}, u32[]{:S(2)}, u32[]{:S(2)}) %all-to-all-start.1) | async-done | bytes 393248 | tf_op jit(solution)/shard_map/all_to_all | solution.py:18
  34.9 1.5 %shard_map.70 = (f32[16,24,256]{2,1,0:T(8,128)S(1)}, f32[16,256]{1,0:T(8,128)S(1)}) custom-call(f32[16,24,256]{2,1,0:T(8,128)S(1)} %all-to-all-done.1.refs_0_, f32[32,256]{1,0:T(8,128)S(1)} %get-tuple-element.24.refs_0_.refs_1_, f32[384,256]{1,0:T(8,128)S(1)} %get-tuple-element.27.refs_2_, f32[384,256]{1,0:T(8,128)S(1)} %get-tuple-element.28.refs_3_), custom_call_target="tpu_custom_call" | custom-call | tf_op jit(solution)/shard_map/pallas_call | solution.py:31
  36.3 11.4 %all_to_all.43.refs_0_ = f32[16,24,256]{2,1,0:T(8,128)S(1)} all-to-all(f32[16,24,256]{2,1,0:T(8,128)S(1)} %get-tuple-element.29), channel_id=1, replica_groups=mesh['zl'=2,'x'=4,'core'=2,'zh'=4,'y'=4] {'x','y'}, dimensions={0} | all-to-all | bytes 786432 | tf_op jit(solution)/shard_map/all_to_all | solution.py:18
  47.8 10.7 %all_to_all.44.refs_0_ = f32[8,24,256]{2,1,0:T(8,128)S(1)} all-to-all(f32[8,24,256]{2,1,0:T(8,128)S(1)} %get-tuple-element.31), channel_id=1, replica_groups=mesh['zl'=2,'x'=4,'core'=2,'zh'=4,'y'=4] {'zl','zh'}, dimensions={0} | all-to-all | bytes 393216 | tf_op jit(solution)/shard_map/all_to_all | solution.py:18
  58.4 4.9 %collective-permute-start.2 = (f32[16,256]{1,0:T(8,128)S(1)}, f32[16,256]{1,0:T(8,128)S(1)}, u32[]{:S(2)}, u32[]{:S(2)}) collective-permute-start(f32[16,256]{1,0:T(8,128)S(1)} %get-tuple-element.34.refs_2_), channel_id=1, source_target_pairs={{0,16},{16,0},{1,17},{17,1},{2,18},{18,2},{3,19},{19,3},{4,20},{20... | collective-permute-start | bytes 49160 | tf_op jit(solution)/shard_map/ppermute | solution.py:23
  63.3 0.8 collective-permute-done.2.refs_3_
  64.1 0.1 shard_map.73
  64.2 12.5 %all_to_all.45.refs_0_ = f32[16,24,256]{2,1,0:T(8,128)S(1)} all-to-all(f32[16,24,256]{2,1,0:T(8,128)S(1)} %get-tuple-element.36), channel_id=1, replica_groups=mesh['zl'=2,'x'=4,'core'=2,'zh'=4,'y'=4] {'x','y'}, dimensions={0} | all-to-all | bytes 786432 | tf_op jit(solution)/shard_map/all_to_all | solution.py:18
  76.8 1.5 %shard_map.74 = (f32[16,24,256]{2,1,0:T(8,128)S(1)}, f32[16,256]{1,0:T(8,128)S(1)}) custom-call(f32[16,24,256]{2,1,0:T(8,128)S(1)} %all_to_all.45.refs_0_, f32[32,256]{1,0:T(8,128)S(1)} %get-tuple-element.37.refs_1_, f32[384,256]{1,0:T(8,128)S(1)} %get-tuple-element.27.refs_2_, f32[384,256]{1,0:T(8,128)S(1)} %get-tuple-element.28.refs_3_), custom_call_target="tpu_custom_call" | custom-call | tf_op jit(solution)/shard_map/pallas_call | solution.py:31
  78.2 11.3 %all_to_all.46.refs_0_ = f32[16,24,256]{2,1,0:T(8,128)S(1)} all-to-all(f32[16,24,256]{2,1,0:T(8,128)S(1)} %get-tuple-element.38), channel_id=1, replica_groups=mesh['zl'=2,'x'=4,'core'=2,'zh'=4,'y'=4] {'x','y'}, dimensions={0} | all-to-all | bytes 786432 | tf_op jit(solution)/shard_map/all_to_all | solution.py:18
  89.5 0.1 shard_map.75
  89.6 9.6 %all_to_all.47.refs_0_ = f32[8,24,128]{2,1,0:T(8,128)S(1)} all-to-all(f32[8,24,128]{2,1,0:T(8,128)S(1)} %shard_map.75), channel_id=1, replica_groups=mesh['zl'=2,'x'=4,'core'=2,'zh'=4,'y'=4] {'zl','zh'}, dimensions={0} | all-to-all | bytes 196608 | tf_op jit(solution)/shard_map/all_to_all | solution.py:18
  99.2 4.3 %collective-permute-start.3 = (f32[24,128]{1,0:T(8,128)S(1)}, f32[24,128]{1,0:T(8,128)S(1)}, u32[]{:S(2)}, u32[]{:S(2)}) collective-permute-start(f32[24,128]{1,0:T(8,128)S(1)} %shard_map.76.refs_1_), channel_id=1, source_target_pairs={{0,16},{16,0},{1,17},{17,1},{2,18},{18,2},{3,19},{19,3},{4,20},{20... | collective-permute-start | bytes 36872 | tf_op jit(solution)/shard_map/ppermute | solution.py:23
  103.5 0.8 collective-permute-done.3.refs_2_
  104.4 0.7 shard_map.77
  (6 shorter events, 0.1 us)
Async XLA Ops:
  0.6 26.2 %copy-start = (f32[12,32,512]{2,1,0:T(8,128)S(1)}, f32[12,32,512]{2,1,0:T(8,128)}, u32[]{:S(2)}) copy-start(f32[12,32,512]{2,1,0:T(8,128)} %param.4) | copy-start | bytes 2359300
  1.5 4.1 %collective-permute-start = (f32[40,256]{1,0:T(8,128)S(1)}, f32[40,256]{1,0:T(8,128)S(1)}, u32[]{:S(2)}, u32[]{:S(2)}) collective-permute-start(f32[40,256]{1,0:T(8,128)S(1)} %select_maximum_fusion.refs_0_), channel_id=1, source_target_pairs={{0,16},{16,0},{1,17},{17,1},{2,18},{18,2},{3,19},{19,3},{4,20},{20... | collective-permute-start | bytes 122888 | tf_op jit(solution)/shard_map/ppermute | solution.py:23
  5.6 21.2 %collective-permute-start.1 = (f32[384,512]{1,0:T(8,128)}, f32[384,512]{1,0:T(8,128)S(1)}, u32[]{:S(2)}, u32[]{:S(2)}) collective-permute-start(f32[384,512]{1,0:T(8,128)} %bitcast.3), channel_id=1, source_target_pairs={{0,16},{16,0},{1,17},{17,1},{2,18},{18,2},{3,19},{19,3},{4,20},{20... | collective-permute-start | bytes 2359304 | tf_op jit(solution)/shard_map/ppermute | solution.py:23
  20.0 14.9 %all-to-all-start.1 = ((f32[16,24,256]{2,1,0:T(8,128)}), f32[16,24,256]{2,1,0:T(8,128)S(1)}, u32[]{:S(2)}, u32[]{:S(2)}) async-start(f32[16,24,256]{2,1,0:T(8,128)} %get-tuple-element.25), calls=%async_computation.1 | async-start | bytes 786432 | tf_op jit(solution)/shard_map/all_to_all | solution.py:18
  58.4 5.7 %collective-permute-start.2 = (f32[16,256]{1,0:T(8,128)S(1)}, f32[16,256]{1,0:T(8,128)S(1)}, u32[]{:S(2)}, u32[]{:S(2)}) collective-permute-start(f32[16,256]{1,0:T(8,128)S(1)} %get-tuple-element.34.refs_2_), channel_id=1, source_target_pairs={{0,16},{16,0},{1,17},{17,1},{2,18},{18,2},{3,19},{19,3},{4,20},{20... | collective-permute-start | bytes 49160 | tf_op jit(solution)/shard_map/ppermute | solution.py:23
  99.2 5.2 %collective-permute-start.3 = (f32[24,128]{1,0:T(8,128)S(1)}, f32[24,128]{1,0:T(8,128)S(1)}, u32[]{:S(2)}, u32[]{:S(2)}) collective-permute-start(f32[24,128]{1,0:T(8,128)S(1)} %shard_map.76.refs_1_), channel_id=1, source_target_pairs={{0,16},{16,0},{1,17},{17,1},{2,18},{18,2},{3,19},{19,3},{4,20},{20... | collective-permute-start | bytes 36872 | tf_op jit(solution)/shard_map/ppermute | solution.py:23
